TPU v7x, 32 devices: a whole 2x2x4 slice. The times are simulated.
32 devices in a mesh: gx: 8 (over y, x, core), gy: 4 (over z).
Axes of the slice: x: 2, y: 2, z: 4, core: 2. Of those that a mesh axis runs over, the one named last changes fastest.
Arguments:
- electric: float32 [3, 16, 64, 512], P(None, None, 'gx', 'gy'), may hold values from -6 to 6
- magnetic: float32 [3, 16, 64, 512], P(None, None, 'gx', 'gy'), may hold values from -6 to 6
- material: int32 [16, 64, 512], P(None, 'gx', 'gy'), may hold values from 0 to 3
- permittivity: float32 [4], replicated, may hold values from 1 to 12
- slab_spectra: float32 [2, 128, 64, 512], P(None, None, 'gx', 'gy'), may hold values from -6 to 6
- monitor_spectra: float32 [16, 2, 4, 64, 512], P(None, None, None, 'gx', 'gy'), may hold values from -6 to 6
- wave_index: int32 [16], replicated, may hold values from 0 to 63
Outputs:
- electric_next: float32 [3, 16, 64, 512], P(None, None, 'gx', 'gy')
- magnetic_next: float32 [3, 16, 64, 512], P(None, None, 'gx', 'gy')
- slab_next: float32 [2, 128, 64, 512], P(None, None, 'gx', 'gy')
- monitor_next: float32 [16, 2, 4, 64, 512], P(None, None, None, 'gx', 'gy')
- orders: float32 [16, 2, 4, 128, 64], P('gy', None, None, 'gx')
All inputs are finite; a program needn't handle non-finite values.
Results may differ from a plain program's by a relative error of at most 0.00007.
Values sent between devices are 32-bit elements; how exact they have to be, the bound alone decides.
No kernel may reach another device: no remote copies, remote signals or barrier semaphores. Data moves between devices by JAX's collectives and lax.ppermute only.
A program may use at most 64 MiB of HBM per device.

v0:
```python
import math

import jax
import jax.numpy as jnp
from jax import lax
from jax.sharding import PartitionSpec as P

OY = 128
OX = 64


TIME_STEP = 0.5
OMEGA_LOW = 0.15
OMEGA_HIGH = 0.8


def passed_along(block, axis, distance):
    devices = range(lax.axis_size(axis))
    route = [((i - distance) % len(devices), i) for i in devices]
    return lax.ppermute(block, axis, route)


def forward_z(values):
    return jnp.concatenate([values[1:], jnp.zeros_like(values[:1])], axis=0) - values


def backward_z(values):
    return values - jnp.concatenate([jnp.zeros_like(values[:1]), values[:-1]], axis=0)


def inverse_map(material, permittivity):
    inverse = jnp.zeros(material.shape, jnp.float32)
    for category in range(permittivity.shape[0]):
        inverse = inverse + jnp.where(material == category, 1.0 / permittivity[category], 0.0)
    return inverse


def all_omegas(freq_count):
    return OMEGA_LOW + (OMEGA_HIGH - OMEGA_LOW) * jnp.arange(freq_count, dtype=jnp.float32) / (
        freq_count - 1
    )


def picked_omegas(wave_index, freq_count):
    matches = wave_index[:, None] == jnp.arange(freq_count, dtype=jnp.int32)[None, :]
    return jnp.sum(jnp.where(matches, all_omegas(freq_count)[None, :], 0.0), axis=1)


def order_table(length, kept_count, modulus):
    position = jnp.arange(length, dtype=jnp.int32)
    wanted = (jnp.arange(kept_count, dtype=jnp.int32) - kept_count // 2) % modulus
    phases = position[:, None] * wanted[None, :] % modulus
    angles = 2.0 * math.pi / modulus * phases.astype(jnp.float32)
    cosine = jnp.cos(angles)
    sine_part = jnp.sin(angles)
    return jnp.stack([jnp.stack([cosine, -sine_part]), jnp.stack([sine_part, cosine])])


def advance(electric, magnetic, inverse):
    electric_x, electric_y, electric_z = (electric[0], electric[1], electric[2])
    faces_ahead_x = passed_along(jnp.stack([electric_y[:, :1, :], electric_z[:, :1, :]]), "gx", -1)
    faces_ahead_y = passed_along(jnp.stack([electric_x[:, :, :1], electric_z[:, :, :1]]), "gy", -1)
    ey_ahead_x = jnp.concatenate([electric_y[:, 1:, :], faces_ahead_x[0]], axis=1)
    ez_ahead_x = jnp.concatenate([electric_z[:, 1:, :], faces_ahead_x[1]], axis=1)
    ex_ahead_y = jnp.concatenate([electric_x[:, :, 1:], faces_ahead_y[0]], axis=2)
    ez_ahead_y = jnp.concatenate([electric_z[:, :, 1:], faces_ahead_y[1]], axis=2)
    magnetic_x = magnetic[0] - TIME_STEP * (ez_ahead_y - electric_z - forward_z(electric_y))
    magnetic_y = magnetic[1] - TIME_STEP * (forward_z(electric_x) - (ez_ahead_x - electric_z))
    magnetic_z = magnetic[2] - TIME_STEP * (ey_ahead_x - electric_y - (ex_ahead_y - electric_x))
    faces_behind_x = passed_along(
        jnp.stack([magnetic_y[:, -1:, :], magnetic_z[:, -1:, :]]), "gx", 1
    )
    faces_behind_y = passed_along(
        jnp.stack([magnetic_x[:, :, -1:], magnetic_z[:, :, -1:]]), "gy", 1
    )
    hy_behind_x = jnp.concatenate([faces_behind_x[0], magnetic_y[:, :-1, :]], axis=1)
    hz_behind_x = jnp.concatenate([faces_behind_x[1], magnetic_z[:, :-1, :]], axis=1)
    hx_behind_y = jnp.concatenate([faces_behind_y[0], magnetic_x[:, :, :-1]], axis=2)
    hz_behind_y = jnp.concatenate([faces_behind_y[1], magnetic_z[:, :, :-1]], axis=2)
    new_x = electric_x + TIME_STEP * inverse * (magnetic_z - hz_behind_y - backward_z(magnetic_y))
    new_y = electric_y + TIME_STEP * inverse * (backward_z(magnetic_x) - (magnetic_z - hz_behind_x))
    new_z = electric_z + TIME_STEP * inverse * (
        magnetic_y - hy_behind_x - (magnetic_x - hx_behind_y)
    )
    return (jnp.stack([new_x, new_y, new_z]), jnp.stack([magnetic_x, magnetic_y, magnetic_z]))


def records_of(electric, magnetic):
    middle = electric.shape[1] // 2
    slab_layer = electric[0:2, middle]
    monitor_plane = jnp.concatenate([electric[0:2, -1], magnetic[0:2, -1]], axis=0)
    return (slab_layer, monitor_plane)


def spectra_update(slab_spectra, monitor_spectra, slab_records, monitor_records, wave_index):
    freq_count = slab_spectra.shape[1] // 2
    times = TIME_STEP * (jnp.arange(2, dtype=jnp.float32) + 1.0)
    slab_angles = times[:, None] * all_omegas(freq_count)[None, :]
    slab_table = jnp.concatenate(
        [TIME_STEP * jnp.cos(slab_angles), -TIME_STEP * jnp.sin(slab_angles)], axis=1
    )
    slab_next = slab_spectra + jnp.einsum(
        "csxy,sf->cfxy", slab_records, slab_table, precision=lax.Precision.HIGHEST
    )
    half_lag = jnp.array([0.0, 0.0, 0.5, 0.5], jnp.float32) * TIME_STEP
    monitor_times = times[None, :] - half_lag[:, None]
    monitor_angles = (
        monitor_times[:, :, None] * picked_omegas(wave_index, freq_count)[None, None, :]
    )
    real_part = jnp.einsum(
        "csxy,csw->wcxy",
        monitor_records,
        TIME_STEP * jnp.cos(monitor_angles),
        precision=lax.Precision.HIGHEST,
    )
    imag_part = jnp.einsum(
        "csxy,csw->wcxy",
        monitor_records,
        -TIME_STEP * jnp.sin(monitor_angles),
        precision=lax.Precision.HIGHEST,
    )
    monitor_next = monitor_spectra + jnp.stack([real_part, imag_part], axis=1)
    return (slab_next, monitor_next)


def per_device(
    electric, magnetic, material, permittivity, slab_spectra, monitor_spectra, wave_index
):
    inverse = inverse_map(material, permittivity)
    slab_list = []
    plane_list = []
    for repeat in range(2):
        electric, magnetic = advance(electric, magnetic, inverse)
        slab_layer, monitor_plane = records_of(electric, magnetic)
        slab_list.append(slab_layer)
        plane_list.append(monitor_plane)
    slab_records = jnp.stack(slab_list, axis=1)
    monitor_records = jnp.stack(plane_list, axis=1)
    slab_next, monitor_next = spectra_update(
        slab_spectra, monitor_spectra, slab_records, monitor_records, wave_index
    )
    local_x = monitor_next.shape[3]
    local_y = monitor_next.shape[4]
    global_x = local_x * lax.axis_size("gx")
    global_y = local_y * lax.axis_size("gy")
    gathered = lax.all_to_all(monitor_next, "gy", split_axis=0, concat_axis=4, tiled=True)
    full_table = order_table(global_y, OY, global_y)
    spectrum_y = jnp.einsum(
        "wicxy,ioyk->wockx", gathered, full_table, precision=lax.Precision.HIGHEST
    )
    x_table = order_table(global_x, OX, global_x)
    scaling = 1.0 / math.sqrt(global_x * global_y)
    orders = (
        jnp.einsum(
            "wicqx,ioxk->wocqk",
            lax.all_to_all(spectrum_y, "gx", split_axis=3, concat_axis=4, tiled=True),
            x_table,
            precision=lax.Precision.HIGHEST,
        )
        * scaling
    )
    return (electric, magnetic, slab_next, monitor_next, orders)


def solution(mesh):
    in_specs = (
        P(None, None, "gx", "gy"),
        P(None, None, "gx", "gy"),
        P(None, "gx", "gy"),
        P(),
        P(None, None, "gx", "gy"),
        P(None, None, None, "gx", "gy"),
        P(),
    )
    out_specs = (
        P(None, None, "gx", "gy"),
        P(None, None, "gx", "gy"),
        P(None, None, "gx", "gy"),
        P(None, None, None, "gx", "gy"),
        P("gy", None, None, "gx", None),
    )
    return jax.shard_map(
        per_device, mesh=mesh, in_specs=in_specs, out_specs=out_specs, check_vma=False
    )
```

profile of v0, /device:TPU:0, one launch (start us, length us, event | category | flops | bytes accessed | tf_op | source)
XLA Modules:
  0.0 81.0 jit_solution(13081951481231345476)
XLA Ops:
  0.7 0.9 %fusion.106 = (f32[1,16,8,128]{3,2,1,0:T(8,128)S(1)}, f32[1,16,8,128]{3,2,1,0:T(8,128)S(1)}, f32[1,16,8,128]{3,2,1,0:T(8,128)S(1)}) fusion(f32[3,16,8,128]{3,2,1,0:T(8,128)} %param.8), kind=kLoop, calls=%fused_computation.212 | loop fusion | bytes 393216 | tf_op jit(solution)/shard_map/slice | solution.py:60
  1.7 3.4 %collective-permute-start = (f32[2,16,1,128]{3,1,2,0:T(8,128)S(1)}, f32[2,16,1,128]{3,1,2,0:T(8,128)S(1)}, u32[]{:S(2)}, u32[]{:S(2)}) collective-permute-start(f32[2,16,1,128]{3,1,2,0:T(8,128)S(1)} %pad_maximum_fusion.3), channel_id=1, source_target_pairs={{4,0},{8,4},{12,8},{16,12},{20,16},{24,20},{28,24},{0,28},{5,1},{9... | collective-permute-start | bytes 49160 | tf_op jit(solution)/shard_map/ppermute | solution.py:20
  5.3 3.7 %collective-permute-start.1 = (f32[2,16,8,1]{1,2,3,0:T(8,128)S(1)}, f32[2,16,8,1]{1,2,3,0:T(8,128)S(1)}, u32[]{:S(2)}, u32[]{:S(2)}) collective-permute-start(f32[2,16,8,1]{1,2,3,0:T(8,128)S(1)} %pad_maximum_fusion.11), channel_id=1, source_target_pairs={{1,0},{2,1},{3,2},{0,3},{5,4},{6,5},{7,6},{4,7},{9,8},{10,9},{11,1... | collective-permute-start | bytes 3080 | tf_op jit(solution)/shard_map/ppermute | solution.py:20
  8.9 0.9 %fusion.104 = (f32[1,15,8,128]{3,2,1,0:T(8,128)S(1)}, f32[1,15,8,128]{3,2,1,0:T(8,128)S(1)}) fusion(f32[3,16,8,128]{3,2,1,0:T(8,128)} %param.8), kind=kLoop, calls=%fused_computation.210 | loop fusion | bytes 245760 | tf_op jit(solution)/shard_map/slice | solution.py:24
  9.9 0.9 %fusion.105 = (f32[1,16,8,128]{3,2,1,0:T(8,128)S(1)}, f32[1,16,8,128]{3,2,1,0:T(8,128)S(1)}) fusion(f32[3,16,8,128]{3,2,1,0:T(8,128)} %param.9), kind=kLoop, calls=%fused_computation.211 | loop fusion | bytes 262144 | tf_op jit(solution)/shard_map/slice | solution.py:67
  10.8 1.0 %fusion.18 = (f32[1,512,128]{2,1,0:T(8,128)S(1)}, f32[1,512,128]{2,1,0:T(8,128)S(1)}, f32[1,512,128]{2,1,0:T(8,128)S(1)}) fusion(s32[128]{0:T(128)S(1)} %and_select_fusion), kind=kLoop, calls=%fused_computation.33 | loop fusion | flops 983040 | bytes 786944 | tf_op jit(solution)/shard_map/neg | solution.py:56
  11.8 0.1 fusion.75
  12.1 0.2 select_reduce_fusion
  12.3 0.6 fusion.108
  16.1 0.1 fusion.29
  16.2 0.2 slice_reduce_fusion.1
  16.4 0.9 %bitcast_subtract_fusion = f32[16,8,128]{2,1,0:T(8,128)S(1)} fusion(f32[16,8,128]{2,0,1:T(8,128)S(1)} %get-tuple-element.43, f32[3,16,8,128]{3,2,1,0:T(8,128)} %param.9), kind=kLoop, calls=%fused_computation.99 | loop fusion | flops 16384 | bytes 196608 | tf_op jit(solution)/shard_map/sub | solution.py:68
  17.4 0.2 slice_reduce_fusion.2
  17.7 5.4 %collective-permute-done.2 = f32[2,16,8,1]{1,2,3,0:T(8,128)S(1)} collective-permute-done((f32[2,16,8,1]{1,2,3,0:T(8,128)S(1)}, f32[2,16,8,1]{1,2,3,0:T(8,128)S(1)}, u32[]{:S(2)}, u32[]{:S(2)}) %collective-permute-start.2) | collective-permute-done | bytes 1056 | tf_op jit(solution)/shard_map/ppermute | solution.py:20
  23.1 0.1 copy.233
  23.7 0.9 %bitcast_add_fusion = f32[16,8,128]{2,1,0:T(8,128)S(1)} fusion(f32[16,8,128]{2,0,1:T(8,128)S(1)} %get-tuple-element.39, f32[3,16,8,128]{3,2,1,0:T(8,128)} %param.8), kind=kLoop, calls=%fused_computation.91 | loop fusion | flops 16384 | bytes 196608 | tf_op jit(solution)/shard_map/add | solution.py:82
  25.0 1.5 %collective-permute-start.4 = (f32[2,16,1,128]{3,1,2,0:T(8,128)S(1)}, f32[2,16,1,128]{3,1,2,0:T(8,128)S(1)}, u32[]{:S(2)}, u32[]{:S(2)}) collective-permute-start(f32[2,16,1,128]{3,1,2,0:T(8,128)S(1)} %pad_maximum_fusion.5), channel_id=1, source_target_pairs={{4,0},{8,4},{12,8},{16,12},{20,16},{24,20},{28,24},{0,28},{5,1},{9... | collective-permute-start | bytes 49160 | tf_op jit(solution)/shard_map/ppermute | solution.py:20
  26.5 1.9 %collective-permute-done.5 = f32[2,16,8,1]{1,2,3,0:T(8,128)S(1)} collective-permute-done((f32[2,16,8,1]{1,2,3,0:T(8,128)S(1)}, f32[2,16,8,1]{1,2,3,0:T(8,128)S(1)}, u32[]{:S(2)}, u32[]{:S(2)}) %collective-permute-start.5) | collective-permute-done | bytes 1056 | tf_op jit(solution)/shard_map/ppermute | solution.py:20
  28.5 0.1 copy.247
  29.1 0.1 copy.256
  29.3 0.1 copy.257
  29.4 1.0 %collective-permute-start.6 = (f32[2,16,8,1]{1,2,3,0:T(8,128)S(1)}, f32[2,16,8,1]{1,2,3,0:T(8,128)S(1)}, u32[]{:S(2)}, u32[]{:S(2)}) collective-permute-start(f32[2,16,8,1]{1,2,3,0:T(8,128)S(1)} %pad_maximum_fusion.14), channel_id=1, source_target_pairs={{3,0},{0,1},{1,2},{2,3},{7,4},{4,5},{5,6},{6,7},{11,8},{8,9},{9,10... | collective-permute-start | bytes 3080 | tf_op jit(solution)/shard_map/ppermute | solution.py:20
  30.6 4.3 %collective-permute-done.6 = f32[2,16,8,1]{1,2,3,0:T(8,128)S(1)} collective-permute-done((f32[2,16,8,1]{1,2,3,0:T(8,128)S(1)}, f32[2,16,8,1]{1,2,3,0:T(8,128)S(1)}, u32[]{:S(2)}, u32[]{:S(2)}) %collective-permute-start.6) | collective-permute-done | bytes 1056 | tf_op jit(solution)/shard_map/ppermute | solution.py:20
  34.9 0.1 copy.259
  35.1 0.1 copy.269
  35.3 0.7 fusion.48
  36.0 0.6 convolution_bitcast_fusion.3
  36.6 0.6 convolution_bitcast_fusion.2
  37.2 0.3 maximum_add_fusion
  37.6 1.0 %copy.286 = f32[16,2,4,8,128]{4,3,2,1,0:T(8,128)} copy(f32[16,2,4,8,128]{4,0,3,2,1:T(8,128)S(1)} %maximum_add_fusion) | data formatting | bytes 1048576
  38.5 4.1 %all-to-all-start = ((f32[16,2,4,8,128]{4,3,2,1,0:T(8,128)}), f32[16,2,4,8,128]{4,3,2,1,0:T(8,128)}, u32[]{:S(2)}, u32[]{:S(2)}) async-start(f32[16,2,4,8,128]{4,3,2,1,0:T(8,128)} %copy.286), calls=%async_computation | async-start | bytes 1048576 | tf_op jit(solution)/shard_map/all_to_all | solution.py:146
  42.9 0.7 pad_maximum_fusion.1
  43.6 0.7 copy.271
  44.3 1.2 %fusion = f32[2,128,8,128]{3,1,2,0:T(8,128)S(1)} fusion(f32[2,128,8,128]{3,2,1,0:T(8,128)S(1)} %copy-done, f32[1,16,8,128]{3,1,2,0:T(8,128)S(1)} %copy.272, f32[1,16,8,128]{3,1,2,0:T(8,128)S(1)} %fusion.41, f32[1,16,8,128]{3,1,2,0:T(8,128)S(1)} %bitcast.224, f32[1,16,8,128]{3,1,2,0:T(8,128)S(1)} %bitcast.218, f32[2,64]{1,0:T(2,128)S(1)} %get-tuple-element.65, ...), kind=kOutput, calls=%fused_computation.1 | convolution fusion | flops 6590720 | bytes 2360320 | tf_op jit(solution)/shard_map/csxy,sf->cfxy/dot_general | solution.py:102
  45.5 1.6 %copy.285 = f32[2,128,8,128]{3,2,1,0:T(8,128)} copy(f32[2,128,8,128]{3,1,2,0:T(8,128)S(1)} %fusion) | data formatting | bytes 2097152
  47.1 7.5 %all-to-all-done = f32[16,2,4,8,128]{4,3,2,1,0:T(8,128)} async-done(((f32[16,2,4,8,128]{4,3,2,1,0:T(8,128)}), f32[16,2,4,8,128]{4,3,2,1,0:T(8,128)}, u32[]{:S(2)}, u32[]{:S(2)}) %all-to-all-start) | async-done | bytes 524320 | tf_op jit(solution)/shard_map/all_to_all | solution.py:146
  54.6 2.4 %convolution_bitcast_fusion.4 = f32[4,2,4,128,8]{3,4,2,0,1:T(8,128)} fusion(f32[1,2,512,128]{3,2,0,1:T(8,128)S(1)} %get-tuple-element.28, f32[1,2,512,128]{3,2,0,1:T(8,128)S(1)} %get-tuple-element.27, f32[4,4,2,4,8,128]{5,4,3,2,1,0:T(8,128)} %bitcast.77), kind=kOutput, calls=%fused_computation.7 | convolution fusion | flops 402915328 | bytes 1703936 | tf_op jit(solution)/shard_map/wicxy,ioyk->wockx/dot_general | solution.py:148
  57.0 2.3 %copy.282 = f32[4,2,4,128,8]{4,2,0,1,3:T(4,128)S(1)} copy(f32[4,2,4,128,8]{3,4,2,0,1:T(8,128)} %convolution_bitcast_fusion.4) | data formatting | bytes 262144 | tf_op jit(solution)/shard_map/wicxy,ioyk->wockx/transpose | solution.py:148
  59.4 3.1 %reshape.361 = f32[8,1,4096]{2,1,0:T(1,128)} reshape(f32[128,2,4,4,8]{4,3,2,1,0:T(4,128)S(1)} %bitcast.215) | data formatting | bytes 262144
  62.4 5.5 %all-to-all-start.1 = ((f32[8,1,4096]{2,1,0:T(1,128)}), f32[8,1,4096]{2,1,0:T(1,128)S(1)}, u32[]{:S(2)}, u32[]{:S(2)}) async-start(f32[8,1,4096]{2,1,0:T(1,128)} %reshape.361), calls=%async_computation.1 | async-start | bytes 262144 | tf_op jit(solution)/shard_map/all_to_all | solution.py:156
  67.9 0.7 pad_maximum_fusion
  68.6 4.8 %all-to-all-done.1 = f32[8,1,4096]{2,1,0:T(1,128)S(1)} async-done(((f32[8,1,4096]{2,1,0:T(1,128)}), f32[8,1,4096]{2,1,0:T(1,128)S(1)}, u32[]{:S(2)}, u32[]{:S(2)}) %all-to-all-start.1) | async-done | bytes 131104 | tf_op jit(solution)/shard_map/all_to_all | solution.py:156
  73.5 0.5 broadcast.523
  74.0 1.0 %reduce.10 = f32[8,4096]{1,0:T(8,128)S(1)} reduce(f32[8,1,4096]{2,1,0:T(1,128)S(1)} %all-to-all-done.1, f32[]{:T(128)} %broadcast.523), dimensions={1}, to_apply=%all_to_all.30.reduce_sub_computation | reduce | bytes 262148 | tf_op jit(solution)/shard_map/all_to_all | solution.py:156
  74.9 2.5 %reshape.362 = f32[128,2,4,4,8]{4,3,2,1,0:T(4,128)S(1)} reshape(f32[8,4096]{1,0:T(8,128)S(1)} %reduce.10) | data formatting | bytes 262144
  77.4 1.0 %copy.298 = f32[4,2,4,8,16,8]{4,5,3,1,2,0:T(8,128)S(1)} copy(f32[4,2,4,8,16,8]{5,2,0,1,4,3:T(4,128)S(1)} %bitcast.216) | data formatting | bytes 262144 | tf_op jit(solution)/shard_map/all_to_all | solution.py:156
  78.5 1.8 %fusion.2 = f32[4,2,4,16,64]{4,3,2,0,1:T(8,128)S(1)} fusion(f32[4,2,4,8,16,8]{4,5,3,1,2,0:T(8,128)S(1)} %copy.298, f32[1,2,64,64]{3,2,0,1:T(8,128)S(1)} %get-tuple-element.47, f32[1,2,64,64]{3,2,0,1:T(8,128)S(1)} %get-tuple-element.46), kind=kOutput, calls=%fused_computation.4 | convolution fusion | flops 50380800 | bytes 327680 | tf_op jit(solution)/shard_map/wicqx,ioxk->wocqk/dot_general | solution.py:154
  80.3 0.7 copy.287
  (103 shorter events, 2.8 us)
Async XLA Ops:
  0.6 11.4 %copy-start.6 = (f32[4]{0:T(128)S(1)}, f32[4]{0:T(128)}, u32[]{:S(2)}) copy-start(f32[4]{0:T(128)} %constant.111) | copy-start | bytes 52
  0.6 11.4 %copy-start.7 = (s32[16]{0:T(128)S(1)}, s32[16]{0:T(128)}, u32[]{:S(2)}) copy-start(s32[16]{0:T(128)} %param.14) | copy-start | bytes 196
  0.7 11.6 %copy-start.5 = (f32[4]{0:T(128)S(1)}, f32[4]{0:T(128)}, u32[]{:S(2)}) copy-start(f32[4]{0:T(128)} %param.11) | copy-start | bytes 52
  1.7 14.4 %collective-permute-start = (f32[2,16,1,128]{3,1,2,0:T(8,128)S(1)}, f32[2,16,1,128]{3,1,2,0:T(8,128)S(1)}, u32[]{:S(2)}, u32[]{:S(2)}) collective-permute-start(f32[2,16,1,128]{3,1,2,0:T(8,128)S(1)} %pad_maximum_fusion.3), channel_id=1, source_target_pairs={{4,0},{8,4},{12,8},{16,12},{20,16},{24,20},{28,24},{0,28},{5,1},{9... | collective-permute-start | bytes 49160 | tf_op jit(solution)/shard_map/ppermute | solution.py:20
  5.3 10.5 %collective-permute-start.1 = (f32[2,16,8,1]{1,2,3,0:T(8,128)S(1)}, f32[2,16,8,1]{1,2,3,0:T(8,128)S(1)}, u32[]{:S(2)}, u32[]{:S(2)}) collective-permute-start(f32[2,16,8,1]{1,2,3,0:T(8,128)S(1)} %pad_maximum_fusion.11), channel_id=1, source_target_pairs={{1,0},{2,1},{3,2},{0,3},{5,4},{6,5},{7,6},{4,7},{9,8},{10,9},{11,1... | collective-permute-start | bytes 3080 | tf_op jit(solution)/shard_map/ppermute | solution.py:20
  10.7 12.4 %copy-start.4 = (s32[16,8,128]{2,1,0:T(8,128)S(1)}, s32[16,8,128]{2,1,0:T(8,128)}, u32[]{:S(2)}) copy-start(s32[16,8,128]{2,1,0:T(8,128)} %param.10) | copy-start | bytes 196612
  17.3 6.3 %collective-permute-start.3 = (f32[2,16,1,128]{3,1,2,0:T(8,128)S(1)}, f32[2,16,1,128]{3,1,2,0:T(8,128)S(1)}, u32[]{:S(2)}, u32[]{:S(2)}) collective-permute-start(f32[2,16,1,128]{3,1,2,0:T(8,128)S(1)} %pad_maximum_fusion.4), channel_id=1, source_target_pairs={{28,0},{0,4},{4,8},{8,12},{12,16},{16,20},{20,24},{24,28},{29,1},{... | collective-permute-start | bytes 49160 | tf_op jit(solution)/shard_map/ppermute | solution.py:20
  17.6 5.5 %collective-permute-start.2 = (f32[2,16,8,1]{1,2,3,0:T(8,128)S(1)}, f32[2,16,8,1]{1,2,3,0:T(8,128)S(1)}, u32[]{:S(2)}, u32[]{:S(2)}) collective-permute-start(f32[2,16,8,1]{1,2,3,0:T(8,128)S(1)} %pad_maximum_fusion.12), channel_id=1, source_target_pairs={{3,0},{0,1},{1,2},{2,3},{7,4},{4,5},{5,6},{6,7},{11,8},{8,9},{9,10... | collective-permute-start | bytes 3080 | tf_op jit(solution)/shard_map/ppermute | solution.py:20
  24.8 3.7 %collective-permute-start.5 = (f32[2,16,8,1]{1,2,3,0:T(8,128)S(1)}, f32[2,16,8,1]{1,2,3,0:T(8,128)S(1)}, u32[]{:S(2)}, u32[]{:S(2)}) collective-permute-start(f32[2,16,8,1]{1,2,3,0:T(8,128)S(1)} %pad_maximum_fusion.13), channel_id=1, source_target_pairs={{1,0},{2,1},{3,2},{0,3},{5,4},{6,5},{7,6},{4,7},{9,8},{10,9},{11,1... | collective-permute-start | bytes 3080 | tf_op jit(solution)/shard_map/ppermute | solution.py:20
  25.0 3.7 %collective-permute-start.4 = (f32[2,16,1,128]{3,1,2,0:T(8,128)S(1)}, f32[2,16,1,128]{3,1,2,0:T(8,128)S(1)}, u32[]{:S(2)}, u32[]{:S(2)}) collective-permute-start(f32[2,16,1,128]{3,1,2,0:T(8,128)S(1)} %pad_maximum_fusion.5), channel_id=1, source_target_pairs={{4,0},{8,4},{12,8},{16,12},{20,16},{24,20},{28,24},{0,28},{5,1},{9... | collective-permute-start | bytes 49160 | tf_op jit(solution)/shard_map/ppermute | solution.py:20
  28.9 8.3 %copy-start.1 = (f32[16,2,4,8,128]{4,3,2,1,0:T(8,128)S(1)}, f32[16,2,4,8,128]{4,3,2,1,0:T(8,128)}, u32[]{:S(2)}) copy-start(f32[16,2,4,8,128]{4,3,2,1,0:T(8,128)} %param.13) | copy-start | bytes 1572868
  29.4 5.5 %collective-permute-start.6 = (f32[2,16,8,1]{1,2,3,0:T(8,128)S(1)}, f32[2,16,8,1]{1,2,3,0:T(8,128)S(1)}, u32[]{:S(2)}, u32[]{:S(2)}) collective-permute-start(f32[2,16,8,1]{1,2,3,0:T(8,128)S(1)} %pad_maximum_fusion.14), channel_id=1, source_target_pairs={{3,0},{0,1},{1,2},{2,3},{7,4},{4,5},{5,6},{6,7},{11,8},{8,9},{9,10... | collective-permute-start | bytes 3080 | tf_op jit(solution)/shard_map/ppermute | solution.py:20
  30.5 4.7 %collective-permute-start.7 = (f32[2,16,1,128]{3,1,2,0:T(8,128)S(1)}, f32[2,16,1,128]{3,1,2,0:T(8,128)S(1)}, u32[]{:S(2)}, u32[]{:S(2)}) collective-permute-start(f32[2,16,1,128]{3,1,2,0:T(8,128)S(1)} %pad_maximum_fusion.6), channel_id=1, source_target_pairs={{28,0},{0,4},{4,8},{8,12},{12,16},{16,20},{20,24},{24,28},{29,1},{... | collective-permute-start | bytes 49160 | tf_op jit(solution)/shard_map/ppermute | solution.py:20
  37.6 6.7 %copy-start = (f32[2,128,8,128]{3,2,1,0:T(8,128)S(1)}, f32[2,128,8,128]{3,2,1,0:T(8,128)}, u32[]{:S(2)}) copy-start(f32[2,128,8,128]{3,2,1,0:T(8,128)} %param.12) | copy-start | bytes 3145732
  38.5 16.0 %all-to-all-start = ((f32[16,2,4,8,128]{4,3,2,1,0:T(8,128)}), f32[16,2,4,8,128]{4,3,2,1,0:T(8,128)}, u32[]{:S(2)}, u32[]{:S(2)}) async-start(f32[16,2,4,8,128]{4,3,2,1,0:T(8,128)} %copy.286), calls=%async_computation | async-start | bytes 1048576 | tf_op jit(solution)/shard_map/all_to_all | solution.py:146
  57.0 10.9 %copy-start.2 = (f32[1,16,8,128]{3,2,1,0:T(8,128)S(1)}, f32[1,16,8,128]{3,2,1,0:T(8,128)}, u32[]{:S(2)}) copy-start(f32[1,16,8,128]{3,2,1,0:T(8,128)} %copy.271) | copy-start | bytes 196612
  57.0 10.9 %copy-start.3 = (f32[1,16,8,128]{3,2,1,0:T(8,128)S(1)}, f32[1,16,8,128]{3,2,1,0:T(8,128)}, u32[]{:S(2)}) copy-start(f32[1,16,8,128]{3,2,1,0:T(8,128)} %get-tuple-element.37) | copy-start | bytes 196612
  62.4 11.0 %all-to-all-start.1 = ((f32[8,1,4096]{2,1,0:T(1,128)}), f32[8,1,4096]{2,1,0:T(1,128)S(1)}, u32[]{:S(2)}, u32[]{:S(2)}) async-start(f32[8,1,4096]{2,1,0:T(1,128)} %reshape.361), calls=%async_computation.1 | async-start | bytes 262144 | tf_op jit(solution)/shard_map/all_to_all | solution.py:156
where the time goes:
time: 81.6 us; the launch traced here: 81 us
  waiting for transfers between devices  24 us (29%)
  local copies, waits for them, and re-layouts  19.4 us (24%)
  starting transfers between devices  19.4 us (24%)
  other arithmetic  7.55 us (9%)
  matrix products  6.57 us (8%)
  between operations  4.05 us (5%)
    ppermute x8, waiting for transfers between devices, passed_along(): return lax.ppermute(block, axis, route)  11.6 us
    ppermute x8, starting transfers between devices, passed_along(): return lax.ppermute(block, axis, route)  9.81 us
    unnamed x24, local copies, waits for them, and re-layouts  8.9 us
    all_to_all x1, waiting for transfers between devices, per_device(): lax.all_to_all(monitor_next, 'gy', split_axis=0, concat_axis=4, tiled=True)  7.54 us
    all_to_all x1, starting transfers between devices, per_device(): lax.all_to_all(spectrum_y, 'gx', split_axis=3, concat_axis=4, tiled=True)  5.48 us
    all_to_all x1, waiting for transfers between devices, per_device(): lax.all_to_all(spectrum_y, 'gx', split_axis=3, concat_axis=4, tiled=True)  4.82 us
    all_to_all x1, starting transfers between devices, per_device(): lax.all_to_all(monitor_next, 'gy', split_axis=0, concat_axis=4, tiled=True)  4.14 us
    dot_general x1, matrix products, per_device(): jnp.einsum('wicxy,ioyk->wockx', gathered, full_table, precision=lax.Preci...  2.42 us
  transfers between devices with their start and end apart: 10, of which 5 were waited for; matrix products, arithmetic and copies ran while one was open for 14% of the time, Pallas kernels for 0%

commit v1 on v0

v1 whole, which is shorter than its diff:
```python
import functools
import math

import jax
import jax.numpy as jnp
import numpy as np
from jax import lax
from jax.experimental import pallas as pl
from jax.experimental.pallas import tpu as pltpu
from jax.sharding import PartitionSpec as P

OY = 128
OX = 64

TIME_STEP = 0.5
OMEGA_LOW = 0.15
OMEGA_HIGH = 0.8

STEPS = 2
EDGE = 2 * STEPS
SEAM = 2 * EDGE
DEEP = 4
KINDS = 7
RECORDS = 4

VMEM = pl.BlockSpec(memory_space=pltpu.VMEM)
SMEM = pl.BlockSpec(memory_space=pltpu.SMEM)
PARAMS = pltpu.CompilerParams(vmem_limit_bytes=48 * 1024 * 1024)


def passed_along(block, axis, distance):
    devices = range(lax.axis_size(axis))
    route = [((i - distance) % len(devices), i) for i in devices]
    return lax.ppermute(block, axis, route)


def rolled(values, shift, axis):
    shift %= values.shape[axis]
    return pltpu.roll(values, shift, axis) if shift else values


def iota(shape, axis):
    return lax.broadcasted_iota(jnp.int32, shape, axis)


def rates_of(permittivity, classes, shape):
    return [TIME_STEP / jnp.full(shape, permittivity[k], jnp.float32) for k in range(classes)]


def rate_at(material, rates):
    rate = rates[-1]
    for k in range(len(rates) - 2, -1, -1):
        rate = jnp.where(material == k, rates[k], rate)
    return rate


class Leapfrog:
    def __init__(self, start, layers=None, above=None, below=None):
        self.start = start
        self.layers = layers
        self.above = above
        self.below = below
        self.known = {}

    def first(self, z):
        if ("0", z) not in self.known:
            self.known["0", z] = self.start(z)
        return self.known["0", z]

    def e(self, s, z):
        if s == 0:
            return self.first(z)[0:3]
        if ("e", s, z) not in self.known:
            ex, ey, ez = self.e(s - 1, z)
            hx, hy, hz = self.h(s, z)
            if self.layers is None:
                down_x, down_y = self.below(hx), self.below(hy)
            else:
                down_x, down_y = self.h(s, z - 1)[:2] if z else (0.0, 0.0)
            rate = self.first(z)[6]
            self.known["e", s, z] = (
                ex + rate * ((hz - rolled(hz, 1, 1)) - (hy - down_y)),
                ey + rate * ((hx - down_x) - (hz - rolled(hz, 1, 0))),
                ez + rate * ((hy - rolled(hy, 1, 0)) - (hx - rolled(hx, 1, 1))),
            )
        return self.known["e", s, z]

    def h(self, s, z):
        if s == 0:
            return self.first(z)[3:6]
        if ("h", s, z) not in self.known:
            ex, ey, ez = self.e(s - 1, z)
            hx, hy, hz = self.h(s - 1, z)
            if self.layers is None:
                up_x, up_y = self.above(ex), self.above(ey)
            else:
                up_x, up_y = self.e(s - 1, z + 1)[:2] if z + 1 < self.layers else (0.0, 0.0)
            self.known["h", s, z] = (
                hx - TIME_STEP * ((rolled(ez, -1, 1) - ez) - (up_y - ey)),
                hy - TIME_STEP * ((up_x - ex) - (rolled(ez, -1, 0) - ez)),
                hz - TIME_STEP * ((rolled(ey, -1, 0) - ey) - (rolled(ex, -1, 1) - ex)),
            )
        return self.known["h", s, z]

    def records(self, s, z):
        return self.e(s, z)[:2] + self.h(s, z)[:2]


def seam_leapfrog(tiles, layers):
    layer = iota(tiles[0].shape, 1) // SEAM % layers
    return Leapfrog(
        lambda z: tiles,
        above=lambda f: jnp.where(layer < layers - 1, rolled(f, -SEAM, 1), 0.0),
        below=lambda f: jnp.where(layer > 0, rolled(f, SEAM, 1), 0.0),
    )


def own_planes(e_ref, h_ref, m_ref, rates):
    def at(z):
        rate = rate_at(m_ref[z], rates)
        return [e_ref[c, z] for c in range(3)] + [h_ref[c, z] for c in range(3)] + [rate]

    return at


def widened_planes(own, before_ref, after_ref, first_group=0):
    def at(z):
        planes = own(z)
        rows = planes[0].shape[0]
        group, place = divmod(z, rows // STEPS)
        row = iota(planes[0].shape, 0)
        wide = []
        for kind in range(KINDS):
            after = rolled(after_ref[kind, group], -STEPS * place, 0)
            before = rolled(before_ref[kind, group], rows - STEPS - STEPS * place, 0)
            halo = jnp.where(row < STEPS, after, before)
            wide.append(jnp.concatenate([planes[kind], halo], axis=0))
        return wide

    return at


def pack_faces(perm_ref, e_ref, h_ref, m_ref, forth_ref, back_ref):
    layers, rows, columns = m_ref.shape
    rates = rates_of(perm_ref, perm_ref.shape[0], (rows, columns))
    own = own_planes(e_ref, h_ref, m_ref, rates)
    row = iota((rows, columns), 0)
    per_group = rows // STEPS
    for group in range(layers // per_group):
        planes = [own(group * per_group + place) for place in range(per_group)]
        for kind in range(KINDS):
            forth = rolled(planes[0][kind], STEPS - rows, 0)
            back = planes[0][kind]
            for place in range(1, per_group):
                spot = STEPS * place
                here = planes[place][kind]
                forth = jnp.where(row >= spot, rolled(here, spot + STEPS - rows, 0), forth)
                back = jnp.where(row >= spot, rolled(here, spot, 0), back)
            forth_ref[kind, group] = forth
            back_ref[kind, group] = back


def packed_edges(planes, layers, spot):
    tile = None
    for z in range(layers):
        here = rolled(planes[z], spot + z * SEAM + EDGE, 1)
        if tile is None:
            tile = here
        else:
            tile = jnp.where(iota(tile.shape, 1) >= spot + z * SEAM, here, tile)
    return tile


def monitor_message(perm_ref, e_ref, h_ref, m_ref, before_ref, after_ref, message_ref):
    layers, rows, columns = m_ref.shape
    rates = rates_of(perm_ref, perm_ref.shape[0], (rows, columns))
    wide = widened_planes(own_planes(e_ref, h_ref, m_ref, rates), before_ref, after_ref)
    walk = Leapfrog(wide, layers=layers)
    span = layers * SEAM
    per_tile = columns // span
    lane = iota((2 * rows, columns), 1)
    for tile in range(-(-KINDS // per_tile)):
        total = None
        for place in range(min(per_tile, KINDS - tile * per_tile)):
            kind = tile * per_tile + place
            edges = packed_edges([walk.first(z)[kind] for z in range(layers)], layers, place * span)
            total = edges if total is None else jnp.where(lane >= place * span, edges, total)
        message_ref[pl.ds(tile * 2 * rows, 2 * rows), :] = total
    base = -(-KINDS // per_tile) * 2 * rows
    for s in range(STEPS):
        for c, record in enumerate(walk.records(s + 1, layers - 1)):
            message_ref[pl.ds(base + (s * RECORDS + c) * rows, rows), :] = record[:rows]


def all_edges(perm_ref, e_ref, h_ref, m_ref, before_ref, after_ref, edges_ref):
    layers, rows, columns = m_ref.shape
    rates = rates_of(perm_ref, perm_ref.shape[0], (rows, columns))
    wide = widened_planes(own_planes(e_ref, h_ref, m_ref, rates), before_ref, after_ref)
    planes = [wide(z) for z in range(layers)]
    for kind in range(KINDS):
        edges_ref[kind] = packed_edges([planes[z][kind] for z in range(layers)], layers, 0)


def waves_of(coef_ref, wave):
    base = wave * (STEPS * 4)
    return lambda s, half, part: coef_ref[base + (s * 2 + half) * 2 + part]


def y_orders(group_waves, blocks, me_ref, wave_ref, coef_ref, table_ref, *refs):
    messages = refs[:blocks]
    spectra = refs[blocks : 2 * blocks]
    out_ref = refs[2 * blocks]
    _, _, _, rows, columns = spectra[0].shape
    me = me_ref[0]
    layers = DEEP
    span = layers * SEAM
    per_tile = columns // span
    lane = iota((2 * rows, columns), 1)
    column = lane % SEAM
    walks = []
    for tile in range(-(-blocks // per_tile)):
        seams = range(tile * per_tile, min(blocks, (tile + 1) * per_tile))
        kinds = []
        for kind in range(KINDS):
            source = pl.ds(kind // per_tile * 2 * rows, 2 * rows)
            total = None
            for seam in seams:
                spot = (seam % per_tile) * span
                shift = spot - kind % per_tile * span
                left = rolled(messages[seam][source, :], shift, 1)
                right = rolled(messages[(seam + 1) % blocks][source, :], shift, 1)
                here = jnp.where(column < EDGE, left, right)
                total = here if total is None else jnp.where(lane >= spot, here, total)
            kinds.append(total)
        walks.append(seam_leapfrog(kinds, layers))
    base = -(-KINDS // per_tile) * 2 * rows
    narrow = iota((rows, columns), 1)
    coefs = [waves_of(coef_ref, wave_ref[me * group_waves + w]) for w in range(group_waves)]
    total = None
    for block in range(blocks):
        record = []
        for s in range(STEPS):
            for c in range(RECORDS):
                value = messages[block][pl.ds(base + (s * RECORDS + c) * rows, rows), :]
                after, before = block, (block - 1) % blocks
                spot_after = (after % per_tile) * span + (layers - 1) * SEAM + EDGE
                spot_before = (before % per_tile) * span + (layers - 1) * SEAM + EDGE
                from_after = walks[after // per_tile].records(s + 1, 0)[c][:rows]
                from_before = walks[before // per_tile].records(s + 1, 0)[c][:rows]
                value = jnp.where(narrow >= columns - STEPS, rolled(from_after, -spot_after, 1), value)
                value = jnp.where(narrow < STEPS, rolled(from_before, -spot_before, 1), value)
                record.append(value)
        parts = []
        for part in range(2):
            for w in range(group_waves):
                for c in range(RECORDS):
                    value = spectra[block][w, part, c]
                    for s in range(STEPS):
                        value = value + coefs[w](s, c // 2, part) * record[s * RECORDS + c]
                    parts.append(value)
        values = jnp.concatenate(parts, axis=0)
        owner = lax.rem(me + block, blocks)
        table = table_ref[pl.ds(pl.multiple_of(owner * columns, columns), columns), :]
        product = jnp.dot(
            values, table, precision=lax.Precision.HIGHEST, preferred_element_type=jnp.float32
        )
        total = product if total is None else total + product
    half = group_waves * RECORDS * rows
    real = total[:half, :OY] + total[half:, OY:]
    imag = total[half:, :OY] - total[:half, OY:]
    sources = group_waves * RECORDS
    targets = out_ref.shape[0]
    kept = OY // targets
    wide = iota((rows, OY), 1)
    per_out = OY // kept
    for target in range(targets):
        for part, values in enumerate((real, imag)):
            for first in range(0, sources, per_out):
                tile = None
                for source in range(first, min(sources, first + per_out)):
                    spot = (source - first) * kept
                    here = values[source * rows : (source + 1) * rows]
                    here = rolled(here, spot - target * kept, 1)
                    tile = here if tile is None else jnp.where(wide >= spot, here, tile)
                place = (first // per_out * 2 + part) * rows
                out_ref[target, pl.ds(place, rows), :] = tile


def x_orders(kept, values_ref, table_ref, out_ref):
    sources, height, lanes = values_ref.shape
    waves, _, records, _, _ = out_ref.shape
    depth = table_ref.shape[0]
    rows = depth // sources
    per_tile = lanes // kept
    for tile in range(height // rows):
        values = jnp.concatenate(
            [values_ref[source, pl.ds(tile * rows, rows), :] for source in range(sources)], axis=0
        )
        result = lax.dot_general(
            values,
            table_ref[...],
            (((0,), (0,)), ((), ())),
            precision=lax.Precision.HIGHEST,
            preferred_element_type=jnp.float32,
        )
        for place in range(per_tile):
            wave, record = divmod(tile * per_tile + place, records)
            if wave < waves:
                here = result[place * kept : (place + 1) * kept]
                out_ref[wave, 0, record] = here[:, :OX]
                out_ref[wave, 1, record] = here[:, OX:]


def local_updates(
    perm_ref,
    wave_ref,
    coef_ref,
    e_ref,
    h_ref,
    m_ref,
    before_ref,
    after_ref,
    edges_ref,
    edges_before_ref,
    edges_after_ref,
    slab_ref,
    monitor_ref,
    e_out,
    h_out,
    slab_out,
    monitor_out,
):
    layers, rows, columns = m_ref.shape
    rates = rates_of(perm_ref, perm_ref.shape[0], (rows, columns))
    wide = widened_planes(own_planes(e_ref, h_ref, m_ref, rates), before_ref, after_ref)
    walk = Leapfrog(wide, layers=layers)
    left = iota((2 * rows, layers * SEAM), 1) % SEAM < EDGE
    mine = [edges_ref[kind] for kind in range(KINDS)]
    after = seam_leapfrog(
        [jnp.where(left, mine[k], edges_after_ref[k]) for k in range(KINDS)], layers
    )
    before = seam_leapfrog(
        [jnp.where(left, edges_before_ref[k], mine[k]) for k in range(KINDS)], layers
    )
    column = iota((rows, columns), 1)
    inner = (column >= STEPS) & (column < columns - STEPS)
    joined = {}

    def mended(s, z, kind):
        if (s, kind) not in joined:
            ends = [(side.e(s, 0) + side.h(s, 0))[kind][:rows] for side in (after, before)]
            joined[s, kind] = jnp.where(left[:rows], ends[0], ends[1])
        value = (walk.e(s, z) + walk.h(s, z))[kind][:rows]
        return jnp.where(inner, value, rolled(joined[s, kind], -(z * SEAM + EDGE), 1))

    middle = layers // 2
    slab_records = [[None] * 2 for _ in range(STEPS)]
    records = [[None] * RECORDS for _ in range(STEPS)]
    for z in range(layers):
        for kind in range(6):
            value = mended(STEPS, z, kind)
            if kind < 3:
                e_out[kind, z] = value
            else:
                h_out[kind - 3, z] = value
        for s in range(STEPS):
            if z == middle:
                slab_records[s] = [mended(s + 1, z, kind) for kind in (0, 1)]
            if z == layers - 1:
                records[s] = [mended(s + 1, z, kind) for kind in (0, 1, 3, 4)]
    frequencies = slab_ref.shape[1] // 2

    def one_frequency(f, carry):
        coef = waves_of(coef_ref, f)
        for c in range(2):
            for part in range(2):
                value = slab_ref[c, part * frequencies + f]
                for s in range(STEPS):
                    value = value + coef(s, 0, part) * slab_records[s][c]
                slab_out[c, part * frequencies + f] = value
        return carry

    lax.fori_loop(0, frequencies, one_frequency, 0, unroll=4)
    for w in range(monitor_ref.shape[0]):
        coef = waves_of(coef_ref, wave_ref[w])
        for part in range(2):
            for c in range(RECORDS):
                value = monitor_ref[w, part, c]
                for s in range(STEPS):
                    value = value + coef(s, c // 2, part) * records[s][c]
                monitor_out[w, part, c] = value


def wave_coefficients(freq_count):
    omegas = OMEGA_LOW + (OMEGA_HIGH - OMEGA_LOW) * np.arange(freq_count) / (freq_count - 1)
    times = TIME_STEP * (np.arange(1, STEPS + 1)[:, None] - np.array([0.0, 0.5])[None, :])
    angles = omegas[:, None, None] * times[None]
    table = np.stack([TIME_STEP * np.cos(angles), -TIME_STEP * np.sin(angles)], axis=-1)
    return table.reshape(-1).astype(np.float32)


def angles_of(length, kept):
    wanted = (np.arange(kept) - kept // 2) % length
    return 2.0 * math.pi / length * (np.arange(length)[:, None] * wanted[None, :] % length)


def y_table(length):
    angles = angles_of(length, OY)
    return np.concatenate([np.cos(angles), np.sin(angles)], axis=1).astype(np.float32)


def x_table(length, blocks, scaling):
    angles = angles_of(length, OX).reshape(blocks, length // blocks, OX)
    real = np.concatenate([np.cos(angles), -np.sin(angles)], axis=2)
    imag = np.concatenate([np.sin(angles), np.cos(angles)], axis=2)
    table = np.stack([real, imag], axis=1) * scaling
    return table.reshape(2 * length, 2 * OX).astype(np.float32)


def call(kernel, in_specs, shapes, *operands, name, flops=0, moved=0, **more):
    out = [jax.ShapeDtypeStruct(shape, jnp.float32) for shape in shapes]
    return pl.pallas_call(
        kernel,
        out_shape=out,
        in_specs=in_specs,
        out_specs=[VMEM] * len(out) if "grid" not in more else more.pop("out_specs"),
        compiler_params=PARAMS,
        cost_estimate=pl.CostEstimate(flops=flops, bytes_accessed=moved, transcendentals=0),
        name=name,
        **more,
    )(*operands)


def per_device(
    electric, magnetic, material, permittivity, slab_spectra, monitor_spectra, wave_index
):
    layers, rows, columns = material.shape
    x_blocks, y_blocks = lax.axis_size("gx"), lax.axis_size("gy")
    waves = monitor_spectra.shape[0]
    group_waves = waves // y_blocks
    me = lax.axis_index("gy")
    fields = (electric, magnetic, material)
    groups = layers * STEPS // rows

    faces = (KINDS, groups, rows, columns)
    forth, back = call(
        pack_faces,
        [SMEM] + [VMEM] * 3,
        [faces, faces],
        permittivity,
        *fields,
        name="pack_faces",
        flops=10**5,
        moved=10**6,
    )
    before = passed_along(forth, "gx", 1)
    after = passed_along(back, "gx", -1)

    spectra = [lax.dynamic_slice_in_dim(monitor_spectra, me * group_waves, group_waves, 0)]
    for distance in range(1, y_blocks):
        target = (me - distance) % y_blocks
        block = lax.dynamic_slice_in_dim(monitor_spectra, target * group_waves, group_waves, 0)
        spectra.append(passed_along(block, "gy", -distance))

    top = (layers - DEEP) // DEEP
    top_group = groups - 1
    tiles = -(-KINDS // (columns // (DEEP * SEAM)))
    height = tiles * 2 * rows + STEPS * RECORDS * rows
    fields_spec = pl.BlockSpec((3, DEEP, rows, columns), lambda i: (0, top, 0, 0))
    faces_spec = pl.BlockSpec((KINDS, 1, rows, columns), lambda i: (0, top_group, 0, 0))
    (message,) = call(
        monitor_message,
        [
            SMEM,
            fields_spec,
            fields_spec,
            pl.BlockSpec((DEEP, rows, columns), lambda i: (top, 0, 0)),
            faces_spec,
            faces_spec,
        ],
        [(height, columns)],
        permittivity,
        *fields,
        before,
        after,
        name="monitor_message",
        flops=10**5,
        moved=10**5,
        grid=(1,),
        out_specs=[pl.BlockSpec((height, columns), lambda i: (0, 0))],
    )
    messages = [message]
    for distance in range(1, y_blocks):
        messages.append(passed_along(message, "gy", -distance))

    (edges,) = call(
        all_edges,
        [SMEM] + [VMEM] * 5,
        [(KINDS, 2 * rows, layers * SEAM)],
        permittivity,
        *fields,
        before,
        after,
        name="all_edges",
        flops=10**5,
        moved=10**6,
    )
    edges_before = passed_along(edges, "gy", 1)
    edges_after = passed_along(edges, "gy", -1)

    coefs = jnp.asarray(wave_coefficients(slab_spectra.shape[1] // 2))
    length_x, length_y = rows * x_blocks, columns * y_blocks
    kept = OY // x_blocks
    out_tiles = -(-group_waves * RECORDS * kept // OY)
    (spectrum_y,) = call(
        functools.partial(y_orders, group_waves, y_blocks),
        [SMEM] * 3 + [VMEM] * (1 + 2 * y_blocks),
        [(x_blocks, out_tiles * 2 * rows, OY)],
        me.reshape(1),
        wave_index,
        coefs,
        jnp.asarray(y_table(length_y)),
        *messages,
        *spectra,
        name="y_orders",
        flops=10**8,
        moved=2 * 10**6,
    )
    swapped = lax.all_to_all(spectrum_y, "gx", split_axis=0, concat_axis=0, tiled=True)

    electric_next, magnetic_next, slab_next, monitor_next = call(
        local_updates,
        [SMEM] * 3 + [VMEM] * 10,
        [electric.shape, magnetic.shape, slab_spectra.shape, monitor_spectra.shape],
        permittivity,
        wave_index,
        coefs,
        *fields,
        before,
        after,
        edges,
        edges_before,
        edges_after,
        slab_spectra,
        monitor_spectra,
        name="local_updates",
        flops=10**7,
        moved=6 * 10**6,
    )

    scaling = 1.0 / math.sqrt(length_x * length_y)
    (orders,) = call(
        functools.partial(x_orders, kept),
        [VMEM] * 2,
        [(group_waves, 2, RECORDS, kept, OX)],
        swapped,
        jnp.asarray(x_table(length_x, x_blocks, scaling)),
        name="x_orders",
        flops=10**7,
        moved=5 * 10**5,
    )
    return (electric_next, magnetic_next, slab_next, monitor_next, orders)


def solution(mesh):
    in_specs = (
        P(None, None, "gx", "gy"),
        P(None, None, "gx", "gy"),
        P(None, "gx", "gy"),
        P(),
        P(None, None, "gx", "gy"),
        P(None, None, None, "gx", "gy"),
        P(),
    )
    out_specs = (
        P(None, None, "gx", "gy"),
        P(None, None, "gx", "gy"),
        P(None, None, "gx", "gy"),
        P(None, None, None, "gx", "gy"),
        P("gy", None, None, "gx", None),
    )
    return jax.shard_map(
        per_device, mesh=mesh, in_specs=in_specs, out_specs=out_specs, check_vma=False
    )
```

time: 81.6 us -> 45.8 us (0.56)
  local copies, waits for them, and re-layouts: 19.4 us -> 1.88 us
  waiting for transfers between devices: 24 us -> 11.9 us
  Pallas kernels: 0 us -> 9.76 us
  other arithmetic: 7.55 us -> 0 us
  matrix products: 6.57 us -> 0 us
  between operations: 4.05 us -> 0.81 us
  starting transfers between devices: 19.4 us -> 21.2 us
    all_to_all x2 -> x1, waiting for transfers between devices: 12.4 us -> 0.01 us  [per_device(): lax.all_to_all(spectrum_y, 'gx', split_axis=0, concat_axis=0, tiled=True)]
    pallas_call x0 -> x6, Pallas kernels: none -> 9.76 us  [call(): pl.pallas_call(kernel, out_shape=out, in_specs=in_specs, out_specs=[VMEM]...]
    unnamed x24 -> x20, local copies, waits for them, and re-layouts: 8.9 us -> 0.68 us
    ppermute x8 -> x10, starting transfers between devices: 9.81 us -> 17.7 us  [passed_along(): return lax.ppermute(block, axis, route)]
    dot_general x5 -> x0, matrix products: 6.57 us -> none  [the longest x1 2.42 us: per_device(): jnp.einsum('wicxy,ioyk->wockx', gathered, full_table, precision=lax.Preci...]
    all_to_all x2 -> x1, starting transfers between devices: 9.62 us -> 3.5 us  [per_device(): lax.all_to_all(spectrum_y, 'gx', split_axis=0, concat_axis=0, tiled=True)]
    slice x29 -> x0, local copies, waits for them, and re-layouts: 4.81 us -> none  [the longest x1 0.93 us: advance(): electric_x, electric_y, electric_z = (electric[0], electric[1], electric[2])]
    another operation x19 -> x0, other arithmetic: 2.35 us -> none  [the longest x5 1.52 us: advance(): jnp.stack([new_x, new_y, new_z])]
  transfers between devices with their start and end apart: 10 -> 11, of which waited for: 5 -> 4; matrix products, arithmetic and copies ran while one was open for 14% -> 0% of each run, Pallas kernels for 0% -> 13%
where the time goes in v1:
time: 45.8 us; the launch traced here: 45.5 us
  starting transfers between devices  21.2 us (46%)
  waiting for transfers between devices  11.9 us (26%)
  Pallas kernels  9.76 us (21%)
  local copies, waits for them, and re-layouts  1.88 us (4%)
  between operations  0.81 us (2%)
    ppermute x10, starting transfers between devices, passed_along(): return lax.ppermute(block, axis, route)  17.7 us
    ppermute x10, waiting for transfers between devices, passed_along(): return lax.ppermute(block, axis, route)  11.9 us
    pallas_call x6, Pallas kernels, call(): pl.pallas_call(kernel, out_shape=out, in_specs=in_specs, out_specs=[VMEM]...  9.76 us
    all_to_all x1, starting transfers between devices, per_device(): lax.all_to_all(spectrum_y, 'gx', split_axis=0, concat_axis=0, tiled=True)  3.5 us
    dynamic_slice x1, local copies, waits for them, and re-layouts, per_device(): lax.dynamic_slice_in_dim(monitor_spectra, target * group_waves, group_wav...  1.19 us
  transfers between devices with their start and end apart: 11, of which 4 were waited for; matrix products, arithmetic and copies ran while one was open for 0% of the time, Pallas kernels for 13%

profile of v1, /device:TPU:0, one launch (start us, length us, event | category | flops | bytes accessed | tf_op | source)
XLA Modules:
  0.0 45.5 jit_solution(2366505596751217681)
XLA Ops:
  0.7 0.0 copy-start
  0.7 0.0 copy-start.1
  0.7 0.0 copy-start.4
  0.7 1.2 %constant_dynamic-slice_fusion = (f32[4,2,4,8,128]{4,3,2,1,0:T(8,128)S(1)}, f32[4,2,4,8,128]{4,3,2,1,0:T(8,128)S(1)}, f32[4,2,4,8,128]{4,3,2,1,0:T(8,128)S(1)}, f32[4,2,4,8,128]{4,3,2,1,0:T(8,128)S(1)}) fusion(f32[16,2,4,8,128]{4,3,2,1,0:T(8,128)} %monitor_ref.1, s32[]{:T(128)S(6)} %select_n.33, s32[]{:T(128)S(6)} %select_n.29, s32[]{:T(128)S(6)} %select_n.27, ...), kind=kLoop, calls=%fused_computation | loop fusion | bytes 1048592 | tf_op jit(solution)/shard_map/dynamic_slice | solution.py:462
  1.9 0.0 copy-start.8
  1.9 0.0 copy-start.5
  2.0 3.1 %collective-permute-start.9 = (f32[4,2,4,8,128]{4,3,2,1,0:T(8,128)S(1)}, f32[4,2,4,8,128]{4,3,2,1,0:T(8,128)S(1)}, u32[]{:S(2)}, u32[]{:S(2)}) collective-permute-start(f32[4,2,4,8,128]{4,3,2,1,0:T(8,128)S(1)} %get-tuple-element.17), channel_id=1, source_target_pairs={{3,0},{0,1},{1,2},{2,3},{7,4},{4,5},{5,6},{6,7},{11,8},{8,9},{9,10... | collective-permute-start | bytes 393224 | tf_op jit(solution)/shard_map/ppermute | solution.py:34
  5.0 0.0 copy-done
  5.0 0.0 copy-done.1
  5.0 0.0 copy-done.4
  5.0 0.0 copy-done.8
  5.0 0.6 %pack_faces.1 = (f32[7,4,8,128]{3,2,1,0:T(8,128)S(1)}, f32[7,4,8,128]{3,2,1,0:T(8,128)S(1)}) custom-call(f32[4]{0:T(128)S(1)} %copy-done.8, f32[3,16,8,128]{3,2,1,0:T(8,128)S(1)} %copy-done, f32[3,16,8,128]{3,2,1,0:T(8,128)S(1)} %copy-done.1, s32[16,8,128]{2,1,0:T(8,128)S(1)} %copy-done.4), custom_call_target="tpu_custom_call" | custom-call | flops 100000 | bytes 1000000 | tf_op jit(solution)/shard_map/pack_faces/pallas_call | solution.py:422
  5.7 0.1 collective-permute-start
  5.7 2.6 %collective-permute-start.1 = (f32[7,4,8,128]{3,2,1,0:T(8,128)S(1)}, f32[7,4,8,128]{3,2,1,0:T(8,128)S(1)}, u32[]{:S(2)}, u32[]{:S(2)}) collective-permute-start(f32[7,4,8,128]{3,2,1,0:T(8,128)S(1)} %get-tuple-element.12), channel_id=1, source_target_pairs={{4,0},{8,4},{12,8},{16,12},{20,16},{24,20},{28,24},{0,28},{5,1},{9... | collective-permute-start | bytes 344072 | tf_op jit(solution)/shard_map/ppermute | solution.py:34
  8.4 2.6 %collective-permute-start.7 = (f32[4,2,4,8,128]{4,3,2,1,0:T(8,128)S(1)}, f32[4,2,4,8,128]{4,3,2,1,0:T(8,128)S(1)}, u32[]{:S(2)}, u32[]{:S(2)}) collective-permute-start(f32[4,2,4,8,128]{4,3,2,1,0:T(8,128)S(1)} %get-tuple-element.18), channel_id=1, source_target_pairs={{1,0},{2,1},{3,2},{0,3},{5,4},{6,5},{7,6},{4,7},{9,8},{10,9},{11,1... | collective-permute-start | bytes 393224 | tf_op jit(solution)/shard_map/ppermute | solution.py:34
  11.0 0.4 collective-permute-start.8
  11.4 0.0 collective-permute-done.before_ref
  11.4 0.0 collective-permute-done.1.after_ref
  11.4 0.8 %monitor_message.1.refs_0_ = f32[96,128]{1,0:T(8,128)S(1)} custom-call(f32[4]{0:T(128)S(1)} %copy-done.8, f32[3,16,8,128]{3,2,1,0:T(8,128)S(1)} %copy-done, f32[3,16,8,128]{3,2,1,0:T(8,128)S(1)} %copy-done.1, s32[16,8,128]{2,1,0:T(8,128)S(1)} %copy-done.4, f32[7,4,8,128]{3,2,1,0:T(8,128)S(1)} %collective-permute-done.before_ref, ...), custom_call_target="tpu_custom_call" | custom-call | flops 100000 | bytes 100000 | tf_op jit(solution)/shard_map/monitor_message/pallas_call | solution.py:422
  12.2 0.0 copy-start.7
  12.2 1.6 %collective-permute-start.6 = (f32[96,128]{1,0:T(8,128)S(1)}, f32[96,128]{1,0:T(8,128)S(1)}, u32[]{:S(2)}, u32[]{:S(2)}) collective-permute-start(f32[96,128]{1,0:T(8,128)S(1)} %monitor_message.1.refs_0_), channel_id=1, source_target_pairs={{3,0},{0,1},{1,2},{2,3},{7,4},{4,5},{5,6},{6,7},{11,8},{8,9},{9,10... | collective-permute-start | bytes 147464 | tf_op jit(solution)/shard_map/ppermute | solution.py:34
  13.8 1.0 %collective-permute-start.5 = (f32[96,128]{1,0:T(8,128)S(1)}, f32[96,128]{1,0:T(8,128)S(1)}, u32[]{:S(2)}, u32[]{:S(2)}) collective-permute-start(f32[96,128]{1,0:T(8,128)S(1)} %monitor_message.1.refs_0_), channel_id=1, source_target_pairs={{2,0},{3,1},{0,2},{1,3},{6,4},{7,5},{4,6},{5,7},{10,8},{11,9},{8,1... | collective-permute-start | bytes 147464 | tf_op jit(solution)/shard_map/ppermute | solution.py:34
  14.9 0.0 collective-permute-done.9.refs_7_
  14.9 2.8 %collective-permute-start.4 = (f32[96,128]{1,0:T(8,128)S(1)}, f32[96,128]{1,0:T(8,128)S(1)}, u32[]{:S(2)}, u32[]{:S(2)}) collective-permute-start(f32[96,128]{1,0:T(8,128)S(1)} %monitor_message.1.refs_0_), channel_id=1, source_target_pairs={{1,0},{2,1},{3,2},{0,3},{5,4},{6,5},{7,6},{4,7},{9,8},{10,9},{11,1... | collective-permute-start | bytes 147464 | tf_op jit(solution)/shard_map/ppermute | solution.py:34
  17.7 0.0 collective-permute-done.7.refs_5_
  17.7 5.4 %collective-permute-done.8.refs_6_ = f32[4,2,4,8,128]{4,3,2,1,0:T(8,128)S(1)} collective-permute-done((f32[4,2,4,8,128]{4,3,2,1,0:T(8,128)S(1)}, f32[4,2,4,8,128]{4,3,2,1,0:T(8,128)S(1)}, u32[]{:S(2)}, u32[]{:S(2)}) %collective-permute-start.8) | collective-permute-done | bytes 131104 | tf_op jit(solution)/shard_map/ppermute | solution.py:34
  23.1 0.0 collective-permute-done.6.refs_3_
  23.1 0.5 %collective-permute-done.5.refs_2_ = f32[96,128]{1,0:T(8,128)S(1)} collective-permute-done((f32[96,128]{1,0:T(8,128)S(1)}, f32[96,128]{1,0:T(8,128)S(1)}, u32[]{:S(2)}, u32[]{:S(2)}) %collective-permute-start.5) | collective-permute-done | bytes 49184 | tf_op jit(solution)/shard_map/ppermute | solution.py:34
  23.6 0.0 collective-permute-done.4.refs_1_
  23.6 0.0 copy-start.9
  23.6 0.0 copy-done.5
  23.6 0.0 copy-done.7
  23.7 0.6 %copy-done.9 = s32[16]{0:T(128)S(1)} copy-done((s32[16]{0:T(128)S(1)}, s32[16]{0:T(128)}, u32[]{:S(2)}) %copy-start.9) | copy-done | bytes 88
  24.3 0.0 copy-start.3
  24.3 2.9 %y_orders.1 = f32[8,32,128]{2,1,0:T(8,128)} custom-call(s32[1]{0:T(128)} %bitcast.me_ref, s32[16]{0:T(128)S(1)} %copy-done.9, f32[512]{0:T(512)S(1)} %copy-done.7, f32[512,256]{1,0:T(8,128)S(1)} %copy-done.5, f32[96,128]{1,0:T(8,128)S(1)} %monitor_message.1.refs_0_, f32[96,128]{1,0:T(8,128)S(1)} %collective-permute-done.4.refs_1_, ...), custom_call_target="tpu_custom_call" | custom-call | flops 100000000 | bytes 2000000 | tf_op jit(solution)/shard_map/y_orders/pallas_call | solution.py:422
  27.2 3.5 %all-to-all-start = ((f32[8,32,128]{2,1,0:T(8,128)}), f32[8,32,128]{2,1,0:T(8,128)S(1)}, u32[]{:S(2)}, u32[]{:S(2)}) async-start(f32[8,32,128]{2,1,0:T(8,128)} %y_orders.1), calls=%async_computation | async-start | bytes 262144 | tf_op jit(solution)/shard_map/all_to_all | solution.py:529
  30.7 0.8 %all_edges.1.edges_ref = f32[7,16,128]{2,1,0:T(8,128)S(1)} custom-call(f32[4]{0:T(128)S(1)} %copy-done.8, f32[3,16,8,128]{3,2,1,0:T(8,128)S(1)} %copy-done, f32[3,16,8,128]{3,2,1,0:T(8,128)S(1)} %copy-done.1, s32[16,8,128]{2,1,0:T(8,128)S(1)} %copy-done.4, f32[7,4,8,128]{3,2,1,0:T(8,128)S(1)} %collective-permute-done.before_ref, ...), custom_call_target="tpu_custom_call" | custom-call | flops 100000 | bytes 1000000 | tf_op jit(solution)/shard_map/all_edges/pallas_call | solution.py:422
  31.6 0.0 copy-start.6
  31.6 3.4 %collective-permute-start.3 = (f32[7,16,128]{2,1,0:T(8,128)S(1)}, f32[7,16,128]{2,1,0:T(8,128)S(1)}, u32[]{:S(2)}, u32[]{:S(2)}) collective-permute-start(f32[7,16,128]{2,1,0:T(8,128)S(1)} %all_edges.1.edges_ref), channel_id=1, source_target_pairs={{1,0},{2,1},{3,2},{0,3},{5,4},{6,5},{7,6},{4,7},{9,8},{10,9},{11,1... | collective-permute-start | bytes 172040 | tf_op jit(solution)/shard_map/ppermute | solution.py:34
  34.9 0.0 collective-permute-start.2
  34.9 2.2 %collective-permute-done.3.edges_after_ref = f32[7,16,128]{2,1,0:T(8,128)S(1)} collective-permute-done((f32[7,16,128]{2,1,0:T(8,128)S(1)}, f32[7,16,128]{2,1,0:T(8,128)S(1)}, u32[]{:S(2)}, u32[]{:S(2)}) %collective-permute-start.3) | collective-permute-done | bytes 57376 | tf_op jit(solution)/shard_map/ppermute | solution.py:34
  37.2 3.7 %collective-permute-done.2.edges_before_ref = f32[7,16,128]{2,1,0:T(8,128)S(1)} collective-permute-done((f32[7,16,128]{2,1,0:T(8,128)S(1)}, f32[7,16,128]{2,1,0:T(8,128)S(1)}, u32[]{:S(2)}, u32[]{:S(2)}) %collective-permute-start.2) | collective-permute-done | bytes 57376 | tf_op jit(solution)/shard_map/ppermute | solution.py:34
  40.9 0.0 copy-done.3
  40.9 0.0 copy-done.2
  40.9 3.5 %local_updates.1 = (f32[3,16,8,128]{3,2,1,0:T(8,128)}, f32[3,16,8,128]{3,2,1,0:T(8,128)}, f32[2,128,8,128]{3,2,1,0:T(8,128)}, f32[16,2,4,8,128]{4,3,2,1,0:T(8,128)}) custom-call(f32[4]{0:T(128)S(1)} %copy-done.8, s32[16]{0:T(128)S(1)} %copy-done.9, f32[512]{0:T(512)S(1)} %copy-done.7, f32[3,16,8,128]{3,2,1,0:T(8,128)S(1)} %copy-done, ...), custom_call_target="tpu_custom_call" | custom-call | flops 10000000 | bytes 6000000 | tf_op jit(solution)/shard_map/local_updates/pallas_call | solution.py:422
  44.4 0.0 all-to-all-done.values_ref
  44.4 0.0 copy-done.6
  44.4 1.1 %x_orders.1 = f32[4,2,4,16,64]{4,3,2,1,0:T(8,128)} custom-call(f32[8,32,128]{2,1,0:T(8,128)S(1)} %all-to-all-done.values_ref, f32[128,128]{1,0:T(8,128)S(1)} %copy-done.6), custom_call_target="tpu_custom_call" | custom-call | flops 10000000 | bytes 500000 | tf_op jit(solution)/shard_map/x_orders/pallas_call | solution.py:422
  (1 shorter events, 0.0 us)
Async XLA Ops:
  0.7 4.3 %copy-start = (f32[3,16,8,128]{3,2,1,0:T(8,128)S(1)}, f32[3,16,8,128]{3,2,1,0:T(8,128)}, u32[]{:S(2)}) copy-start(f32[3,16,8,128]{3,2,1,0:T(8,128)} %e_ref.7) | copy-start | bytes 589828
  0.7 4.3 %copy-start.1 = (f32[3,16,8,128]{3,2,1,0:T(8,128)S(1)}, f32[3,16,8,128]{3,2,1,0:T(8,128)}, u32[]{:S(2)}) copy-start(f32[3,16,8,128]{3,2,1,0:T(8,128)} %h_ref.7) | copy-start | bytes 589828
  0.7 4.3 %copy-start.4 = (s32[16,8,128]{2,1,0:T(8,128)S(1)}, s32[16,8,128]{2,1,0:T(8,128)}, u32[]{:S(2)}) copy-start(s32[16,8,128]{2,1,0:T(8,128)} %m_ref.7) | copy-start | bytes 196612
  1.9 3.1 %copy-start.8 = (f32[4]{0:T(128)S(1)}, f32[4]{0:T(128)}, u32[]{:S(2)}) copy-start(f32[4]{0:T(128)} %perm_ref.7) | copy-start | bytes 52
  1.9 21.7 %copy-start.5 = (f32[512,256]{1,0:T(8,128)S(1)}, f32[512,256]{1,0:T(8,128)}, u32[]{:S(2)}) copy-start(f32[512,256]{1,0:T(8,128)} %constant.44.clone.table_ref) | copy-start | bytes 1572868
  2.0 12.9 %collective-permute-start.9 = (f32[4,2,4,8,128]{4,3,2,1,0:T(8,128)S(1)}, f32[4,2,4,8,128]{4,3,2,1,0:T(8,128)S(1)}, u32[]{:S(2)}, u32[]{:S(2)}) collective-permute-start(f32[4,2,4,8,128]{4,3,2,1,0:T(8,128)S(1)} %get-tuple-element.17), channel_id=1, source_target_pairs={{3,0},{0,1},{1,2},{2,3},{7,4},{4,5},{5,6},{6,7},{11,8},{8,9},{9,10... | collective-permute-start | bytes 393224 | tf_op jit(solution)/shard_map/ppermute | solution.py:34
  5.7 5.7 %collective-permute-start = (f32[7,4,8,128]{3,2,1,0:T(8,128)S(1)}, f32[7,4,8,128]{3,2,1,0:T(8,128)S(1)}, u32[]{:S(2)}, u32[]{:S(2)}) collective-permute-start(f32[7,4,8,128]{3,2,1,0:T(8,128)S(1)} %get-tuple-element.11), channel_id=1, source_target_pairs={{28,0},{0,4},{4,8},{8,12},{12,16},{16,20},{20,24},{24,28},{29,1},{... | collective-permute-start | bytes 344072 | tf_op jit(solution)/shard_map/ppermute | solution.py:34
  5.7 5.7 %collective-permute-start.1 = (f32[7,4,8,128]{3,2,1,0:T(8,128)S(1)}, f32[7,4,8,128]{3,2,1,0:T(8,128)S(1)}, u32[]{:S(2)}, u32[]{:S(2)}) collective-permute-start(f32[7,4,8,128]{3,2,1,0:T(8,128)S(1)} %get-tuple-element.12), channel_id=1, source_target_pairs={{4,0},{8,4},{12,8},{16,12},{20,16},{24,20},{28,24},{0,28},{5,1},{9... | collective-permute-start | bytes 344072 | tf_op jit(solution)/shard_map/ppermute | solution.py:34
  8.4 9.4 %collective-permute-start.7 = (f32[4,2,4,8,128]{4,3,2,1,0:T(8,128)S(1)}, f32[4,2,4,8,128]{4,3,2,1,0:T(8,128)S(1)}, u32[]{:S(2)}, u32[]{:S(2)}) collective-permute-start(f32[4,2,4,8,128]{4,3,2,1,0:T(8,128)S(1)} %get-tuple-element.18), channel_id=1, source_target_pairs={{1,0},{2,1},{3,2},{0,3},{5,4},{6,5},{7,6},{4,7},{9,8},{10,9},{11,1... | collective-permute-start | bytes 393224 | tf_op jit(solution)/shard_map/ppermute | solution.py:34
  11.0 12.1 %collective-permute-start.8 = (f32[4,2,4,8,128]{4,3,2,1,0:T(8,128)S(1)}, f32[4,2,4,8,128]{4,3,2,1,0:T(8,128)S(1)}, u32[]{:S(2)}, u32[]{:S(2)}) collective-permute-start(f32[4,2,4,8,128]{4,3,2,1,0:T(8,128)S(1)} %get-tuple-element.20), channel_id=1, source_target_pairs={{2,0},{3,1},{0,2},{1,3},{6,4},{7,5},{4,6},{5,7},{10,8},{11,9},{8,1... | collective-permute-start | bytes 393224 | tf_op jit(solution)/shard_map/ppermute | solution.py:34
  12.2 11.4 %copy-start.7 = (f32[512]{0:T(512)S(1)}, f32[512]{0:T(512)}, u32[]{:S(2)}) copy-start(f32[512]{0:T(512)} %constant.43.clone.coef_ref) | copy-start | bytes 6148
  12.2 10.9 %collective-permute-start.6 = (f32[96,128]{1,0:T(8,128)S(1)}, f32[96,128]{1,0:T(8,128)S(1)}, u32[]{:S(2)}, u32[]{:S(2)}) collective-permute-start(f32[96,128]{1,0:T(8,128)S(1)} %monitor_message.1.refs_0_), channel_id=1, source_target_pairs={{3,0},{0,1},{1,2},{2,3},{7,4},{4,5},{5,6},{6,7},{11,8},{8,9},{9,10... | collective-permute-start | bytes 147464 | tf_op jit(solution)/shard_map/ppermute | solution.py:34
  13.8 9.8 %collective-permute-start.5 = (f32[96,128]{1,0:T(8,128)S(1)}, f32[96,128]{1,0:T(8,128)S(1)}, u32[]{:S(2)}, u32[]{:S(2)}) collective-permute-start(f32[96,128]{1,0:T(8,128)S(1)} %monitor_message.1.refs_0_), channel_id=1, source_target_pairs={{2,0},{3,1},{0,2},{1,3},{6,4},{7,5},{4,6},{5,7},{10,8},{11,9},{8,1... | collective-permute-start | bytes 147464 | tf_op jit(solution)/shard_map/ppermute | solution.py:34
  14.9 8.8 %collective-permute-start.4 = (f32[96,128]{1,0:T(8,128)S(1)}, f32[96,128]{1,0:T(8,128)S(1)}, u32[]{:S(2)}, u32[]{:S(2)}) collective-permute-start(f32[96,128]{1,0:T(8,128)S(1)} %monitor_message.1.refs_0_), channel_id=1, source_target_pairs={{1,0},{2,1},{3,2},{0,3},{5,4},{6,5},{7,6},{4,7},{9,8},{10,9},{11,1... | collective-permute-start | bytes 147464 | tf_op jit(solution)/shard_map/ppermute | solution.py:34
  23.6 0.7 %copy-start.9 = (s32[16]{0:T(128)S(1)}, s32[16]{0:T(128)}, u32[]{:S(2)}) copy-start(s32[16]{0:T(128)} %wave_ref.3) | copy-start | bytes 196
  24.3 16.6 %copy-start.3 = (f32[2,128,8,128]{3,2,1,0:T(8,128)S(1)}, f32[2,128,8,128]{3,2,1,0:T(8,128)}, u32[]{:S(2)}) copy-start(f32[2,128,8,128]{3,2,1,0:T(8,128)} %slab_ref.1) | copy-start | bytes 3145732
  27.2 13.7 %copy-start.2 = (f32[16,2,4,8,128]{4,3,2,1,0:T(8,128)S(1)}, f32[16,2,4,8,128]{4,3,2,1,0:T(8,128)}, u32[]{:S(2)}) copy-start(f32[16,2,4,8,128]{4,3,2,1,0:T(8,128)} %monitor_ref.1) | copy-start | bytes 1572868
  27.2 17.2 %all-to-all-start = ((f32[8,32,128]{2,1,0:T(8,128)}), f32[8,32,128]{2,1,0:T(8,128)S(1)}, u32[]{:S(2)}, u32[]{:S(2)}) async-start(f32[8,32,128]{2,1,0:T(8,128)} %y_orders.1), calls=%async_computation | async-start | bytes 262144 | tf_op jit(solution)/shard_map/all_to_all | solution.py:529
  31.6 12.9 %copy-start.6 = (f32[128,128]{1,0:T(8,128)S(1)}, f32[128,128]{1,0:T(8,128)}, u32[]{:S(2)}) copy-start(f32[128,128]{1,0:T(8,128)} %constant.45.clone.table_ref) | copy-start | bytes 196612
  31.6 5.6 %collective-permute-start.3 = (f32[7,16,128]{2,1,0:T(8,128)S(1)}, f32[7,16,128]{2,1,0:T(8,128)S(1)}, u32[]{:S(2)}, u32[]{:S(2)}) collective-permute-start(f32[7,16,128]{2,1,0:T(8,128)S(1)} %all_edges.1.edges_ref), channel_id=1, source_target_pairs={{1,0},{2,1},{3,2},{0,3},{5,4},{6,5},{7,6},{4,7},{9,8},{10,9},{11,1... | collective-permute-start | bytes 172040 | tf_op jit(solution)/shard_map/ppermute | solution.py:34
  34.9 6.0 %collective-permute-start.2 = (f32[7,16,128]{2,1,0:T(8,128)S(1)}, f32[7,16,128]{2,1,0:T(8,128)S(1)}, u32[]{:S(2)}, u32[]{:S(2)}) collective-permute-start(f32[7,16,128]{2,1,0:T(8,128)S(1)} %all_edges.1.edges_ref), channel_id=1, source_target_pairs={{3,0},{0,1},{1,2},{2,3},{7,4},{4,5},{5,6},{6,7},{11,8},{8,9},{9,10... | collective-permute-start | bytes 172040 | tf_op jit(solution)/shard_map/ppermute | solution.py:34

commit v2 on v1

--- a/solution.py
+++ b/solution.py
@@ -24,6 +24,7 @@
 RECORDS = 4
 
 VMEM = pl.BlockSpec(memory_space=pltpu.VMEM)
+HBM = pl.BlockSpec(memory_space=pltpu.HBM)
 SMEM = pl.BlockSpec(memory_space=pltpu.SMEM)
 PARAMS = pltpu.CompilerParams(vmem_limit_bytes=48 * 1024 * 1024)
 
@@ -171,34 +172,35 @@
     return tile
 
 
-def monitor_message(perm_ref, e_ref, h_ref, m_ref, before_ref, after_ref, message_ref):
+def monitor_message(perm_ref, e_ref, h_ref, m_ref, before_ref, after_ref, near_ref, far_ref):
     layers, rows, columns = m_ref.shape
     rates = rates_of(perm_ref, perm_ref.shape[0], (rows, columns))
     wide = widened_planes(own_planes(e_ref, h_ref, m_ref, rates), before_ref, after_ref)
-    walk = Leapfrog(wide, layers=layers)
-    span = layers * SEAM
+    low = layers - DEEP
+    walk = Leapfrog(lambda z: wide(low + z), layers=DEEP)
+    height = 2 * rows
+    base = KINDS * height
+    far_base = far_tiles(columns) * height
+    for s in range(STEPS):
+        for c, record in enumerate(walk.records(s + 1, DEEP - 1)):
+            place = (s * RECORDS + c) * rows
+            near_ref[pl.ds(base + place, rows), :] = record[:rows]
+            far_ref[pl.ds(far_base + place, rows), :] = record[:rows]
+    planes = [wide(z) for z in range(low)] + [walk.first(z) for z in range(DEEP)]
+    span = DEEP * SEAM
     per_tile = columns // span
-    lane = iota((2 * rows, columns), 1)
-    for tile in range(-(-KINDS // per_tile)):
-        total = None
-        for place in range(min(per_tile, KINDS - tile * per_tile)):
-            kind = tile * per_tile + place
-            edges = packed_edges([walk.first(z)[kind] for z in range(layers)], layers, place * span)
-            total = edges if total is None else jnp.where(lane >= place * span, edges, total)
-        message_ref[pl.ds(tile * 2 * rows, 2 * rows), :] = total
-    base = -(-KINDS // per_tile) * 2 * rows
-    for s in range(STEPS):
-        for c, record in enumerate(walk.records(s + 1, layers - 1)):
-            message_ref[pl.ds(base + (s * RECORDS + c) * rows, rows), :] = record[:rows]
-
-
-def all_edges(perm_ref, e_ref, h_ref, m_ref, before_ref, after_ref, edges_ref):
-    layers, rows, columns = m_ref.shape
-    rates = rates_of(perm_ref, perm_ref.shape[0], (rows, columns))
-    wide = widened_planes(own_planes(e_ref, h_ref, m_ref, rates), before_ref, after_ref)
-    planes = [wide(z) for z in range(layers)]
+    total = None
     for kind in range(KINDS):
-        edges_ref[kind] = packed_edges([planes[z][kind] for z in range(layers)], layers, 0)
+        edges = packed_edges([planes[z][kind] for z in range(layers)], layers, 0)
+        near_ref[pl.ds(kind * height, height), :] = edges
+        spot = kind % per_tile * span
+        here = rolled(edges, spot - low * SEAM, 1)
+        total = jnp.where(iota(here.shape, 1) >= spot, here, total) if spot else here
+        far_ref[pl.ds(kind // per_tile * height, height), :] = total
+
+
+def far_tiles(columns):
+    return -(-KINDS // (columns // (DEEP * SEAM)))
 
 
 def waves_of(coef_ref, wave):
@@ -206,84 +208,150 @@
     return lambda s, half, part: coef_ref[base + (s * 2 + half) * 2 + part]
 
 
-def y_orders(group_waves, blocks, me_ref, wave_ref, coef_ref, table_ref, *refs):
-    messages = refs[:blocks]
-    spectra = refs[blocks : 2 * blocks]
-    out_ref = refs[2 * blocks]
-    _, _, _, rows, columns = spectra[0].shape
-    me = me_ref[0]
-    layers = DEEP
-    span = layers * SEAM
+def exact_dot(left, right, contracted):
+    return lax.dot_general(
+        left,
+        right,
+        (contracted, ((), ())),
+        precision=lax.Precision.HIGHEST,
+        preferred_element_type=jnp.float32,
+    )
+
+
+def packed_orders(values, planes, kept, target):
+    rows = values.shape[0] // planes
+    lane = iota((rows, OY), 1)
+    per_tile = OY // kept
+    tiles = []
+    for first in range(0, planes, per_tile):
+        tile = None
+        for plane in range(first, min(planes, first + per_tile)):
+            spot = (plane - first) * kept
+            here = rolled(values[plane * rows : (plane + 1) * rows], spot - target * kept, 1)
+            tile = here if tile is None else jnp.where(lane >= spot, here, tile)
+        tiles.append(tile)
+    return tiles
+
+
+def y_monitor(group_waves, table_ref, spectra_ref, out_ref):
+    waves, _, records, rows, columns = spectra_ref.shape
+    total = None
+    for block in range(waves // group_waves):
+        table = table_ref[pl.ds(block * columns, columns), :]
+        parts = []
+        for part in range(2):
+            for w in range(group_waves):
+                parts += [spectra_ref[block * group_waves + w, part, c] for c in range(records)]
+        product = exact_dot(jnp.concatenate(parts, axis=0), table, ((1,), (0,)))
+        total = product if total is None else total + product
+    waves = group_waves
+    half = waves * records * rows
+    real = total[:half, :OY] + total[half:, OY:]
+    imag = total[half:, :OY] - total[:half, OY:]
+    targets = out_ref.shape[0]
+    for target in range(targets):
+        for part, values in enumerate((real, imag)):
+            tiles = packed_orders(values, waves * records, OY // targets, target)
+            for i, tile in enumerate(tiles):
+                out_ref[target, pl.ds((i * 2 + part) * rows, rows), :] = tile
+
+
+def y_records(waves, wave_ref, coef_ref, table_ref, monitor_ref, *refs):
+    *messages, out_ref = refs
+    blocks = len(messages)
+    columns = messages[0].shape[1]
+    targets, height, _ = out_ref.shape
+    kept = OY // targets
+    out_tiles = -(-waves * RECORDS * kept // OY)
+    rows = height // (2 * out_tiles)
+    me = lax.axis_index("gy")
+    span = DEEP * SEAM
     per_tile = columns // span
     lane = iota((2 * rows, columns), 1)
     column = lane % SEAM
+
+    near_height = (KINDS * 2 + STEPS * RECORDS) * rows
+
+    def edges_of(block, kind, spot):
+        if messages[block].shape[0] == near_height:
+            return rolled(messages[block][pl.ds(kind * 2 * rows, 2 * rows), :], spot + span, 1)
+        source = pl.ds(kind // per_tile * 2 * rows, 2 * rows)
+        return rolled(messages[block][source, :], spot - kind % per_tile * span, 1)
+
     walks = []
     for tile in range(-(-blocks // per_tile)):
         seams = range(tile * per_tile, min(blocks, (tile + 1) * per_tile))
         kinds = []
         for kind in range(KINDS):
-            source = pl.ds(kind // per_tile * 2 * rows, 2 * rows)
             total = None
             for seam in seams:
                 spot = (seam % per_tile) * span
-                shift = spot - kind % per_tile * span
-                left = rolled(messages[seam][source, :], shift, 1)
-                right = rolled(messages[(seam + 1) % blocks][source, :], shift, 1)
+                left = edges_of(seam, kind, spot)
+                right = edges_of((seam + 1) % blocks, kind, spot)
                 here = jnp.where(column < EDGE, left, right)
                 total = here if total is None else jnp.where(lane >= spot, here, total)
             kinds.append(total)
-        walks.append(seam_leapfrog(kinds, layers))
-    base = -(-KINDS // per_tile) * 2 * rows
+        walks.append(seam_leapfrog(kinds, DEEP))
     narrow = iota((rows, columns), 1)
-    coefs = [waves_of(coef_ref, wave_ref[me * group_waves + w]) for w in range(group_waves)]
     total = None
     for block in range(blocks):
         record = []
+        base = messages[block].shape[0] - STEPS * RECORDS * rows
         for s in range(STEPS):
             for c in range(RECORDS):
                 value = messages[block][pl.ds(base + (s * RECORDS + c) * rows, rows), :]
                 after, before = block, (block - 1) % blocks
-                spot_after = (after % per_tile) * span + (layers - 1) * SEAM + EDGE
-                spot_before = (before % per_tile) * span + (layers - 1) * SEAM + EDGE
+                spot_after = (after % per_tile) * span + (DEEP - 1) * SEAM + EDGE
+                spot_before = (before % per_tile) * span + (DEEP - 1) * SEAM + EDGE
                 from_after = walks[after // per_tile].records(s + 1, 0)[c][:rows]
                 from_before = walks[before // per_tile].records(s + 1, 0)[c][:rows]
                 value = jnp.where(narrow >= columns - STEPS, rolled(from_after, -spot_after, 1), value)
                 value = jnp.where(narrow < STEPS, rolled(from_before, -spot_before, 1), value)
                 record.append(value)
-        parts = []
-        for part in range(2):
-            for w in range(group_waves):
-                for c in range(RECORDS):
-                    value = spectra[block][w, part, c]
-                    for s in range(STEPS):
-                        value = value + coefs[w](s, c // 2, part) * record[s * RECORDS + c]
-                    parts.append(value)
-        values = jnp.concatenate(parts, axis=0)
         owner = lax.rem(me + block, blocks)
         table = table_ref[pl.ds(pl.multiple_of(owner * columns, columns), columns), :]
-        product = jnp.dot(
-            values, table, precision=lax.Precision.HIGHEST, preferred_element_type=jnp.float32
-        )
+        product = exact_dot(jnp.concatenate(record, axis=0), table, ((1,), (0,)))
         total = product if total is None else total + product
-    half = group_waves * RECORDS * rows
-    real = total[:half, :OY] + total[half:, OY:]
-    imag = total[half:, :OY] - total[:half, OY:]
-    sources = group_waves * RECORDS
-    targets = out_ref.shape[0]
-    kept = OY // targets
-    wide = iota((rows, OY), 1)
-    per_out = OY // kept
+    lane = iota((rows, OY), 1)
+    per_wave = RECORDS * kept
+    per_tile = OY // per_wave
+    weights = []
+    for tile in range(out_tiles):
+        some = range(tile * per_tile, min(waves, (tile + 1) * per_tile))
+        coefs = [waves_of(coef_ref, wave_ref[me * waves + w]) for w in some]
+        for s in range(STEPS):
+            for part in range(2):
+                weight = None
+                for i, coef in enumerate(coefs):
+                    for half in range(2):
+                        value = jnp.full((rows, OY), coef(s, half, part), jnp.float32)
+                        spot = i * per_wave + half * (per_wave // 2)
+                        weight = value if weight is None else jnp.where(lane >= spot, value, weight)
+                weights.append(weight)
     for target in range(targets):
-        for part, values in enumerate((real, imag)):
-            for first in range(0, sources, per_out):
-                tile = None
-                for source in range(first, min(sources, first + per_out)):
-                    spot = (source - first) * kept
-                    here = values[source * rows : (source + 1) * rows]
-                    here = rolled(here, spot - target * kept, 1)
-                    tile = here if tile is None else jnp.where(wide >= spot, here, tile)
-                place = (first // per_out * 2 + part) * rows
-                out_ref[target, pl.ds(place, rows), :] = tile
+        sides = []
+        for part in range(2):
+            values = total[:, part * OY : (part + 1) * OY]
+            (packed,) = packed_orders(values, STEPS * RECORDS, kept, target)
+            steps = []
+            for s in range(STEPS):
+                spread = None
+                for i in range(min(per_tile, waves)):
+                    here = rolled(packed, i * per_wave - s * per_wave, 1)
+                    spread = here if i == 0 else jnp.where(lane >= i * per_wave, here, spread)
+                steps.append(spread)
+            sides.append(steps)
+        for tile in range(out_tiles):
+            for part in range(2):
+                place = pl.ds((tile * 2 + part) * rows, rows)
+                value = monitor_ref[target, place, :]
+                for s in range(STEPS):
+                    real, imag = weights[(tile * STEPS + s) * 2 : (tile * STEPS + s) * 2 + 2]
+                    if part == 0:
+                        value = value + (real * sides[0][s] + imag * sides[1][s])
+                    else:
+                        value = value + (imag * sides[0][s] - real * sides[1][s])
+                out_ref[target, place, :] = value
 
 
 def x_orders(kept, values_ref, table_ref, out_ref):
@@ -296,13 +364,7 @@
         values = jnp.concatenate(
             [values_ref[source, pl.ds(tile * rows, rows), :] for source in range(sources)], axis=0
         )
-        result = lax.dot_general(
-            values,
-            table_ref[...],
-            (((0,), (0,)), ((), ())),
-            precision=lax.Precision.HIGHEST,
-            preferred_element_type=jnp.float32,
-        )
+        result = exact_dot(values, table_ref[...], ((0,), (0,)))
         for place in range(per_tile):
             wave, record = divmod(tile * per_tile + place, records)
             if wave < waves:
@@ -320,9 +382,9 @@
     m_ref,
     before_ref,
     after_ref,
-    edges_ref,
-    edges_before_ref,
-    edges_after_ref,
+    message_ref,
+    message_before_ref,
+    message_after_ref,
     slab_ref,
     monitor_ref,
     e_out,
@@ -335,13 +397,12 @@
     wide = widened_planes(own_planes(e_ref, h_ref, m_ref, rates), before_ref, after_ref)
     walk = Leapfrog(wide, layers=layers)
     left = iota((2 * rows, layers * SEAM), 1) % SEAM < EDGE
-    mine = [edges_ref[kind] for kind in range(KINDS)]
-    after = seam_leapfrog(
-        [jnp.where(left, mine[k], edges_after_ref[k]) for k in range(KINDS)], layers
-    )
-    before = seam_leapfrog(
-        [jnp.where(left, edges_before_ref[k], mine[k]) for k in range(KINDS)], layers
-    )
+    edges = [
+        [ref[pl.ds(kind * 2 * rows, 2 * rows), :] for kind in range(KINDS)]
+        for ref in (message_before_ref, message_ref, message_after_ref)
+    ]
+    before = seam_leapfrog([jnp.where(left, edges[0][k], edges[1][k]) for k in range(KINDS)], layers)
+    after = seam_leapfrog([jnp.where(left, edges[1][k], edges[2][k]) for k in range(KINDS)], layers)
     column = iota((rows, columns), 1)
     inner = (column >= STEPS) & (column < columns - STEPS)
     joined = {}
@@ -438,9 +499,10 @@
     x_blocks, y_blocks = lax.axis_size("gx"), lax.axis_size("gy")
     waves = monitor_spectra.shape[0]
     group_waves = waves // y_blocks
-    me = lax.axis_index("gy")
     fields = (electric, magnetic, material)
     groups = layers * STEPS // rows
+
+    spectra = lax.all_to_all(monitor_spectra, "gy", split_axis=0, concat_axis=0, tiled=True)
 
     faces = (KINDS, groups, rows, columns)
     forth, back = call(
@@ -456,73 +518,50 @@
     before = passed_along(forth, "gx", 1)
     after = passed_along(back, "gx", -1)
 
-    spectra = [lax.dynamic_slice_in_dim(monitor_spectra, me * group_waves, group_waves, 0)]
-    for distance in range(1, y_blocks):
-        target = (me - distance) % y_blocks
-        block = lax.dynamic_slice_in_dim(monitor_spectra, target * group_waves, group_waves, 0)
-        spectra.append(passed_along(block, "gy", -distance))
-
-    top = (layers - DEEP) // DEEP
-    top_group = groups - 1
-    tiles = -(-KINDS // (columns // (DEEP * SEAM)))
-    height = tiles * 2 * rows + STEPS * RECORDS * rows
-    fields_spec = pl.BlockSpec((3, DEEP, rows, columns), lambda i: (0, top, 0, 0))
-    faces_spec = pl.BlockSpec((KINDS, 1, rows, columns), lambda i: (0, top_group, 0, 0))
-    (message,) = call(
+    near_height = (KINDS * 2 + STEPS * RECORDS) * rows
+    far_height = (far_tiles(columns) * 2 + STEPS * RECORDS) * rows
+    near, far = call(
         monitor_message,
-        [
-            SMEM,
-            fields_spec,
-            fields_spec,
-            pl.BlockSpec((DEEP, rows, columns), lambda i: (top, 0, 0)),
-            faces_spec,
-            faces_spec,
-        ],
-        [(height, columns)],
+        [SMEM] + [VMEM] * 5,
+        [(near_height, columns), (far_height, columns)],
         permittivity,
         *fields,
         before,
         after,
         name="monitor_message",
         flops=10**5,
-        moved=10**5,
-        grid=(1,),
-        out_specs=[pl.BlockSpec((height, columns), lambda i: (0, 0))],
-    )
-    messages = [message]
+        moved=10**6,
+    )
+    messages = [near]
     for distance in range(1, y_blocks):
+        message = near if distance in (1, y_blocks - 1) else far
         messages.append(passed_along(message, "gy", -distance))
-
-    (edges,) = call(
-        all_edges,
-        [SMEM] + [VMEM] * 5,
-        [(KINDS, 2 * rows, layers * SEAM)],
-        permittivity,
-        *fields,
-        before,
-        after,
-        name="all_edges",
-        flops=10**5,
-        moved=10**6,
-    )
-    edges_before = passed_along(edges, "gy", 1)
-    edges_after = passed_along(edges, "gy", -1)
 
     coefs = jnp.asarray(wave_coefficients(slab_spectra.shape[1] // 2))
     length_x, length_y = rows * x_blocks, columns * y_blocks
     kept = OY // x_blocks
     out_tiles = -(-group_waves * RECORDS * kept // OY)
+    sums_y = jnp.asarray(y_table(length_y))
+    (monitor_y,) = call(
+        functools.partial(y_monitor, group_waves),
+        [VMEM] * 2,
+        [(x_blocks, out_tiles * 2 * rows, OY)],
+        sums_y,
+        spectra,
+        name="y_monitor",
+        flops=10**8,
+        moved=2 * 10**6,
+    )
     (spectrum_y,) = call(
-        functools.partial(y_orders, group_waves, y_blocks),
-        [SMEM] * 3 + [VMEM] * (1 + 2 * y_blocks),
-        [(x_blocks, out_tiles * 2 * rows, OY)],
-        me.reshape(1),
+        functools.partial(y_records, group_waves),
+        [SMEM] * 2 + [VMEM] * (2 + y_blocks),
+        [monitor_y.shape],
         wave_index,
         coefs,
-        jnp.asarray(y_table(length_y)),
+        sums_y,
+        monitor_y,
         *messages,
-        *spectra,
-        name="y_orders",
+        name="y_records",
         flops=10**8,
         moved=2 * 10**6,
     )
@@ -538,9 +577,9 @@
         *fields,
         before,
         after,
-        edges,
-        edges_before,
-        edges_after,
+        messages[0],
+        messages[-1],
+        messages[1 % y_blocks],
         slab_spectra,
         monitor_spectra,
         name="local_updates",

time: 45.8 us -> 40.6 us (0.89)
  starting transfers between devices: 21.2 us -> 17.8 us
  local copies, waits for them, and re-layouts: 1.88 us -> 0.05 us
    ppermute x10 -> x5, starting transfers between devices: 17.7 us -> 7.64 us  [passed_along(): return lax.ppermute(block, axis, route)]
    all_to_all x0 -> x1, starting transfers between devices: none -> 6.46 us  [per_device(): lax.all_to_all(monitor_spectra, 'gy', split_axis=0, concat_axis=0, tiled=...]
    ppermute x10 -> x5, waiting for transfers between devices: 11.9 us -> 6.21 us  [passed_along(): return lax.ppermute(block, axis, route)]
    all_to_all x0 -> x1, waiting for transfers between devices: none -> 3.58 us  [per_device(): lax.all_to_all(monitor_spectra, 'gy', split_axis=0, concat_axis=0, tiled=...]
    all_to_all x1, waiting for transfers between devices: 0.01 us -> 2.02 us  [per_device(): lax.all_to_all(spectrum_y, 'gx', split_axis=0, concat_axis=0, tiled=True)]
    dynamic_slice x1 -> x0, local copies, waits for them, and re-layouts: 1.19 us -> none  [per_device(): lax.dynamic_slice_in_dim(monitor_spectra, target * group_waves, group_wav...]
    unnamed x20, local copies, waits for them, and re-layouts: 0.68 us -> 0.05 us
  transfers between devices with their start and end apart: 11 -> 7, of which waited for: 4 -> 4; matrix products, arithmetic and copies ran while one was open for 0% -> 0% of each run, Pallas kernels for 13% -> 16%
where the time goes in v2:
time: 40.6 us; the launch traced here: 40.3 us
  starting transfers between devices  17.8 us (44%)
  waiting for transfers between devices  11.8 us (29%)
  Pallas kernels  9.85 us (24%)
  between operations  0.76 us (2%)
    pallas_call x6, Pallas kernels, call(): pl.pallas_call(kernel, out_shape=out, in_specs=in_specs, out_specs=[VMEM]...  9.85 us
    ppermute x5, starting transfers between devices, passed_along(): return lax.ppermute(block, axis, route)  7.64 us
    all_to_all x1, starting transfers between devices, per_device(): lax.all_to_all(monitor_spectra, 'gy', split_axis=0, concat_axis=0, tiled=...  6.46 us
    ppermute x5, waiting for transfers between devices, passed_along(): return lax.ppermute(block, axis, route)  6.21 us
    all_to_all x1, starting transfers between devices, per_device(): lax.all_to_all(spectrum_y, 'gx', split_axis=0, concat_axis=0, tiled=True)  3.72 us
    all_to_all x1, waiting for transfers between devices, per_device(): lax.all_to_all(monitor_spectra, 'gy', split_axis=0, concat_axis=0, tiled=...  3.58 us
    all_to_all x1, waiting for transfers between devices, per_device(): lax.all_to_all(spectrum_y, 'gx', split_axis=0, concat_axis=0, tiled=True)  2.02 us
  transfers between devices with their start and end apart: 7, of which 4 were waited for; matrix products, arithmetic and copies ran while one was open for 0% of the time, Pallas kernels for 16%

profile of v2, /device:TPU:0, one launch (start us, length us, event | category | flops | bytes accessed | tf_op | source)
XLA Modules:
  0.0 40.3 jit_solution(12028436625194350481)
XLA Ops:
  0.6 0.0 copy-start.8
  0.6 0.0 copy-start.5
  0.7 0.0 copy-start.3
  0.7 0.0 copy-start.2
  0.7 6.5 %all-to-all-start = ((f32[16,2,4,8,128]{4,3,2,1,0:T(8,128)}), f32[16,2,4,8,128]{4,3,2,1,0:T(8,128)S(1)}, u32[]{:S(2)}, u32[]{:S(2)}) async-start(f32[16,2,4,8,128]{4,3,2,1,0:T(8,128)} %monitor_ref.1), calls=%async_computation | async-start | bytes 1048576 | tf_op jit(solution)/shard_map/all_to_all | solution.py:505
  7.1 0.0 copy-done.8
  7.1 0.0 copy-done.5
  7.1 0.0 copy-done.3
  7.1 0.0 copy-done.2
  7.2 0.0 copy-start
  7.2 0.6 %pack_faces.1 = (f32[7,4,8,128]{3,2,1,0:T(8,128)S(1)}, f32[7,4,8,128]{3,2,1,0:T(8,128)S(1)}) custom-call(f32[4]{0:T(128)S(1)} %copy-done.8, f32[3,16,8,128]{3,2,1,0:T(8,128)S(1)} %copy-done.2, f32[3,16,8,128]{3,2,1,0:T(8,128)S(1)} %copy-done.3, s32[16,8,128]{2,1,0:T(8,128)S(1)} %copy-done.5), custom_call_target="tpu_custom_call" | custom-call | flops 100000 | bytes 1000000 | tf_op jit(solution)/shard_map/pack_faces/pallas_call | solution.py:483
  7.8 0.1 collective-permute-start
  7.8 2.6 %collective-permute-start.1 = (f32[7,4,8,128]{3,2,1,0:T(8,128)S(1)}, f32[7,4,8,128]{3,2,1,0:T(8,128)S(1)}, u32[]{:S(2)}, u32[]{:S(2)}) collective-permute-start(f32[7,4,8,128]{3,2,1,0:T(8,128)S(1)} %get-tuple-element.14), channel_id=1, source_target_pairs={{4,0},{8,4},{12,8},{16,12},{20,16},{24,20},{28,24},{0,28},{5,1},{9... | collective-permute-start | bytes 344072 | tf_op jit(solution)/shard_map/ppermute | solution.py:35
  10.5 2.5 %collective-permute-done.before_ref = f32[7,4,8,128]{3,2,1,0:T(8,128)S(1)} collective-permute-done((f32[7,4,8,128]{3,2,1,0:T(8,128)S(1)}, f32[7,4,8,128]{3,2,1,0:T(8,128)S(1)}, u32[]{:S(2)}, u32[]{:S(2)}) %collective-permute-start) | collective-permute-done | bytes 114720 | tf_op jit(solution)/shard_map/ppermute | solution.py:35
  12.9 0.0 collective-permute-done.1.after_ref
  12.9 1.1 %monitor_message.1 = (f32[176,128]{1,0:T(8,128)S(1)}, f32[96,128]{1,0:T(8,128)S(1)}) custom-call(f32[4]{0:T(128)S(1)} %copy-done.8, f32[3,16,8,128]{3,2,1,0:T(8,128)S(1)} %copy-done.2, f32[3,16,8,128]{3,2,1,0:T(8,128)S(1)} %copy-done.3, s32[16,8,128]{2,1,0:T(8,128)S(1)} %copy-done.5, f32[7,4,8,128]{3,2,1,0:T(8,128)S(1)} %collective-permute-done.before_ref, ...), custom_call_target="tpu_custom_call" | custom-call | flops 100000 | bytes 1000000 | tf_op jit(solution)/shard_map/monitor_message/pallas_call | solution.py:483
  14.1 3.8 %collective-permute-start.3 = (f32[176,128]{1,0:T(8,128)S(1)}, f32[176,128]{1,0:T(8,128)S(1)}, u32[]{:S(2)}, u32[]{:S(2)}) collective-permute-start(f32[176,128]{1,0:T(8,128)S(1)} %get-tuple-element.15.message_ref.refs_0_), channel_id=1, source_target_pairs={{1,0},{2,1},{3,2},{0,3},{5,4},{6,5},{7,6},{4,7},{9,8},{10,9},{11,1... | collective-permute-start | bytes 270344 | tf_op jit(solution)/shard_map/ppermute | solution.py:35
  17.9 0.0 collective-permute-start.2
  17.9 0.0 copy-start.7
  17.9 0.0 copy-start.9
  17.9 0.0 copy-start.4
  17.9 1.1 %collective-permute-start.4 = (f32[96,128]{1,0:T(8,128)S(1)}, f32[96,128]{1,0:T(8,128)S(1)}, u32[]{:S(2)}, u32[]{:S(2)}) collective-permute-start(f32[96,128]{1,0:T(8,128)S(1)} %get-tuple-element.20), channel_id=1, source_target_pairs={{2,0},{3,1},{0,2},{1,3},{6,4},{7,5},{4,6},{5,7},{10,8},{11,9},{8,1... | collective-permute-start | bytes 147464 | tf_op jit(solution)/shard_map/ppermute | solution.py:35
  19.0 3.6 %all-to-all-done.spectra_ref = f32[16,2,4,8,128]{4,3,2,1,0:T(8,128)S(1)} async-done(((f32[16,2,4,8,128]{4,3,2,1,0:T(8,128)}), f32[16,2,4,8,128]{4,3,2,1,0:T(8,128)S(1)}, u32[]{:S(2)}, u32[]{:S(2)}) %all-to-all-start) | async-done | bytes 524320 | tf_op jit(solution)/shard_map/all_to_all | solution.py:505
  22.6 0.0 copy-done
  22.6 1.3 %y_monitor.1.monitor_ref = f32[8,32,128]{2,1,0:T(8,128)S(1)} custom-call(f32[512,256]{1,0:T(8,128)S(1)} %copy-done, f32[16,2,4,8,128]{4,3,2,1,0:T(8,128)S(1)} %all-to-all-done.spectra_ref), custom_call_target="tpu_custom_call" | custom-call | flops 100000000 | bytes 2000000 | tf_op jit(solution)/shard_map/y_monitor/pallas_call | solution.py:483
  23.9 0.0 copy-start.1
  23.9 3.7 %collective-permute-done.4.refs_2_ = f32[96,128]{1,0:T(8,128)S(1)} collective-permute-done((f32[96,128]{1,0:T(8,128)S(1)}, f32[96,128]{1,0:T(8,128)S(1)}, u32[]{:S(2)}, u32[]{:S(2)}) %collective-permute-start.4) | collective-permute-done | bytes 49184 | tf_op jit(solution)/shard_map/ppermute | solution.py:35
  27.6 0.0 collective-permute-done.3.message_after_ref.refs_1_
  27.6 0.0 collective-permute-done.2.message_before_ref.refs_3_
  27.6 0.0 copy-done.7
  27.6 0.0 copy-done.9
  27.6 2.3 %y_records.1 = f32[8,32,128]{2,1,0:T(8,128)} custom-call(s32[16]{0:T(128)S(1)} %copy-done.9, f32[512]{0:T(512)S(1)} %copy-done.7, f32[512,256]{1,0:T(8,128)S(1)} %copy-done, f32[8,32,128]{2,1,0:T(8,128)S(1)} %y_monitor.1.monitor_ref, f32[176,128]{1,0:T(8,128)S(1)} %get-tuple-element.15.message_ref.refs_0_, ...), custom_call_target="tpu_custom_call" | custom-call | flops 100000000 | bytes 2000000 | tf_op jit(solution)/shard_map/y_records/pallas_call | solution.py:483
  29.9 3.7 %all-to-all-start.1 = ((f32[8,32,128]{2,1,0:T(8,128)}), f32[8,32,128]{2,1,0:T(8,128)S(1)}, u32[]{:S(2)}, u32[]{:S(2)}) async-start(f32[8,32,128]{2,1,0:T(8,128)} %y_records.1), calls=%async_computation.1 | async-start | bytes 262144 | tf_op jit(solution)/shard_map/all_to_all | solution.py:568
  33.6 0.0 copy-done.4
  33.6 0.0 copy-done.1
  33.6 0.0 copy-start.6
  33.7 3.5 %local_updates.1 = (f32[3,16,8,128]{3,2,1,0:T(8,128)}, f32[3,16,8,128]{3,2,1,0:T(8,128)}, f32[2,128,8,128]{3,2,1,0:T(8,128)}, f32[16,2,4,8,128]{4,3,2,1,0:T(8,128)}) custom-call(f32[4]{0:T(128)S(1)} %copy-done.8, s32[16]{0:T(128)S(1)} %copy-done.9, f32[512]{0:T(512)S(1)} %copy-done.7, f32[3,16,8,128]{3,2,1,0:T(8,128)S(1)} %copy-done.2, ...), custom_call_target="tpu_custom_call" | custom-call | flops 10000000 | bytes 6000000 | tf_op jit(solution)/shard_map/local_updates/pallas_call | solution.py:483
  37.1 2.0 %all-to-all-done.1.values_ref = f32[8,32,128]{2,1,0:T(8,128)S(1)} async-done(((f32[8,32,128]{2,1,0:T(8,128)}), f32[8,32,128]{2,1,0:T(8,128)S(1)}, u32[]{:S(2)}, u32[]{:S(2)}) %all-to-all-start.1) | async-done | bytes 131104 | tf_op jit(solution)/shard_map/all_to_all | solution.py:568
  39.2 0.0 copy-done.6
  39.2 1.1 %x_orders.1 = f32[4,2,4,16,64]{4,3,2,1,0:T(8,128)} custom-call(f32[8,32,128]{2,1,0:T(8,128)S(1)} %all-to-all-done.1.values_ref, f32[128,128]{1,0:T(8,128)S(1)} %copy-done.6), custom_call_target="tpu_custom_call" | custom-call | flops 10000000 | bytes 500000 | tf_op jit(solution)/shard_map/x_orders/pallas_call | solution.py:483
Async XLA Ops:
  0.6 6.5 %copy-start.8 = (f32[4]{0:T(128)S(1)}, f32[4]{0:T(128)}, u32[]{:S(2)}) copy-start(f32[4]{0:T(128)} %perm_ref.5) | copy-start | bytes 52
  0.6 6.5 %copy-start.5 = (s32[16,8,128]{2,1,0:T(8,128)S(1)}, s32[16,8,128]{2,1,0:T(8,128)}, u32[]{:S(2)}) copy-start(s32[16,8,128]{2,1,0:T(8,128)} %m_ref.5) | copy-start | bytes 196612
  0.7 6.5 %copy-start.3 = (f32[3,16,8,128]{3,2,1,0:T(8,128)S(1)}, f32[3,16,8,128]{3,2,1,0:T(8,128)}, u32[]{:S(2)}) copy-start(f32[3,16,8,128]{3,2,1,0:T(8,128)} %h_ref.5) | copy-start | bytes 589828
  0.7 6.5 %copy-start.2 = (f32[3,16,8,128]{3,2,1,0:T(8,128)S(1)}, f32[3,16,8,128]{3,2,1,0:T(8,128)}, u32[]{:S(2)}) copy-start(f32[3,16,8,128]{3,2,1,0:T(8,128)} %e_ref.5) | copy-start | bytes 589828
  0.7 21.9 %all-to-all-start = ((f32[16,2,4,8,128]{4,3,2,1,0:T(8,128)}), f32[16,2,4,8,128]{4,3,2,1,0:T(8,128)S(1)}, u32[]{:S(2)}, u32[]{:S(2)}) async-start(f32[16,2,4,8,128]{4,3,2,1,0:T(8,128)} %monitor_ref.1), calls=%async_computation | async-start | bytes 1048576 | tf_op jit(solution)/shard_map/all_to_all | solution.py:505
  7.2 15.4 %copy-start = (f32[512,256]{1,0:T(8,128)S(1)}, f32[512,256]{1,0:T(8,128)}, u32[]{:S(2)}) copy-start(f32[512,256]{1,0:T(8,128)} %constant.7.clone.table_ref) | copy-start | bytes 1572868
  7.8 5.2 %collective-permute-start = (f32[7,4,8,128]{3,2,1,0:T(8,128)S(1)}, f32[7,4,8,128]{3,2,1,0:T(8,128)S(1)}, u32[]{:S(2)}, u32[]{:S(2)}) collective-permute-start(f32[7,4,8,128]{3,2,1,0:T(8,128)S(1)} %get-tuple-element.13), channel_id=1, source_target_pairs={{28,0},{0,4},{4,8},{8,12},{12,16},{16,20},{20,24},{24,28},{29,1},{... | collective-permute-start | bytes 344072 | tf_op jit(solution)/shard_map/ppermute | solution.py:35
  7.8 5.1 %collective-permute-start.1 = (f32[7,4,8,128]{3,2,1,0:T(8,128)S(1)}, f32[7,4,8,128]{3,2,1,0:T(8,128)S(1)}, u32[]{:S(2)}, u32[]{:S(2)}) collective-permute-start(f32[7,4,8,128]{3,2,1,0:T(8,128)S(1)} %get-tuple-element.14), channel_id=1, source_target_pairs={{4,0},{8,4},{12,8},{16,12},{20,16},{24,20},{28,24},{0,28},{5,1},{9... | collective-permute-start | bytes 344072 | tf_op jit(solution)/shard_map/ppermute | solution.py:35
  14.1 13.5 %collective-permute-start.3 = (f32[176,128]{1,0:T(8,128)S(1)}, f32[176,128]{1,0:T(8,128)S(1)}, u32[]{:S(2)}, u32[]{:S(2)}) collective-permute-start(f32[176,128]{1,0:T(8,128)S(1)} %get-tuple-element.15.message_ref.refs_0_), channel_id=1, source_target_pairs={{1,0},{2,1},{3,2},{0,3},{5,4},{6,5},{7,6},{4,7},{9,8},{10,9},{11,1... | collective-permute-start | bytes 270344 | tf_op jit(solution)/shard_map/ppermute | solution.py:35
  17.9 9.7 %collective-permute-start.2 = (f32[176,128]{1,0:T(8,128)S(1)}, f32[176,128]{1,0:T(8,128)S(1)}, u32[]{:S(2)}, u32[]{:S(2)}) collective-permute-start(f32[176,128]{1,0:T(8,128)S(1)} %get-tuple-element.15.message_ref.refs_0_), channel_id=1, source_target_pairs={{3,0},{0,1},{1,2},{2,3},{7,4},{4,5},{5,6},{6,7},{11,8},{8,9},{9,10... | collective-permute-start | bytes 270344 | tf_op jit(solution)/shard_map/ppermute | solution.py:35
  17.9 9.7 %copy-start.7 = (f32[512]{0:T(512)S(1)}, f32[512]{0:T(512)}, u32[]{:S(2)}) copy-start(f32[512]{0:T(512)} %constant.6.clone.coef_ref) | copy-start | bytes 6148
  17.9 9.7 %copy-start.9 = (s32[16]{0:T(128)S(1)}, s32[16]{0:T(128)}, u32[]{:S(2)}) copy-start(s32[16]{0:T(128)} %wave_ref.3) | copy-start | bytes 196
  17.9 15.7 %copy-start.4 = (f32[2,128,8,128]{3,2,1,0:T(8,128)S(1)}, f32[2,128,8,128]{3,2,1,0:T(8,128)}, u32[]{:S(2)}) copy-start(f32[2,128,8,128]{3,2,1,0:T(8,128)} %slab_ref.1) | copy-start | bytes 3145732
  17.9 9.7 %collective-permute-start.4 = (f32[96,128]{1,0:T(8,128)S(1)}, f32[96,128]{1,0:T(8,128)S(1)}, u32[]{:S(2)}, u32[]{:S(2)}) collective-permute-start(f32[96,128]{1,0:T(8,128)S(1)} %get-tuple-element.20), channel_id=1, source_target_pairs={{2,0},{3,1},{0,2},{1,3},{6,4},{7,5},{4,6},{5,7},{10,8},{11,9},{8,1... | collective-permute-start | bytes 147464 | tf_op jit(solution)/shard_map/ppermute | solution.py:35
  23.9 9.8 %copy-start.1 = (f32[16,2,4,8,128]{4,3,2,1,0:T(8,128)S(1)}, f32[16,2,4,8,128]{4,3,2,1,0:T(8,128)}, u32[]{:S(2)}) copy-start(f32[16,2,4,8,128]{4,3,2,1,0:T(8,128)} %monitor_ref.1) | copy-start | bytes 1572868
  29.9 9.3 %all-to-all-start.1 = ((f32[8,32,128]{2,1,0:T(8,128)}), f32[8,32,128]{2,1,0:T(8,128)S(1)}, u32[]{:S(2)}, u32[]{:S(2)}) async-start(f32[8,32,128]{2,1,0:T(8,128)} %y_records.1), calls=%async_computation.1 | async-start | bytes 262144 | tf_op jit(solution)/shard_map/all_to_all | solution.py:568
  33.6 5.5 %copy-start.6 = (f32[128,128]{1,0:T(8,128)S(1)}, f32[128,128]{1,0:T(8,128)}, u32[]{:S(2)}) copy-start(f32[128,128]{1,0:T(8,128)} %constant.8.clone.table_ref) | copy-start | bytes 196612

commit v3 on v2

--- a/solution.py
+++ b/solution.py
@@ -3,6 +3,7 @@
 
 import jax
 import jax.numpy as jnp
+import ml_dtypes
 import numpy as np
 from jax import lax
 from jax.experimental import pallas as pl
@@ -20,6 +21,7 @@
 EDGE = 2 * STEPS
 SEAM = 2 * EDGE
 DEEP = 4
+OUTER = SEAM // STEPS
 KINDS = 7
 RECORDS = 4
 
@@ -27,6 +29,10 @@
 HBM = pl.BlockSpec(memory_space=pltpu.HBM)
 SMEM = pl.BlockSpec(memory_space=pltpu.SMEM)
 PARAMS = pltpu.CompilerParams(vmem_limit_bytes=48 * 1024 * 1024)
+
+
+def in_hbm(array):
+    return pltpu.with_memory_space_constraint(array, pltpu.HBM)
 
 
 def passed_along(block, axis, distance):
@@ -141,7 +147,37 @@
     return at
 
 
-def pack_faces(perm_ref, e_ref, h_ref, m_ref, forth_ref, back_ref):
+def block_copy(distance, spectra_any, block_ref, semaphore):
+    waves = block_ref.shape[0]
+    blocks = spectra_any.shape[0] // waves
+    owner = lax.rem(lax.axis_index("gy") + blocks - distance, blocks)
+    source = spectra_any.at[pl.ds(owner * waves, waves)]
+    return pltpu.make_async_copy(source, block_ref, semaphore)
+
+
+def pack_faces(
+    distances,
+    perm_any,
+    e_any,
+    h_any,
+    m_any,
+    spectra_any,
+    forth_ref,
+    back_ref,
+    *refs,
+):
+    *block_refs, perm_ref, e_ref, h_ref, m_ref, ready, sent = refs
+    sources, targets = (e_any, h_any, m_any, perm_any), (e_ref, h_ref, m_ref, perm_ref)
+    copies = [
+        pltpu.make_async_copy(source, target, ready.at[i])
+        for i, (source, target) in enumerate(zip(sources, targets))
+    ]
+    for i, (distance, block_ref) in enumerate(zip(distances, block_refs)):
+        copies.append(block_copy(distance, spectra_any, block_ref, sent.at[i]))
+    for copy in copies:
+        copy.start()
+    for copy in copies[:4]:
+        copy.wait()
     layers, rows, columns = m_ref.shape
     rates = rates_of(perm_ref, perm_ref.shape[0], (rows, columns))
     own = own_planes(e_ref, h_ref, m_ref, rates)
@@ -159,6 +195,25 @@
                 back = jnp.where(row >= spot, rolled(here, spot, 0), back)
             forth_ref[kind, group] = forth
             back_ref[kind, group] = back
+    for copy in copies[4:]:
+        copy.wait()
+
+
+def blocks_transposed(tiles):
+    tiles = list(tiles)
+    count = len(tiles)
+    width = tiles[0].shape[1] // count
+    block = iota(tiles[0].shape, 1) // width
+    bit = 1
+    while bit < count:
+        low = (block & bit) == 0
+        for i in range(count):
+            if not i & bit:
+                first, second = tiles[i], tiles[i + bit]
+                tiles[i] = jnp.where(low, first, rolled(second, bit * width, 1))
+                tiles[i + bit] = jnp.where(low, rolled(first, -bit * width, 1), second)
+        bit *= 2
+    return tiles
 
 
 def packed_edges(planes, layers, spot):
@@ -172,34 +227,69 @@
     return tile
 
 
-def monitor_message(perm_ref, e_ref, h_ref, m_ref, before_ref, after_ref, near_ref, far_ref):
+def monitor_message(
+    distances,
+    perm_ref,
+    e_ref,
+    h_ref,
+    m_ref,
+    before_ref,
+    after_ref,
+    spectra_any,
+    forth_ref,
+    back_ref,
+    far_ref,
+    edges_ref,
+    *refs,
+):
+    *block_refs, sent = refs
+    copies = [
+        block_copy(distance, spectra_any, block_ref, sent.at[i])
+        for i, (distance, block_ref) in enumerate(zip(distances, block_refs))
+    ]
+    for copy in copies:
+        copy.start()
     layers, rows, columns = m_ref.shape
     rates = rates_of(perm_ref, perm_ref.shape[0], (rows, columns))
     wide = widened_planes(own_planes(e_ref, h_ref, m_ref, rates), before_ref, after_ref)
     low = layers - DEEP
     walk = Leapfrog(lambda z: wide(low + z), layers=DEEP)
     height = 2 * rows
-    base = KINDS * height
-    far_base = far_tiles(columns) * height
+    messages = (forth_ref, back_ref, far_ref)
     for s in range(STEPS):
         for c, record in enumerate(walk.records(s + 1, DEEP - 1)):
-            place = (s * RECORDS + c) * rows
-            near_ref[pl.ds(base + place, rows), :] = record[:rows]
-            far_ref[pl.ds(far_base + place, rows), :] = record[:rows]
+            place = pl.ds((s * RECORDS + c) * rows, rows)
+            for ref in messages:
+                ref[place, :] = record[:rows]
     planes = [wide(z) for z in range(low)] + [walk.first(z) for z in range(DEEP)]
     span = DEEP * SEAM
     per_tile = columns // span
-    total = None
+    base = STEPS * RECORDS * rows
+    outer = base + message_tiles(columns) * height
+    total = forth = back = None
     for kind in range(KINDS):
         edges = packed_edges([planes[z][kind] for z in range(layers)], layers, 0)
-        near_ref[pl.ds(kind * height, height), :] = edges
+        edges_ref[kind] = edges
+        lane = iota(edges.shape, 1)
         spot = kind % per_tile * span
         here = rolled(edges, spot - low * SEAM, 1)
-        total = jnp.where(iota(here.shape, 1) >= spot, here, total) if spot else here
-        far_ref[pl.ds(kind // per_tile * height, height), :] = total
-
-
-def far_tiles(columns):
+        total = jnp.where(lane >= spot, here, total) if spot else here
+        place = pl.ds(base + kind // per_tile * height, height)
+        for ref in messages:
+            ref[place, :] = total
+        spot = kind % OUTER * STEPS
+        here = rolled(edges, spot - STEPS, 1)
+        forth = jnp.where(lane % SEAM >= spot, here, forth) if spot else here
+        here = rolled(edges, spot - EDGE, 1)
+        back = jnp.where(lane % SEAM >= spot, here, back) if spot else here
+        place = pl.ds(outer + kind // OUTER * height, height)
+        forth_ref[place, :] = forth
+        back_ref[place, :] = back
+    for copy in copies:
+        copy.wait()
+
+
+def message_tiles(columns):
     return -(-KINDS // (columns // (DEEP * SEAM)))
 
 
@@ -218,45 +308,88 @@
     )
 
 
-def packed_orders(values, planes, kept, target):
+def split_dot(values, tables, total):
+    coarse = values.astype(jnp.bfloat16)
+    fine = (values - coarse.astype(jnp.float32)).astype(jnp.bfloat16)
+    for left, right in ((coarse, tables[0]), (fine, tables[0]), (coarse, tables[1])):
+        product = jnp.dot(left, right, preferred_element_type=jnp.float32)
+        total = product if total is None else total + product
+    return total
+
+
+def packed_orders(values, planes, kept):
     rows = values.shape[0] // planes
+    parts = [values[plane * rows : (plane + 1) * rows] for plane in range(planes)]
+    targets = per_tile = OY // kept
+    if planes % per_tile == 0 and not targets & (targets - 1):
+        groups = [parts[i : i + per_tile] for i in range(0, planes, per_tile)]
+        return list(zip(*[blocks_transposed(group) for group in groups]))
     lane = iota((rows, OY), 1)
-    per_tile = OY // kept
-    tiles = []
-    for first in range(0, planes, per_tile):
-        tile = None
-        for plane in range(first, min(planes, first + per_tile)):
-            spot = (plane - first) * kept
-            here = rolled(values[plane * rows : (plane + 1) * rows], spot - target * kept, 1)
-            tile = here if tile is None else jnp.where(lane >= spot, here, tile)
-        tiles.append(tile)
-    return tiles
-
-
-def y_monitor(group_waves, table_ref, spectra_ref, out_ref):
-    waves, _, records, rows, columns = spectra_ref.shape
+    packed = []
+    for target in range(targets):
+        tiles = []
+        for first in range(0, planes, per_tile):
+            tile = None
+            for plane in range(first, min(planes, first + per_tile)):
+                spot = (plane - first) * kept
+                here = rolled(parts[plane], spot - target * kept, 1)
+                tile = here if tile is None else jnp.where(lane >= spot, here, tile)
+            tiles.append(tile)
+        packed.append(tiles)
+    return packed
+
+
+def y_monitor(wave_ref, coef_ref, table_ref, slab_any, monitor_any, *refs):
+    *spectra, out_ref, weights_ref, slab_ref, monitor_ref, ready = refs
+    copies = [
+        pltpu.make_async_copy(slab_any, slab_ref, ready.at[0]),
+        pltpu.make_async_copy(monitor_any, monitor_ref, ready.at[1]),
+    ]
+    for copy in copies:
+        copy.start()
+    blocks = len(spectra)
+    waves, _, records, rows, columns = spectra[0].shape
+    me = lax.axis_index("gy")
     total = None
-    for block in range(waves // group_waves):
-        table = table_ref[pl.ds(block * columns, columns), :]
+    for block in range(blocks):
+        owner = lax.rem(me + block, blocks)
+        table = table_ref[pl.ds(pl.multiple_of(owner * columns, columns), columns), :]
         parts = []
         for part in range(2):
-            for w in range(group_waves):
-                parts += [spectra_ref[block * group_waves + w, part, c] for c in range(records)]
+            for w in range(waves):
+                parts += [spectra[block][w, part, c] for c in range(records)]
         product = exact_dot(jnp.concatenate(parts, axis=0), table, ((1,), (0,)))
         total = product if total is None else total + product
-    waves = group_waves
     half = waves * records * rows
     real = total[:half, :OY] + total[half:, OY:]
     imag = total[half:, :OY] - total[:half, OY:]
     targets = out_ref.shape[0]
-    for target in range(targets):
-        for part, values in enumerate((real, imag)):
-            tiles = packed_orders(values, waves * records, OY // targets, target)
-            for i, tile in enumerate(tiles):
+    for part, values in enumerate((real, imag)):
+        packed = packed_orders(values, waves * records, OY // targets)
+        for target in range(targets):
+            for i, tile in enumerate(packed[target]):
                 out_ref[target, pl.ds((i * 2 + part) * rows, rows), :] = tile
-
-
-def y_records(waves, wave_ref, coef_ref, table_ref, monitor_ref, *refs):
+    kept = OY // targets
+    lane = iota((rows, OY), 1)
+    per_wave = RECORDS * kept
+    per_tile = OY // per_wave
+    for tile in range(weights_ref.shape[0] // (2 * STEPS)):
+        some = range(tile * per_tile, min(waves, (tile + 1) * per_tile))
+        coefs = [waves_of(coef_ref, wave_ref[me * waves + w]) for w in some]
+        for s in range(STEPS):
+            for part in range(2):
+                weight = None
+                for i, coef in enumerate(coefs):
+                    for half in range(2):
+                        value = jnp.full((rows, OY), coef(s, half, part), jnp.float32)
+                        spot = i * per_wave + half * (per_wave // 2)
+                        weight = value if weight is None else jnp.where(lane >= spot, value, weight)
+                weights_ref[(tile * STEPS + s) * 2 + part] = weight
+    for copy in copies:
+        copy.wait()
+
+
+def y_records(waves, table_ref, monitor_ref, weights_ref, *refs):
     *messages, out_ref = refs
     blocks = len(messages)
     columns = messages[0].shape[1]
@@ -267,72 +400,51 @@
     me = lax.axis_index("gy")
     span = DEEP * SEAM
     per_tile = columns // span
+    base = STEPS * RECORDS * rows
     lane = iota((2 * rows, columns), 1)
     column = lane % SEAM
 
-    near_height = (KINDS * 2 + STEPS * RECORDS) * rows
-
-    def edges_of(block, kind, spot):
-        if messages[block].shape[0] == near_height:
-            return rolled(messages[block][pl.ds(kind * 2 * rows, 2 * rows), :], spot + span, 1)
-        source = pl.ds(kind // per_tile * 2 * rows, 2 * rows)
-        return rolled(messages[block][source, :], spot - kind % per_tile * span, 1)
-
-    walks = []
+    def edges_of(block, tile):
+        return messages[block][pl.ds(base + tile * 2 * rows, 2 * rows), :]
+
+    total = None
     for tile in range(-(-blocks // per_tile)):
         seams = range(tile * per_tile, min(blocks, (tile + 1) * per_tile))
         kinds = []
-        for kind in range(KINDS):
-            total = None
-            for seam in seams:
-                spot = (seam % per_tile) * span
-                left = edges_of(seam, kind, spot)
-                right = edges_of((seam + 1) % blocks, kind, spot)
-                here = jnp.where(column < EDGE, left, right)
-                total = here if total is None else jnp.where(lane >= spot, here, total)
-            kinds.append(total)
-        walks.append(seam_leapfrog(kinds, DEEP))
-    narrow = iota((rows, columns), 1)
-    total = None
+        for part in range(message_tiles(columns)):
+            mixed = []
+            for seam in list(seams) + [seams[0]] * (per_tile - len(seams)):
+                here, after = edges_of(seam, part), edges_of((seam + 1) % blocks, part)
+                mixed.append(jnp.where(column < EDGE, here, after))
+            kinds += blocks_transposed(mixed)
+        walk = seam_leapfrog(kinds[:KINDS], DEEP)
+        record = []
+        for s in range(STEPS):
+            record += [value[:rows] for value in walk.records(s + 1, 0)]
+        values = jnp.concatenate(record, axis=0)[:, : len(seams) * span]
+        owners = [lax.rem(me + seam, blocks) for seam in seams]
+        places = [pl.ds(pl.multiple_of(owner * span, span), span) for owner in owners]
+        tables = [
+            jnp.concatenate([table_ref[part, place, :] for place in places], axis=0)
+            for part in range(2)
+        ]
+        total = split_dot(values, tables, total)
     for block in range(blocks):
-        record = []
-        base = messages[block].shape[0] - STEPS * RECORDS * rows
-        for s in range(STEPS):
-            for c in range(RECORDS):
-                value = messages[block][pl.ds(base + (s * RECORDS + c) * rows, rows), :]
-                after, before = block, (block - 1) % blocks
-                spot_after = (after % per_tile) * span + (DEEP - 1) * SEAM + EDGE
-                spot_before = (before % per_tile) * span + (DEEP - 1) * SEAM + EDGE
-                from_after = walks[after // per_tile].records(s + 1, 0)[c][:rows]
-                from_before = walks[before // per_tile].records(s + 1, 0)[c][:rows]
-                value = jnp.where(narrow >= columns - STEPS, rolled(from_after, -spot_after, 1), value)
-                value = jnp.where(narrow < STEPS, rolled(from_before, -spot_before, 1), value)
-                record.append(value)
         owner = lax.rem(me + block, blocks)
-        table = table_ref[pl.ds(pl.multiple_of(owner * columns, columns), columns), :]
-        product = exact_dot(jnp.concatenate(record, axis=0), table, ((1,), (0,)))
-        total = product if total is None else total + product
+        place = pl.ds(pl.multiple_of(blocks * span + owner * columns, span), columns)
+        values = messages[block][pl.ds(0, base), :]
+        total = split_dot(values, [table_ref[part, place, :] for part in range(2)], total)
     lane = iota((rows, OY), 1)
     per_wave = RECORDS * kept
     per_tile = OY // per_wave
-    weights = []
-    for tile in range(out_tiles):
-        some = range(tile * per_tile, min(waves, (tile + 1) * per_tile))
-        coefs = [waves_of(coef_ref, wave_ref[me * waves + w]) for w in some]
-        for s in range(STEPS):
-            for part in range(2):
-                weight = None
-                for i, coef in enumerate(coefs):
-                    for half in range(2):
-                        value = jnp.full((rows, OY), coef(s, half, part), jnp.float32)
-                        spot = i * per_wave + half * (per_wave // 2)
-                        weight = value if weight is None else jnp.where(lane >= spot, value, weight)
-                weights.append(weight)
+    packed_parts = [
+        packed_orders(total[:, part * OY : (part + 1) * OY], STEPS * RECORDS, kept)
+        for part in range(2)
+    ]
     for target in range(targets):
         sides = []
         for part in range(2):
-            values = total[:, part * OY : (part + 1) * OY]
-            (packed,) = packed_orders(values, STEPS * RECORDS, kept, target)
+            (packed,) = packed_parts[part][target]
             steps = []
             for s in range(STEPS):
                 spread = None
@@ -346,12 +458,13 @@
                 place = pl.ds((tile * 2 + part) * rows, rows)
                 value = monitor_ref[target, place, :]
                 for s in range(STEPS):
-                    real, imag = weights[(tile * STEPS + s) * 2 : (tile * STEPS + s) * 2 + 2]
+                    first = (tile * STEPS + s) * 2
+                    real, imag = weights_ref[first], weights_ref[first + 1]
                     if part == 0:
-                        value = value + (real * sides[0][s] + imag * sides[1][s])
+                        value = value + (real * sides[0][s] - imag * sides[1][s])
                     else:
-                        value = value + (imag * sides[0][s] - real * sides[1][s])
-                out_ref[target, place, :] = value
+                        value = value + (imag * sides[0][s] + real * sides[1][s])
+                out_ref[order_of(targets).index(target), place, :] = value
 
 
 def x_orders(kept, values_ref, table_ref, out_ref):
@@ -382,27 +495,38 @@
     m_ref,
     before_ref,
     after_ref,
-    message_ref,
+    edges_ref,
     message_before_ref,
     message_after_ref,
     slab_ref,
     monitor_ref,
+    e_any,
+    h_any,
+    slab_out_any,
+    monitor_out_any,
     e_out,
     h_out,
     slab_out,
     monitor_out,
+    done,
 ):
     layers, rows, columns = m_ref.shape
     rates = rates_of(perm_ref, perm_ref.shape[0], (rows, columns))
     wide = widened_planes(own_planes(e_ref, h_ref, m_ref, rates), before_ref, after_ref)
     walk = Leapfrog(wide, layers=layers)
     left = iota((2 * rows, layers * SEAM), 1) % SEAM < EDGE
-    edges = [
-        [ref[pl.ds(kind * 2 * rows, 2 * rows), :] for kind in range(KINDS)]
-        for ref in (message_before_ref, message_ref, message_after_ref)
-    ]
-    before = seam_leapfrog([jnp.where(left, edges[0][k], edges[1][k]) for k in range(KINDS)], layers)
-    after = seam_leapfrog([jnp.where(left, edges[1][k], edges[2][k]) for k in range(KINDS)], layers)
+    outer = message_before_ref.shape[0] - -(-KINDS // OUTER) * 2 * rows
+    before, after = [], []
+    for kind in range(KINDS):
+        mine = edges_ref[kind]
+        place = pl.ds(outer + kind // OUTER * 2 * rows, 2 * rows)
+        spot = kind % OUTER * STEPS
+        from_before = rolled(message_before_ref[place, :], STEPS - spot, 1)
+        from_after = rolled(message_after_ref[place, :], EDGE - spot, 1)
+        before.append(jnp.where(left, from_before, mine))
+        after.append(jnp.where(left, mine, from_after))
+    before = seam_leapfrog(before, layers)
+    after = seam_leapfrog(after, layers)
     column = iota((rows, columns), 1)
     inner = (column >= STEPS) & (column < columns - STEPS)
     joined = {}
@@ -429,6 +553,12 @@
                 slab_records[s] = [mended(s + 1, z, kind) for kind in (0, 1)]
             if z == layers - 1:
                 records[s] = [mended(s + 1, z, kind) for kind in (0, 1, 3, 4)]
+    sent = [
+        pltpu.make_async_copy(e_out, e_any, done.at[0]),
+        pltpu.make_async_copy(h_out, h_any, done.at[1]),
+    ]
+    for copy in sent:
+        copy.start()
     frequencies = slab_ref.shape[1] // 2
 
     def one_frequency(f, carry):
@@ -442,6 +572,8 @@
         return carry
 
     lax.fori_loop(0, frequencies, one_frequency, 0, unroll=4)
+    sent.append(pltpu.make_async_copy(slab_out, slab_out_any, done.at[2]))
+    sent[-1].start()
     for w in range(monitor_ref.shape[0]):
         coef = waves_of(coef_ref, wave_ref[w])
         for part in range(2):
@@ -450,6 +582,10 @@
                 for s in range(STEPS):
                     value = value + coef(s, c // 2, part) * records[s][c]
                 monitor_out[w, part, c] = value
+    sent.append(pltpu.make_async_copy(monitor_out, monitor_out_any, done.at[3]))
+    sent[-1].start()
+    for copy in sent:
+        copy.wait()
 
 
 def wave_coefficients(freq_count):
@@ -470,8 +606,34 @@
     return np.concatenate([np.cos(angles), np.sin(angles)], axis=1).astype(np.float32)
 
 
+def split_table(table):
+    table = table.astype(np.float32)
+    coarse = table.astype(ml_dtypes.bfloat16)
+    fine = (table - coarse.astype(np.float32)).astype(ml_dtypes.bfloat16)
+    return jnp.asarray(np.stack([coarse, fine]))
+
+
+def record_table(length, blocks):
+    angles = angles_of(length, OY)
+    table = np.concatenate([np.cos(angles), -np.sin(angles)], axis=1)
+    columns = length // blocks
+    seams = np.zeros((blocks, DEEP, SEAM, 2 * OY))
+    for block in range(blocks):
+        for column in range(-STEPS, STEPS):
+            row = ((block + 1) * columns + column) % length
+            seams[block, DEEP - 1, EDGE + column] = table[row]
+    inner = table.copy()
+    place = np.arange(length) % columns
+    inner[(place < STEPS) | (place >= columns - STEPS)] = 0.0
+    return split_table(np.concatenate([seams.reshape(-1, 2 * OY), inner]))
+
+
+def order_of(blocks):
+    return list(reversed(range(blocks)))
+
+
 def x_table(length, blocks, scaling):
-    angles = angles_of(length, OX).reshape(blocks, length // blocks, OX)
+    angles = angles_of(length, OX).reshape(blocks, length // blocks, OX)[order_of(blocks)]
     real = np.concatenate([np.cos(angles), -np.sin(angles)], axis=2)
     imag = np.concatenate([np.sin(angles), np.cos(angles)], axis=2)
     table = np.stack([real, imag], axis=1) * scaling
@@ -479,12 +641,13 @@
 
 
 def call(kernel, in_specs, shapes, *operands, name, flops=0, moved=0, **more):
-    out = [jax.ShapeDtypeStruct(shape, jnp.float32) for shape in shapes]
+    kind = jax.ShapeDtypeStruct
+    out = [kind(shape, jnp.float32) for shape in shapes]
     return pl.pallas_call(
         kernel,
         out_shape=out,
         in_specs=in_specs,
-        out_specs=[VMEM] * len(out) if "grid" not in more else more.pop("out_specs"),
+        out_specs=more.pop("out_specs", [VMEM] * len(out)),
         compiler_params=PARAMS,
         cost_estimate=pl.CostEstimate(flops=flops, bytes_accessed=moved, transcendentals=0),
         name=name,
@@ -502,70 +665,108 @@
     fields = (electric, magnetic, material)
     groups = layers * STEPS // rows
 
-    spectra = lax.all_to_all(monitor_spectra, "gy", split_axis=0, concat_axis=0, tiled=True)
-
     faces = (KINDS, groups, rows, columns)
-    forth, back = call(
-        pack_faces,
-        [SMEM] + [VMEM] * 3,
-        [faces, faces],
-        permittivity,
-        *fields,
+    block = (group_waves,) + monitor_spectra.shape[1:]
+    late = [1]
+    early = [distance for distance in range(y_blocks) if distance not in late]
+    forth, back, *blocks = call(
+        functools.partial(pack_faces, early),
+        [HBM] * 5,
+        [faces, faces] + [block] * len(early),
+        *[in_hbm(array) for array in (permittivity, *fields, monitor_spectra)],
         name="pack_faces",
         flops=10**5,
         moved=10**6,
+        scratch_shapes=[
+            pltpu.SMEM(permittivity.shape, jnp.float32),
+            pltpu.VMEM(electric.shape, jnp.float32),
+            pltpu.VMEM(magnetic.shape, jnp.float32),
+            pltpu.VMEM(material.shape, jnp.int32),
+            pltpu.SemaphoreType.DMA((4,)),
+            pltpu.SemaphoreType.DMA((len(early),)),
+        ],
     )
     before = passed_along(forth, "gx", 1)
     after = passed_along(back, "gx", -1)
-
-    near_height = (KINDS * 2 + STEPS * RECORDS) * rows
-    far_height = (far_tiles(columns) * 2 + STEPS * RECORDS) * rows
-    near, far = call(
-        monitor_message,
-        [SMEM] + [VMEM] * 5,
-        [(near_height, columns), (far_height, columns)],
+    spectra = {
+        distance: passed_along(block, "gy", -distance) if distance else block
+        for distance, block in zip(early, blocks)
+    }
+
+    far_height = (STEPS * RECORDS + message_tiles(columns) * 2) * rows
+    near_height = far_height + -(-KINDS // OUTER) * 2 * rows
+    forth, back, far, edges, *blocks = call(
+        functools.partial(monitor_message, late),
+        [SMEM] + [VMEM] * 5 + [HBM],
+        [
+            (near_height, columns),
+            (near_height, columns),
+            (far_height, columns),
+            (KINDS, 2 * rows, layers * SEAM),
+        ]
+        + [block] * len(late),
         permittivity,
         *fields,
         before,
         after,
+        in_hbm(monitor_spectra),
+        scratch_shapes=[pltpu.SemaphoreType.DMA((len(late),))],
         name="monitor_message",
         flops=10**5,
         moved=10**6,
     )
-    messages = [near]
-    for distance in range(1, y_blocks):
-        message = near if distance in (1, y_blocks - 1) else far
-        messages.append(passed_along(message, "gy", -distance))
+    message_after = passed_along(back, "gy", -1)
+    message_before = passed_along(forth, "gy", 1)
+    for distance, block in zip(late, blocks):
+        spectra[distance] = passed_along(block, "gy", -distance)
+    messages = [far, message_after]
+    for distance in range(2, y_blocks - 1):
+        messages.append(passed_along(far, "gy", -distance))
+    messages = (messages + [message_before])[:y_blocks]
 
     coefs = jnp.asarray(wave_coefficients(slab_spectra.shape[1] // 2))
     length_x, length_y = rows * x_blocks, columns * y_blocks
     kept = OY // x_blocks
     out_tiles = -(-group_waves * RECORDS * kept // OY)
     sums_y = jnp.asarray(y_table(length_y))
-    (monitor_y,) = call(
-        functools.partial(y_monitor, group_waves),
-        [VMEM] * 2,
-        [(x_blocks, out_tiles * 2 * rows, OY)],
-        sums_y,
-        spectra,
-        name="y_monitor",
-        flops=10**8,
-        moved=2 * 10**6,
-    )
-    (spectrum_y,) = call(
-        functools.partial(y_records, group_waves),
-        [SMEM] * 2 + [VMEM] * (2 + y_blocks),
-        [monitor_y.shape],
+    monitor_y, weights, slab_here, monitor_here = call(
+        y_monitor,
+        [SMEM] * 2 + [VMEM] + [HBM] * 2 + [VMEM] * y_blocks,
+        [
+            (x_blocks, out_tiles * 2 * rows, OY),
+            (out_tiles * STEPS * 2, rows, OY),
+            slab_spectra.shape,
+            monitor_spectra.shape,
+        ],
         wave_index,
         coefs,
         sums_y,
+        in_hbm(slab_spectra),
+        in_hbm(monitor_spectra),
+        *[spectra[distance] for distance in range(y_blocks)],
+        name="y_monitor",
+        scratch_shapes=[pltpu.SemaphoreType.DMA((2,))],
+        flops=10**8,
+        moved=2 * 10**6,
+    )
+    (spectrum_y,) = call(
+        functools.partial(y_records, group_waves),
+        [VMEM] * (3 + y_blocks),
+        [monitor_y.shape],
+        record_table(length_y, y_blocks),
         monitor_y,
+        weights,
         *messages,
         name="y_records",
         flops=10**8,
         moved=2 * 10**6,
     )
-    swapped = lax.all_to_all(spectrum_y, "gx", split_axis=0, concat_axis=0, tiled=True)
+    members = [
+        [x * y_blocks + y for x in order_of(x_blocks)] for y in range(y_blocks)
+    ]
+    swapped = lax.all_to_all(
+        spectrum_y, ("gx", "gy"), split_axis=0, concat_axis=0, axis_index_groups=members, tiled=True
+    )
 
     electric_next, magnetic_next, slab_next, monitor_next = call(
         local_updates,
@@ -577,12 +778,20 @@
         *fields,
         before,
         after,
-        messages[0],
-        messages[-1],
-        messages[1 % y_blocks],
-        slab_spectra,
-        monitor_spectra,
+        edges,
+        message_before,
+        message_after,
+        slab_here,
+        monitor_here,
         name="local_updates",
+        scratch_shapes=[
+            pltpu.VMEM(electric.shape, jnp.float32),
+            pltpu.VMEM(magnetic.shape, jnp.float32),
+            pltpu.VMEM(slab_spectra.shape, jnp.float32),
+            pltpu.VMEM(monitor_spectra.shape, jnp.float32),
+            pltpu.SemaphoreType.DMA((4,)),
+        ],
+        out_specs=[HBM] * 4,
         flops=10**7,
         moved=6 * 10**6,
     )

time: 40.6 us -> 35.1 us (0.86)
  waiting for transfers between devices: 11.8 us -> 3.2 us
  Pallas kernels: 9.85 us -> 12.3 us
  starting transfers between devices: 17.8 us -> 18.5 us
    ppermute x5 -> x8, starting transfers between devices: 7.64 us -> 14.4 us  [passed_along(): return lax.ppermute(block, axis, route)]
    all_to_all x2 -> x1, starting transfers between devices: 10.2 us -> 4.09 us  [per_device(): lax.all_to_all(spectrum_y, ('gx', 'gy'), split_axis=0, concat_axis=0, axi...]
    all_to_all x2 -> x1, waiting for transfers between devices: 5.59 us -> 0.01 us  [per_device(): lax.all_to_all(spectrum_y, ('gx', 'gy'), split_axis=0, concat_axis=0, axi...]
    ppermute x5 -> x8, waiting for transfers between devices: 6.21 us -> 3.19 us  [passed_along(): return lax.ppermute(block, axis, route)]
    pallas_call x6, Pallas kernels: 9.85 us -> 12.3 us  [call(): pl.pallas_call(kernel, out_shape=out, in_specs=in_specs, out_specs=more.p...]
  transfers between devices with their start and end apart: 7 -> 9, of which waited for: 4 -> 2; matrix products, arithmetic and copies ran while one was open for 0% -> 0% of each run, Pallas kernels for 16% -> 24%
where the time goes in v3:
time: 35.1 us; the launch traced here: 34.8 us
  starting transfers between devices  18.5 us (53%)
  Pallas kernels  12.3 us (35%)
  waiting for transfers between devices  3.2 us (9%)
  between operations  0.77 us (2%)
    ppermute x8, starting transfers between devices, passed_along(): return lax.ppermute(block, axis, route)  14.4 us
    pallas_call x6, Pallas kernels, call(): pl.pallas_call(kernel, out_shape=out, in_specs=in_specs, out_specs=more.p...  12.3 us
    all_to_all x1, starting transfers between devices, per_device(): lax.all_to_all(spectrum_y, ('gx', 'gy'), split_axis=0, concat_axis=0, axi...  4.09 us
    ppermute x8, waiting for transfers between devices, passed_along(): return lax.ppermute(block, axis, route)  3.19 us
  transfers between devices with their start and end apart: 9, of which 2 were waited for; matrix products, arithmetic and copies ran while one was open for 0% of the time, Pallas kernels for 24%

profile of v3, /device:TPU:0, one launch (start us, length us, event | category | flops | bytes accessed | tf_op | source)
XLA Modules:
  0.0 34.8 jit_solution(9740261202830030949)
XLA Ops:
  0.6 0.0 copy-start.3
  0.6 0.0 copy-start.1
  0.7 0.0 copy-start
  0.7 1.3 %pack_faces.1 = (f32[7,4,8,128]{3,2,1,0:T(8,128)S(1)}, f32[7,4,8,128]{3,2,1,0:T(8,128)S(1)}, f32[4,2,4,8,128]{4,3,2,1,0:T(8,128)S(1)}, f32[4,2,4,8,128]{4,3,2,1,0:T(8,128)S(1)}, f32[4,2,4,8,128]{4,3,2,1,0:T(8,128)S(1)}) custom-call(f32[4]{0:T(128)} %perm_ref.3, f32[3,16,8,128]{3,2,1,0:T(8,128)} %e_ref.3, f32[3,16,8,128]{3,2,1,0:T(8,128)} %h_ref.3, ...), custom_call_target="tpu_custom_call" | custom-call | flops 100000 | bytes 1000000 | tf_op jit(solution)/shard_map/pack_faces/pallas_call | solution.py:646
  2.0 0.5 %collective-permute-start = (f32[7,4,8,128]{3,2,1,0:T(8,128)S(1)}, f32[7,4,8,128]{3,2,1,0:T(8,128)S(1)}, u32[]{:S(2)}, u32[]{:S(2)}) collective-permute-start(f32[7,4,8,128]{3,2,1,0:T(8,128)S(1)} %get-tuple-element.23), channel_id=1, source_target_pairs={{28,0},{0,4},{4,8},{8,12},{12,16},{16,20},{20,24},{24,28},{29,1},{... | collective-permute-start | bytes 344072 | tf_op jit(solution)/shard_map/ppermute | solution.py:41
  2.5 2.9 %collective-permute-start.1 = (f32[7,4,8,128]{3,2,1,0:T(8,128)S(1)}, f32[7,4,8,128]{3,2,1,0:T(8,128)S(1)}, u32[]{:S(2)}, u32[]{:S(2)}) collective-permute-start(f32[7,4,8,128]{3,2,1,0:T(8,128)S(1)} %get-tuple-element.24), channel_id=1, source_target_pairs={{4,0},{8,4},{12,8},{16,12},{20,16},{24,20},{28,24},{0,28},{5,1},{9... | collective-permute-start | bytes 344072 | tf_op jit(solution)/shard_map/ppermute | solution.py:41
  5.5 0.0 copy-start.7
  5.5 3.3 %collective-permute-start.5 = (f32[4,2,4,8,128]{4,3,2,1,0:T(8,128)S(1)}, f32[4,2,4,8,128]{4,3,2,1,0:T(8,128)S(1)}, u32[]{:S(2)}, u32[]{:S(2)}) collective-permute-start(f32[4,2,4,8,128]{4,3,2,1,0:T(8,128)S(1)} %get-tuple-element.30), channel_id=1, source_target_pairs={{2,0},{3,1},{0,2},{1,3},{6,4},{7,5},{4,6},{5,7},{10,8},{11,9},{8,1... | collective-permute-start | bytes 393224 | tf_op jit(solution)/shard_map/ppermute | solution.py:41
  8.7 0.0 copy-start.4
  8.7 1.6 %collective-permute-start.6 = (f32[4,2,4,8,128]{4,3,2,1,0:T(8,128)S(1)}, f32[4,2,4,8,128]{4,3,2,1,0:T(8,128)S(1)}, u32[]{:S(2)}, u32[]{:S(2)}) collective-permute-start(f32[4,2,4,8,128]{4,3,2,1,0:T(8,128)S(1)} %get-tuple-element.31), channel_id=1, source_target_pairs={{3,0},{0,1},{1,2},{2,3},{7,4},{4,5},{5,6},{6,7},{11,8},{8,9},{9,10... | collective-permute-start | bytes 393224 | tf_op jit(solution)/shard_map/ppermute | solution.py:41
  10.3 0.0 collective-permute-done.before_ref
  10.3 0.0 collective-permute-done.1.after_ref
  10.3 0.0 copy-done.3
  10.3 0.0 copy-done.1
  10.3 0.0 copy-done
  10.4 0.0 copy-done.7
  10.4 2.1 %monitor_message.1 = (f32[128,128]{1,0:T(8,128)S(1)}, f32[128,128]{1,0:T(8,128)S(1)}, f32[96,128]{1,0:T(8,128)S(1)}, f32[7,16,128]{2,1,0:T(8,128)S(1)}, f32[4,2,4,8,128]{4,3,2,1,0:T(8,128)S(1)}) custom-call(f32[4]{0:T(128)S(1)} %copy-done.7, f32[3,16,8,128]{3,2,1,0:T(8,128)S(1)} %copy-done, f32[3,16,8,128]{3,2,1,0:T(8,128)S(1)} %copy-done.1, ...), custom_call_target="tpu_custom_call" | custom-call | flops 100000 | bytes 1000000 | tf_op jit(solution)/shard_map/monitor_message/pallas_call | solution.py:646
  12.5 2.3 %collective-permute-start.4 = (f32[4,2,4,8,128]{4,3,2,1,0:T(8,128)S(1)}, f32[4,2,4,8,128]{4,3,2,1,0:T(8,128)S(1)}, u32[]{:S(2)}, u32[]{:S(2)}) collective-permute-start(f32[4,2,4,8,128]{4,3,2,1,0:T(8,128)S(1)} %get-tuple-element.29), channel_id=1, source_target_pairs={{1,0},{2,1},{3,2},{0,3},{5,4},{6,5},{7,6},{4,7},{9,8},{10,9},{11,1... | collective-permute-start | bytes 393224 | tf_op jit(solution)/shard_map/ppermute | solution.py:41
  14.8 0.0 collective-permute-start.2
  14.8 0.0 copy-start.6
  14.8 3.8 %collective-permute-start.3 = (f32[128,128]{1,0:T(8,128)S(1)}, f32[128,128]{1,0:T(8,128)S(1)}, u32[]{:S(2)}, u32[]{:S(2)}) collective-permute-start(f32[128,128]{1,0:T(8,128)S(1)} %get-tuple-element.27), channel_id=1, source_target_pairs={{1,0},{2,1},{3,2},{0,3},{5,4},{6,5},{7,6},{4,7},{9,8},{10,9},{11,1... | collective-permute-start | bytes 196616 | tf_op jit(solution)/shard_map/ppermute | solution.py:41
  18.6 0.0 collective-permute-done.5.refs_2_
  18.6 0.0 copy-start.8
  18.6 0.0 collective-permute-start.7
  18.6 0.0 collective-permute-done.6.refs_3_
  18.6 2.5 %collective-permute-done.4.refs_1_ = f32[4,2,4,8,128]{4,3,2,1,0:T(8,128)S(1)} collective-permute-done((f32[4,2,4,8,128]{4,3,2,1,0:T(8,128)S(1)}, f32[4,2,4,8,128]{4,3,2,1,0:T(8,128)S(1)}, u32[]{:S(2)}, u32[]{:S(2)}) %collective-permute-start.4) | collective-permute-done | bytes 131104 | tf_op jit(solution)/shard_map/ppermute | solution.py:41
  21.2 0.0 copy-done.4
  21.2 0.0 copy-done.6
  21.2 0.0 copy-done.8
  21.2 0.0 copy-start.2
  21.2 2.9 %y_monitor.1 = (f32[8,32,128]{2,1,0:T(8,128)S(1)}, f32[8,8,128]{2,1,0:T(8,128)S(1)}, f32[2,128,8,128]{3,2,1,0:T(8,128)S(1)}, f32[16,2,4,8,128]{4,3,2,1,0:T(8,128)S(1)}) custom-call(s32[16]{0:T(128)S(1)} %copy-done.8, f32[512]{0:T(512)S(1)} %copy-done.6, f32[512,256]{1,0:T(8,128)S(1)} %copy-done.4, f32[2,128,8,128]{3,2,1,0:T(8,128)} %slab_any.1, ...), custom_call_target="tpu_custom_call" | custom-call | flops 100000000 | bytes 2000000 | tf_op jit(solution)/shard_map/y_monitor/pallas_call | solution.py:646
  24.1 0.6 %collective-permute-done.7.refs_2_ = f32[96,128]{1,0:T(8,128)S(1)} collective-permute-done((f32[96,128]{1,0:T(8,128)S(1)}, f32[96,128]{1,0:T(8,128)S(1)}, u32[]{:S(2)}, u32[]{:S(2)}) %collective-permute-start.7) | collective-permute-done | bytes 49184 | tf_op jit(solution)/shard_map/ppermute | solution.py:41
  24.8 0.0 collective-permute-done.2.message_before_ref.refs_3_
  24.8 0.0 collective-permute-done.3.message_after_ref.refs_1_
  24.8 0.0 copy-done.2
  24.8 1.6 %y_records.1 = f32[8,32,128]{2,1,0:T(8,128)} custom-call(bf16[2,640,256]{2,1,0:T(8,128)(2,1)S(1)} %copy-done.2, f32[8,32,128]{2,1,0:T(8,128)S(1)} %get-tuple-element.38.monitor_ref, f32[8,8,128]{2,1,0:T(8,128)S(1)} %get-tuple-element.39.weights_ref, f32[96,128]{1,0:T(8,128)S(1)} %get-tuple-element.40.refs_0_, ...), custom_call_target="tpu_custom_call" | custom-call | flops 100000000 | bytes 2000000 | tf_op jit(solution)/shard_map/y_records/pallas_call | solution.py:646
  26.4 4.1 %all-to-all-start = ((f32[8,32,128]{2,1,0:T(8,128)}), f32[8,32,128]{2,1,0:T(8,128)S(1)}, u32[]{:S(2)}, u32[]{:S(2)}) async-start(f32[8,32,128]{2,1,0:T(8,128)} %y_records.1), calls=%async_computation | async-start | bytes 262144 | tf_op jit(solution)/shard_map/all_to_all | solution.py:767
  30.5 0.0 copy-start.5
  30.5 3.2 %local_updates.1 = (f32[3,16,8,128]{3,2,1,0:T(8,128)}, f32[3,16,8,128]{3,2,1,0:T(8,128)}, f32[2,128,8,128]{3,2,1,0:T(8,128)}, f32[16,2,4,8,128]{4,3,2,1,0:T(8,128)}) custom-call(f32[4]{0:T(128)S(1)} %copy-done.7, s32[16]{0:T(128)S(1)} %copy-done.8, f32[512]{0:T(512)S(1)} %copy-done.6, f32[3,16,8,128]{3,2,1,0:T(8,128)S(1)} %copy-done, ...), custom_call_target="tpu_custom_call" | custom-call | flops 10000000 | bytes 6000000 | tf_op jit(solution)/shard_map/local_updates/pallas_call | solution.py:646
  33.7 0.0 all-to-all-done.values_ref
  33.7 0.0 copy-done.5
  33.7 1.1 %x_orders.1 = f32[4,2,4,16,64]{4,3,2,1,0:T(8,128)} custom-call(f32[8,32,128]{2,1,0:T(8,128)S(1)} %all-to-all-done.values_ref, f32[128,128]{1,0:T(8,128)S(1)} %copy-done.5), custom_call_target="tpu_custom_call" | custom-call | flops 10000000 | bytes 500000 | tf_op jit(solution)/shard_map/x_orders/pallas_call | solution.py:646
Async XLA Ops:
  0.6 9.7 %copy-start.3 = (s32[16,8,128]{2,1,0:T(8,128)S(1)}, s32[16,8,128]{2,1,0:T(8,128)}, u32[]{:S(2)}) copy-start(s32[16,8,128]{2,1,0:T(8,128)} %m_ref.3) | copy-start | bytes 196612
  0.6 9.7 %copy-start.1 = (f32[3,16,8,128]{3,2,1,0:T(8,128)S(1)}, f32[3,16,8,128]{3,2,1,0:T(8,128)}, u32[]{:S(2)}) copy-start(f32[3,16,8,128]{3,2,1,0:T(8,128)} %h_ref.3) | copy-start | bytes 589828
  0.7 9.7 %copy-start = (f32[3,16,8,128]{3,2,1,0:T(8,128)S(1)}, f32[3,16,8,128]{3,2,1,0:T(8,128)}, u32[]{:S(2)}) copy-start(f32[3,16,8,128]{3,2,1,0:T(8,128)} %e_ref.3) | copy-start | bytes 589828
  2.0 8.3 %collective-permute-start = (f32[7,4,8,128]{3,2,1,0:T(8,128)S(1)}, f32[7,4,8,128]{3,2,1,0:T(8,128)S(1)}, u32[]{:S(2)}, u32[]{:S(2)}) collective-permute-start(f32[7,4,8,128]{3,2,1,0:T(8,128)S(1)} %get-tuple-element.23), channel_id=1, source_target_pairs={{28,0},{0,4},{4,8},{8,12},{12,16},{16,20},{20,24},{24,28},{29,1},{... | collective-permute-start | bytes 344072 | tf_op jit(solution)/shard_map/ppermute | solution.py:41
  2.5 7.8 %collective-permute-start.1 = (f32[7,4,8,128]{3,2,1,0:T(8,128)S(1)}, f32[7,4,8,128]{3,2,1,0:T(8,128)S(1)}, u32[]{:S(2)}, u32[]{:S(2)}) collective-permute-start(f32[7,4,8,128]{3,2,1,0:T(8,128)S(1)} %get-tuple-element.24), channel_id=1, source_target_pairs={{4,0},{8,4},{12,8},{16,12},{20,16},{24,20},{28,24},{0,28},{5,1},{9... | collective-permute-start | bytes 344072 | tf_op jit(solution)/shard_map/ppermute | solution.py:41
  5.5 4.9 %copy-start.7 = (f32[4]{0:T(128)S(1)}, f32[4]{0:T(128)}, u32[]{:S(2)}) copy-start(f32[4]{0:T(128)} %perm_ref.3) | copy-start | bytes 52
  5.5 13.2 %collective-permute-start.5 = (f32[4,2,4,8,128]{4,3,2,1,0:T(8,128)S(1)}, f32[4,2,4,8,128]{4,3,2,1,0:T(8,128)S(1)}, u32[]{:S(2)}, u32[]{:S(2)}) collective-permute-start(f32[4,2,4,8,128]{4,3,2,1,0:T(8,128)S(1)} %get-tuple-element.30), channel_id=1, source_target_pairs={{2,0},{3,1},{0,2},{1,3},{6,4},{7,5},{4,6},{5,7},{10,8},{11,9},{8,1... | collective-permute-start | bytes 393224 | tf_op jit(solution)/shard_map/ppermute | solution.py:41
  8.7 12.4 %copy-start.4 = (f32[512,256]{1,0:T(8,128)S(1)}, f32[512,256]{1,0:T(8,128)}, u32[]{:S(2)}) copy-start(f32[512,256]{1,0:T(8,128)} %constant.9.clone.table_ref) | copy-start | bytes 1572868
  8.7 9.9 %collective-permute-start.6 = (f32[4,2,4,8,128]{4,3,2,1,0:T(8,128)S(1)}, f32[4,2,4,8,128]{4,3,2,1,0:T(8,128)S(1)}, u32[]{:S(2)}, u32[]{:S(2)}) collective-permute-start(f32[4,2,4,8,128]{4,3,2,1,0:T(8,128)S(1)} %get-tuple-element.31), channel_id=1, source_target_pairs={{3,0},{0,1},{1,2},{2,3},{7,4},{4,5},{5,6},{6,7},{11,8},{8,9},{9,10... | collective-permute-start | bytes 393224 | tf_op jit(solution)/shard_map/ppermute | solution.py:41
  12.5 8.7 %collective-permute-start.4 = (f32[4,2,4,8,128]{4,3,2,1,0:T(8,128)S(1)}, f32[4,2,4,8,128]{4,3,2,1,0:T(8,128)S(1)}, u32[]{:S(2)}, u32[]{:S(2)}) collective-permute-start(f32[4,2,4,8,128]{4,3,2,1,0:T(8,128)S(1)} %get-tuple-element.29), channel_id=1, source_target_pairs={{1,0},{2,1},{3,2},{0,3},{5,4},{6,5},{7,6},{4,7},{9,8},{10,9},{11,1... | collective-permute-start | bytes 393224 | tf_op jit(solution)/shard_map/ppermute | solution.py:41
  14.8 10.0 %collective-permute-start.2 = (f32[128,128]{1,0:T(8,128)S(1)}, f32[128,128]{1,0:T(8,128)S(1)}, u32[]{:S(2)}, u32[]{:S(2)}) collective-permute-start(f32[128,128]{1,0:T(8,128)S(1)} %get-tuple-element.26), channel_id=1, source_target_pairs={{3,0},{0,1},{1,2},{2,3},{7,4},{4,5},{5,6},{6,7},{11,8},{8,9},{9,10... | collective-permute-start | bytes 196616 | tf_op jit(solution)/shard_map/ppermute | solution.py:41
  14.8 6.4 %copy-start.6 = (f32[512]{0:T(512)S(1)}, f32[512]{0:T(512)}, u32[]{:S(2)}) copy-start(f32[512]{0:T(512)} %constant.8.clone.coef_ref) | copy-start | bytes 6148
  14.8 10.0 %collective-permute-start.3 = (f32[128,128]{1,0:T(8,128)S(1)}, f32[128,128]{1,0:T(8,128)S(1)}, u32[]{:S(2)}, u32[]{:S(2)}) collective-permute-start(f32[128,128]{1,0:T(8,128)S(1)} %get-tuple-element.27), channel_id=1, source_target_pairs={{1,0},{2,1},{3,2},{0,3},{5,4},{6,5},{7,6},{4,7},{9,8},{10,9},{11,1... | collective-permute-start | bytes 196616 | tf_op jit(solution)/shard_map/ppermute | solution.py:41
  18.6 2.6 %copy-start.8 = (s32[16]{0:T(128)S(1)}, s32[16]{0:T(128)}, u32[]{:S(2)}) copy-start(s32[16]{0:T(128)} %wave_ref.3) | copy-start | bytes 196
  18.6 6.1 %collective-permute-start.7 = (f32[96,128]{1,0:T(8,128)S(1)}, f32[96,128]{1,0:T(8,128)S(1)}, u32[]{:S(2)}, u32[]{:S(2)}) collective-permute-start(f32[96,128]{1,0:T(8,128)S(1)} %get-tuple-element.40.refs_0_), channel_id=1, source_target_pairs={{2,0},{3,1},{0,2},{1,3},{6,4},{7,5},{4,6},{5,7},{10,8},{11,9},{8,1... | collective-permute-start | bytes 147464 | tf_op jit(solution)/shard_map/ppermute | solution.py:41
  21.2 3.6 %copy-start.2 = (bf16[2,640,256]{2,1,0:T(8,128)(2,1)S(1)}, bf16[2,640,256]{2,1,0:T(8,128)(2,1)}, u32[]{:S(2)}) copy-start(bf16[2,640,256]{2,1,0:T(8,128)(2,1)} %constant.10.clone.table_ref) | copy-start | bytes 1966084
  26.4 7.3 %all-to-all-start = ((f32[8,32,128]{2,1,0:T(8,128)}), f32[8,32,128]{2,1,0:T(8,128)S(1)}, u32[]{:S(2)}, u32[]{:S(2)}) async-start(f32[8,32,128]{2,1,0:T(8,128)} %y_records.1), calls=%async_computation | async-start | bytes 262144 | tf_op jit(solution)/shard_map/all_to_all | solution.py:767
  30.5 3.2 %copy-start.5 = (f32[128,128]{1,0:T(8,128)S(1)}, f32[128,128]{1,0:T(8,128)}, u32[]{:S(2)}) copy-start(f32[128,128]{1,0:T(8,128)} %constant.11.clone.table_ref) | copy-start | bytes 196612

commit v4 on v3

--- a/solution.py
+++ b/solution.py
@@ -27,6 +27,7 @@
 
 VMEM = pl.BlockSpec(memory_space=pltpu.VMEM)
 HBM = pl.BlockSpec(memory_space=pltpu.HBM)
+ANY = pl.BlockSpec(memory_space=pl.ANY)
 SMEM = pl.BlockSpec(memory_space=pltpu.SMEM)
 PARAMS = pltpu.CompilerParams(vmem_limit_bytes=48 * 1024 * 1024)
 
@@ -130,7 +131,9 @@
     return at
 
 
-def widened_planes(own, before_ref, after_ref, first_group=0):
+def widened_planes(own, same_ref, cross_ref):
+    even = lax.rem(lax.axis_index("gx"), 2) == 0
+
     def at(z):
         planes = own(z)
         rows = planes[0].shape[0]
@@ -138,8 +141,9 @@
         row = iota(planes[0].shape, 0)
         wide = []
         for kind in range(KINDS):
-            after = rolled(after_ref[kind, group], -STEPS * place, 0)
-            before = rolled(before_ref[kind, group], rows - STEPS - STEPS * place, 0)
+            same, cross = same_ref[kind, group], cross_ref[kind, group]
+            after = rolled(jnp.where(even, same, cross), -STEPS * place, 0)
+            before = rolled(jnp.where(even, cross, same), rows - STEPS - STEPS * place, 0)
             halo = jnp.where(row < STEPS, after, before)
             wide.append(jnp.concatenate([planes[kind], halo], axis=0))
         return wide
@@ -162,10 +166,11 @@
     h_any,
     m_any,
     spectra_any,
-    forth_ref,
-    back_ref,
+    same_ref,
+    cross_ref,
     *refs,
 ):
+    even = lax.rem(lax.axis_index("gx"), 2) == 0
     *block_refs, perm_ref, e_ref, h_ref, m_ref, ready, sent = refs
     sources, targets = (e_any, h_any, m_any, perm_any), (e_ref, h_ref, m_ref, perm_ref)
     copies = [
@@ -193,8 +198,8 @@
                 here = planes[place][kind]
                 forth = jnp.where(row >= spot, rolled(here, spot + STEPS - rows, 0), forth)
                 back = jnp.where(row >= spot, rolled(here, spot, 0), back)
-            forth_ref[kind, group] = forth
-            back_ref[kind, group] = back
+            same_ref[kind, group] = jnp.where(even, forth, back)
+            cross_ref[kind, group] = jnp.where(even, back, forth)
     for copy in copies[4:]:
         copy.wait()
 
@@ -227,70 +232,75 @@
     return tile
 
 
+def squeezed(first, second):
+    rows = first.shape[0] // 2
+    row = iota((rows, first.shape[1]), 0)
+    ends = (row < STEPS) | (row >= rows - STEPS)
+    second_halo = second[rows:]
+    moved = jnp.where(
+        row < 2 * STEPS, rolled(second_halo, STEPS, 0), rolled(second_halo, -STEPS, 0)
+    )
+    return first[:rows], second[:rows], jnp.where(ends, first[rows:], moved)
+
+
+def stretched(first, second, halo):
+    rows = first.shape[0]
+    row = iota(halo.shape, 0)
+    moved = jnp.where(row < 2 * STEPS, rolled(halo, -STEPS, 0), rolled(halo, STEPS, 0))
+    return jnp.concatenate([first, halo], axis=0), jnp.concatenate([second, moved], axis=0)
+
+
+def pair_of_tiles(ref, pair, rows):
+    base = (STEPS * RECORDS + 3 * pair) * rows
+    return stretched(*[ref[pl.ds(base + i * rows, rows), :] for i in range(3)])
+
+
 def monitor_message(
-    distances,
     perm_ref,
     e_ref,
     h_ref,
     m_ref,
-    before_ref,
-    after_ref,
-    spectra_any,
+    same_ref,
+    cross_ref,
+    block_any,
     forth_ref,
     back_ref,
     far_ref,
     edges_ref,
-    *refs,
+    block_out,
 ):
-    *block_refs, sent = refs
-    copies = [
-        block_copy(distance, spectra_any, block_ref, sent.at[i])
-        for i, (distance, block_ref) in enumerate(zip(distances, block_refs))
-    ]
-    for copy in copies:
-        copy.start()
     layers, rows, columns = m_ref.shape
     rates = rates_of(perm_ref, perm_ref.shape[0], (rows, columns))
-    wide = widened_planes(own_planes(e_ref, h_ref, m_ref, rates), before_ref, after_ref)
+    wide = widened_planes(own_planes(e_ref, h_ref, m_ref, rates), same_ref, cross_ref)
     low = layers - DEEP
     walk = Leapfrog(lambda z: wide(low + z), layers=DEEP)
-    height = 2 * rows
-    messages = (forth_ref, back_ref, far_ref)
     for s in range(STEPS):
         for c, record in enumerate(walk.records(s + 1, DEEP - 1)):
             place = pl.ds((s * RECORDS + c) * rows, rows)
-            for ref in messages:
+            for ref in (forth_ref, back_ref, far_ref):
                 ref[place, :] = record[:rows]
     planes = [wide(z) for z in range(low)] + [walk.first(z) for z in range(DEEP)]
     span = DEEP * SEAM
     per_tile = columns // span
-    base = STEPS * RECORDS * rows
-    outer = base + message_tiles(columns) * height
-    total = forth = back = None
+    tops, lasts, firsts = ([None, None] for _ in range(3))
     for kind in range(KINDS):
         edges = packed_edges([planes[z][kind] for z in range(layers)], layers, 0)
         edges_ref[kind] = edges
         lane = iota(edges.shape, 1)
-        spot = kind % per_tile * span
-        here = rolled(edges, spot - low * SEAM, 1)
-        total = jnp.where(lane >= spot, here, total) if spot else here
-        place = pl.ds(base + kind // per_tile * height, height)
-        for ref in messages:
-            ref[place, :] = total
-        spot = kind % OUTER * STEPS
-        here = rolled(edges, spot - STEPS, 1)
-        forth = jnp.where(lane % SEAM >= spot, here, forth) if spot else here
-        here = rolled(edges, spot - EDGE, 1)
-        back = jnp.where(lane % SEAM >= spot, here, back) if spot else here
-        place = pl.ds(outer + kind // OUTER * height, height)
-        forth_ref[place, :] = forth
-        back_ref[place, :] = back
-    for copy in copies:
-        copy.wait()
-
-
-def message_tiles(columns):
-    return -(-KINDS // (columns // (DEEP * SEAM)))
+        tile, spot = divmod(kind, per_tile)
+        here = rolled(edges, spot * span - low * SEAM, 1)
+        tops[tile] = jnp.where(lane >= spot * span, here, tops[tile]) if spot else here
+        tile, spot = divmod(kind, OUTER)
+        for tiles, shift in ((lasts, STEPS), (firsts, EDGE)):
+            here = rolled(edges, spot * STEPS - shift, 1)
+            tiles[tile] = jnp.where(lane % SEAM >= spot * STEPS, here, tiles[tile]) if spot else here
+    base = STEPS * RECORDS * rows
+    for i, part in enumerate(squeezed(*tops)):
+        for ref in (forth_ref, back_ref, far_ref):
+            ref[pl.ds(base + i * rows, rows), :] = part
+    for ref, tiles in ((forth_ref, lasts), (back_ref, firsts)):
+        for i, part in enumerate(squeezed(*tiles)):
+            ref[pl.ds(base + (3 + i) * rows, rows), :] = part
 
 
 def waves_of(coef_ref, wave):
@@ -339,27 +349,32 @@
     return packed
 
 
-def y_monitor(wave_ref, coef_ref, table_ref, slab_any, monitor_any, *refs):
-    *spectra, out_ref, weights_ref, slab_ref, monitor_ref, ready = refs
+def fetch(after_this, slab_any, monitor_any, slab_ref, monitor_ref, ready):
     copies = [
         pltpu.make_async_copy(slab_any, slab_ref, ready.at[0]),
         pltpu.make_async_copy(monitor_any, monitor_ref, ready.at[1]),
     ]
     for copy in copies:
         copy.start()
+    for copy in copies:
+        copy.wait()
+
+
+def y_monitor(wave_ref, coef_ref, table_ref, after_this, *refs):
+    *spectra, out_ref, weights_ref = refs
     blocks = len(spectra)
     waves, _, records, rows, columns = spectra[0].shape
     me = lax.axis_index("gy")
     total = None
     for block in range(blocks):
         owner = lax.rem(me + block, blocks)
-        table = table_ref[pl.ds(pl.multiple_of(owner * columns, columns), columns), :]
+        place = pl.ds(pl.multiple_of(owner * columns, columns), columns)
         parts = []
         for part in range(2):
             for w in range(waves):
                 parts += [spectra[block][w, part, c] for c in range(records)]
-        product = exact_dot(jnp.concatenate(parts, axis=0), table, ((1,), (0,)))
-        total = product if total is None else total + product
+        tables = [table_ref[i, place, :] for i in range(2)]
+        total = split_dot(jnp.concatenate(parts, axis=0), tables, total)
     half = waves * records * rows
     real = total[:half, :OY] + total[half:, OY:]
     imag = total[half:, :OY] - total[:half, OY:]
@@ -385,8 +400,6 @@
                         spot = i * per_wave + half * (per_wave // 2)
                         weight = value if weight is None else jnp.where(lane >= spot, value, weight)
                 weights_ref[(tile * STEPS + s) * 2 + part] = weight
-    for copy in copies:
-        copy.wait()
 
 
 def y_records(waves, table_ref, monitor_ref, weights_ref, *refs):
@@ -401,20 +414,17 @@
     span = DEEP * SEAM
     per_tile = columns // span
     base = STEPS * RECORDS * rows
-    lane = iota((2 * rows, columns), 1)
-    column = lane % SEAM
-
-    def edges_of(block, tile):
-        return messages[block][pl.ds(base + tile * 2 * rows, 2 * rows), :]
+    column = iota((2 * rows, columns), 1) % SEAM
+    edges = [pair_of_tiles(message, 0, rows) for message in messages]
 
     total = None
     for tile in range(-(-blocks // per_tile)):
         seams = range(tile * per_tile, min(blocks, (tile + 1) * per_tile))
         kinds = []
-        for part in range(message_tiles(columns)):
+        for part in range(2):
             mixed = []
             for seam in list(seams) + [seams[0]] * (per_tile - len(seams)):
-                here, after = edges_of(seam, part), edges_of((seam + 1) % blocks, part)
+                here, after = edges[seam][part], edges[(seam + 1) % blocks][part]
                 mixed.append(jnp.where(column < EDGE, here, after))
             kinds += blocks_transposed(mixed)
         walk = seam_leapfrog(kinds[:KINDS], DEEP)
@@ -493,8 +503,8 @@
     e_ref,
     h_ref,
     m_ref,
-    before_ref,
-    after_ref,
+    same_ref,
+    cross_ref,
     edges_ref,
     message_before_ref,
     message_after_ref,
@@ -512,17 +522,17 @@
 ):
     layers, rows, columns = m_ref.shape
     rates = rates_of(perm_ref, perm_ref.shape[0], (rows, columns))
-    wide = widened_planes(own_planes(e_ref, h_ref, m_ref, rates), before_ref, after_ref)
+    wide = widened_planes(own_planes(e_ref, h_ref, m_ref, rates), same_ref, cross_ref)
     walk = Leapfrog(wide, layers=layers)
     left = iota((2 * rows, layers * SEAM), 1) % SEAM < EDGE
-    outer = message_before_ref.shape[0] - -(-KINDS // OUTER) * 2 * rows
+    last = pair_of_tiles(message_before_ref, 1, rows)
+    first = pair_of_tiles(message_after_ref, 1, rows)
     before, after = [], []
     for kind in range(KINDS):
         mine = edges_ref[kind]
-        place = pl.ds(outer + kind // OUTER * 2 * rows, 2 * rows)
-        spot = kind % OUTER * STEPS
-        from_before = rolled(message_before_ref[place, :], STEPS - spot, 1)
-        from_after = rolled(message_after_ref[place, :], EDGE - spot, 1)
+        tile, spot = divmod(kind, OUTER)
+        from_before = rolled(last[tile], STEPS - spot * STEPS, 1)
+        from_after = rolled(first[tile], EDGE - spot * STEPS, 1)
         before.append(jnp.where(left, from_before, mine))
         after.append(jnp.where(left, mine, from_after))
     before = seam_leapfrog(before, layers)
@@ -603,7 +613,7 @@
 
 def y_table(length):
     angles = angles_of(length, OY)
-    return np.concatenate([np.cos(angles), np.sin(angles)], axis=1).astype(np.float32)
+    return split_table(np.concatenate([np.cos(angles), np.sin(angles)], axis=1))
 
 
 def split_table(table):
@@ -669,10 +679,10 @@
     block = (group_waves,) + monitor_spectra.shape[1:]
     late = [1]
     early = [distance for distance in range(y_blocks) if distance not in late]
-    forth, back, *blocks = call(
-        functools.partial(pack_faces, early),
+    same, cross, *blocks = call(
+        functools.partial(pack_faces, early + late),
         [HBM] * 5,
-        [faces, faces] + [block] * len(early),
+        [faces, faces] + [block] * y_blocks,
         *[in_hbm(array) for array in (permittivity, *fields, monitor_spectra)],
         name="pack_faces",
         flops=10**5,
@@ -683,21 +693,23 @@
             pltpu.VMEM(magnetic.shape, jnp.float32),
             pltpu.VMEM(material.shape, jnp.int32),
             pltpu.SemaphoreType.DMA((4,)),
-            pltpu.SemaphoreType.DMA((len(early),)),
+            pltpu.SemaphoreType.DMA((y_blocks,)),
         ],
     )
-    before = passed_along(forth, "gx", 1)
-    after = passed_along(back, "gx", -1)
+    line = range(x_blocks)
+    same = lax.ppermute(same, "gx", [(i, i ^ 1) for i in line])
+    cross = lax.ppermute(cross, "gx", [(i, (i + (1 if i % 2 else -1)) % x_blocks) for i in line])
     spectra = {
         distance: passed_along(block, "gy", -distance) if distance else block
         for distance, block in zip(early, blocks)
     }
-
-    far_height = (STEPS * RECORDS + message_tiles(columns) * 2) * rows
-    near_height = far_height + -(-KINDS // OUTER) * 2 * rows
+    held_back = blocks[len(early) :]
+
+    far_height = (STEPS * RECORDS + 3) * rows
+    near_height = far_height + 3 * rows
     forth, back, far, edges, *blocks = call(
-        functools.partial(monitor_message, late),
-        [SMEM] + [VMEM] * 5 + [HBM],
+        monitor_message,
+        [SMEM] + [VMEM] * 5 + [ANY],
         [
             (near_height, columns),
             (near_height, columns),
@@ -707,10 +719,11 @@
         + [block] * len(late),
         permittivity,
         *fields,
-        before,
-        after,
-        in_hbm(monitor_spectra),
-        scratch_shapes=[pltpu.SemaphoreType.DMA((len(late),))],
+        same,
+        cross,
+        *held_back,
+        input_output_aliases={6: 4},
+        out_specs=[VMEM] * 4 + [ANY],
         name="monitor_message",
         flops=10**5,
         moved=10**6,
@@ -728,24 +741,29 @@
     length_x, length_y = rows * x_blocks, columns * y_blocks
     kept = OY // x_blocks
     out_tiles = -(-group_waves * RECORDS * kept // OY)
-    sums_y = jnp.asarray(y_table(length_y))
-    monitor_y, weights, slab_here, monitor_here = call(
+    sums_y = y_table(length_y)
+    slab_here, monitor_here = call(
+        fetch,
+        [ANY] + [HBM] * 2,
+        [slab_spectra.shape, monitor_spectra.shape],
+        far,
+        in_hbm(slab_spectra),
+        in_hbm(monitor_spectra),
+        name="fetch",
+        flops=1,
+        moved=3 * 10**6,
+        scratch_shapes=[pltpu.SemaphoreType.DMA((2,))],
+    )
+    monitor_y, weights = call(
         y_monitor,
-        [SMEM] * 2 + [VMEM] + [HBM] * 2 + [VMEM] * y_blocks,
-        [
-            (x_blocks, out_tiles * 2 * rows, OY),
-            (out_tiles * STEPS * 2, rows, OY),
-            slab_spectra.shape,
-            monitor_spectra.shape,
-        ],
+        [SMEM] * 2 + [VMEM, ANY] + [VMEM] * y_blocks,
+        [(x_blocks, out_tiles * 2 * rows, OY), (out_tiles * STEPS * 2, rows, OY)],
         wave_index,
         coefs,
         sums_y,
-        in_hbm(slab_spectra),
-        in_hbm(monitor_spectra),
+        slab_here,
         *[spectra[distance] for distance in range(y_blocks)],
         name="y_monitor",
-        scratch_shapes=[pltpu.SemaphoreType.DMA((2,))],
         flops=10**8,
         moved=2 * 10**6,
     )
@@ -776,8 +794,8 @@
         wave_index,
         coefs,
         *fields,
-        before,
-        after,
+        same,
+        cross,
         edges,
         message_before,
         message_after,

time: 35.1 us -> 34.6 us (0.986)
  Pallas kernels: 12.3 us -> 11.3 us
  local copies, waits for them, and re-layouts: 0.04 us -> 0.68 us
  waiting for transfers between devices: 3.2 us -> 2.8 us
    ppermute x0 -> x2, starting transfers between devices: none -> 4.07 us  [the longest x1 3.56 us: per_device(): lax.ppermute(cross, 'gx', [(i, (i + (1 if i % 2 else -1)) % x_blocks) for...]
    ppermute x8 -> x6, starting transfers between devices: 14.4 us -> 10.7 us  [passed_along(): return lax.ppermute(block, axis, route)]
    pallas_call x6 -> x7, Pallas kernels: 12.3 us -> 11.3 us  [call(): pl.pallas_call(kernel, out_shape=out, in_specs=in_specs, out_specs=more.p...]
    unnamed x18, local copies, waits for them, and re-layouts: 0.04 us -> 0.68 us
    ppermute x8 -> x6, waiting for transfers between devices: 3.19 us -> 2.79 us  [passed_along(): return lax.ppermute(block, axis, route)]
  transfers between devices with their start and end apart: 9 -> 9, of which waited for: 2 -> 3; matrix products, arithmetic and copies ran while one was open for 0% -> 0% of each run, Pallas kernels for 24% -> 21%
where the time goes in v4:
time: 34.6 us; the launch traced here: 34.3 us
  starting transfers between devices  18.8 us (54%)
  Pallas kernels  11.3 us (33%)
  waiting for transfers between devices  2.8 us (8%)
  between operations  0.77 us (2%)
  local copies, waits for them, and re-layouts  0.68 us (2%)
    pallas_call x7, Pallas kernels, call(): pl.pallas_call(kernel, out_shape=out, in_specs=in_specs, out_specs=more.p...  11.3 us
    ppermute x6, starting transfers between devices, passed_along(): return lax.ppermute(block, axis, route)  10.7 us
    all_to_all x1, starting transfers between devices, per_device(): lax.all_to_all(spectrum_y, ('gx', 'gy'), split_axis=0, concat_axis=0, axi...  4.01 us
    ppermute x1, starting transfers between devices, per_device(): lax.ppermute(cross, 'gx', [(i, (i + (1 if i % 2 else -1)) % x_blocks) for...  3.56 us
    ppermute x6, waiting for transfers between devices, passed_along(): return lax.ppermute(block, axis, route)  2.79 us
  transfers between devices with their start and end apart: 9, of which 3 were waited for; matrix products, arithmetic and copies ran while one was open for 0% of the time, Pallas kernels for 21%

profile of v4, /device:TPU:0, one launch (start us, length us, event | category | flops | bytes accessed | tf_op | source)
XLA Modules:
  0.0 34.3 jit_solution(10852692094488005522)
XLA Ops:
  0.6 0.0 copy-start.3
  0.6 0.0 copy-start.1
  0.7 0.0 copy-start
  0.7 1.4 %pack_faces.1 = (f32[7,4,8,128]{3,2,1,0:T(8,128)S(1)}, f32[7,4,8,128]{3,2,1,0:T(8,128)S(1)}, f32[4,2,4,8,128]{4,3,2,1,0:T(8,128)S(1)}, f32[4,2,4,8,128]{4,3,2,1,...) custom-call(f32[4]{0:T(128)} %perm_ref.3, f32[3,16,8,128]{3,2,1,0:T(8,128)} %e_ref.3, ...), custom_call_target="tpu_custom_call" | custom-call | flops 100000 | bytes 1000000 | tf_op jit(solution)/shard_map/pack_faces/pallas_call | solution.py:656
  2.0 0.5 %collective-permute-start = (f32[7,4,8,128]{3,2,1,0:T(8,128)S(1)}, f32[7,4,8,128]{3,2,1,0:T(8,128)S(1)}, u32[]{:S(2)}, u32[]{:S(2)}) collective-permute-start(f32[7,4,8,128]{3,2,1,0:T(8,128)S(1)} %get-tuple-element.24), channel_id=1, source_target_pairs={{0,4},{4,0},{8,12},{12,8},{16,20},{20,16},{24,28},{28,24},{1,5},{5... | collective-permute-start | bytes 344072 | tf_op jit(solution)/shard_map/ppermute | solution.py:700
  2.6 3.6 %collective-permute-start.1 = (f32[7,4,8,128]{3,2,1,0:T(8,128)S(1)}, f32[7,4,8,128]{3,2,1,0:T(8,128)S(1)}, u32[]{:S(2)}, u32[]{:S(2)}) collective-permute-start(f32[7,4,8,128]{3,2,1,0:T(8,128)S(1)} %get-tuple-element.25), channel_id=1, source_target_pairs={{0,28},{4,8},{8,4},{12,16},{16,12},{20,24},{24,20},{28,0},{1,29},{... | collective-permute-start | bytes 344072 | tf_op jit(solution)/shard_map/ppermute | solution.py:701
  6.1 2.6 %collective-permute-start.5 = (f32[4,2,4,8,128]{4,3,2,1,0:T(8,128)S(1)}, f32[4,2,4,8,128]{4,3,2,1,0:T(8,128)S(1)}, u32[]{:S(2)}, u32[]{:S(2)}) collective-permute-start(f32[4,2,4,8,128]{4,3,2,1,0:T(8,128)S(1)} %get-tuple-element.39), channel_id=1, source_target_pairs={{2,0},{3,1},{0,2},{1,3},{6,4},{7,5},{4,6},{5,7},{10,8},{11,9},{8,1... | collective-permute-start | bytes 393224 | tf_op jit(solution)/shard_map/ppermute | solution.py:42
  8.7 0.0 copy-start.7
  8.7 1.6 %collective-permute-start.6 = (f32[4,2,4,8,128]{4,3,2,1,0:T(8,128)S(1)}, f32[4,2,4,8,128]{4,3,2,1,0:T(8,128)S(1)}, u32[]{:S(2)}, u32[]{:S(2)}) collective-permute-start(f32[4,2,4,8,128]{4,3,2,1,0:T(8,128)S(1)} %get-tuple-element.40), channel_id=1, source_target_pairs={{3,0},{0,1},{1,2},{2,3},{7,4},{4,5},{5,6},{6,7},{11,8},{8,9},{9,10... | collective-permute-start | bytes 393224 | tf_op jit(solution)/shard_map/ppermute | solution.py:42
  10.3 0.0 collective-permute-done.same_ref
  10.3 0.0 collective-permute-done.1.cross_ref
  10.3 0.0 copy-done.3
  10.3 0.0 copy-done.1
  10.3 0.0 copy-done
  10.3 0.0 copy-done.7
  10.3 1.3 %monitor_message.1 = (f32[112,128]{1,0:T(8,128)S(1)}, f32[112,128]{1,0:T(8,128)S(1)}, f32[88,128]{1,0:T(8,128)S(1)}, f32[7,16,128]{2,1,0:T(8,128)S(1)}, f32[4,2,4,8,128]{4,3,2,1,0:T(8,128)S(1)}) custom-call(f32[4]{0:T(128)S(1)} %copy-done.7, f32[3,16,8,128]{3,2,1,0:T(8,128)S(1)} %copy-done, ...), custom_call_target="tpu_custom_call", output_to_operand_aliasing={{4}: (6, {})} | custom-call | flops 100000 | bytes 1000000 | tf_op jit(solution)/shard_map/monitor_message/pallas_call | solution.py:656
  11.6 2.7 %collective-permute-start.4 = (f32[4,2,4,8,128]{4,3,2,1,0:T(8,128)S(1)}, f32[4,2,4,8,128]{4,3,2,1,0:T(8,128)S(1)}, u32[]{:S(2)}, u32[]{:S(2)}) collective-permute-start(f32[4,2,4,8,128]{4,3,2,1,0:T(8,128)S(1)} %get-tuple-element.38), channel_id=1, source_target_pairs={{1,0},{2,1},{3,2},{0,3},{5,4},{6,5},{7,6},{4,7},{9,8},{10,9},{11,1... | collective-permute-start | bytes 393224 | tf_op jit(solution)/shard_map/ppermute | solution.py:42
  14.3 0.0 collective-permute-start.2
  14.3 3.8 %collective-permute-start.3 = (f32[112,128]{1,0:T(8,128)S(1)}, f32[112,128]{1,0:T(8,128)S(1)}, u32[]{:S(2)}, u32[]{:S(2)}) collective-permute-start(f32[112,128]{1,0:T(8,128)S(1)} %get-tuple-element.29), channel_id=1, source_target_pairs={{1,0},{2,1},{3,2},{0,3},{5,4},{6,5},{7,6},{4,7},{9,8},{10,9},{11,1... | collective-permute-start | bytes 172040 | tf_op jit(solution)/shard_map/ppermute | solution.py:42
  18.1 0.3 collective-permute-done.5.refs_2_
  18.4 0.0 copy-start.4
  18.4 0.0 collective-permute-start.7
  18.4 1.4 %fetch.1 = (f32[2,128,8,128]{3,2,1,0:T(8,128)S(1)}, f32[16,2,4,8,128]{4,3,2,1,0:T(8,128)S(1)}) custom-call(f32[88,128]{1,0:T(8,128)S(1)} %get-tuple-element.30.after_this.refs_0_, f32[2,128,8,128]{3,2,1,0:T(8,128)} %slab_any.1, f32[16,2,4,8,128]{4,3,2,1,0:T(8,128)} %monitor_any.1), custom_call_target="tpu_custom_call" | custom-call | flops 1 | bytes 3000000 | tf_op jit(solution)/shard_map/fetch/pallas_call | solution.py:656
  19.8 0.0 copy-start.6
  19.8 0.0 collective-permute-done.6.refs_3_
  19.9 1.5 %collective-permute-done.4.refs_1_ = f32[4,2,4,8,128]{4,3,2,1,0:T(8,128)S(1)} collective-permute-done((f32[4,2,4,8,128]{4,3,2,1,0:T(8,128)S(1)}, f32[4,2,4,8,128]{4,3,2,1,0:T(8,128)S(1)}, u32[]{:S(2)}, u32[]{:S(2)}) %collective-permute-start.4) | collective-permute-done | bytes 131104 | tf_op jit(solution)/shard_map/ppermute | solution.py:42
  21.4 0.0 copy-start.8
  21.4 0.0 copy-done.4
  21.4 0.0 copy-done.6
  21.4 0.6 %copy-done.8 = s32[16]{0:T(128)S(1)} copy-done((s32[16]{0:T(128)S(1)}, s32[16]{0:T(128)}, u32[]{:S(2)}) %copy-start.8) | copy-done | bytes 88
  22.0 0.0 copy-start.2
  22.0 1.4 %y_monitor.1 = (f32[8,32,128]{2,1,0:T(8,128)S(1)}, f32[8,8,128]{2,1,0:T(8,128)S(1)}) custom-call(s32[16]{0:T(128)S(1)} %copy-done.8, f32[512]{0:T(512)S(1)} %copy-done.6, bf16[2,512,256]{2,1,0:T(8,128)(2,1)S(1)} %copy-done.4, f32[2,128,8,128]{3,2,1,0:T(8,128)S(1)} %get-tuple-element.31.slab_ref.after_this, ...), custom_call_target="tpu_custom_call" | custom-call | flops 100000000 | bytes 2000000 | tf_op jit(solution)/shard_map/y_monitor/pallas_call | solution.py:656
  23.4 1.0 %collective-permute-done.7.refs_2_ = f32[88,128]{1,0:T(8,128)S(1)} collective-permute-done((f32[88,128]{1,0:T(8,128)S(1)}, f32[88,128]{1,0:T(8,128)S(1)}, u32[]{:S(2)}, u32[]{:S(2)}) %collective-permute-start.7) | collective-permute-done | bytes 45088 | tf_op jit(solution)/shard_map/ppermute | solution.py:42
  24.4 0.0 collective-permute-done.2.message_before_ref.refs_3_
  24.4 0.0 collective-permute-done.3.message_after_ref.refs_1_
  24.4 0.0 copy-done.2
  24.4 1.6 %y_records.1 = f32[8,32,128]{2,1,0:T(8,128)} custom-call(bf16[2,640,256]{2,1,0:T(8,128)(2,1)S(1)} %copy-done.2, f32[8,32,128]{2,1,0:T(8,128)S(1)} %get-tuple-element.41.monitor_ref, f32[8,8,128]{2,1,0:T(8,128)S(1)} %get-tuple-element.42.weights_ref, f32[88,128]{1,0:T(8,128)S(1)} %get-tuple-element.30.after_this.refs_0_, ...), custom_call_target="tpu_custom_call" | custom-call | flops 100000000 | bytes 2000000 | tf_op jit(solution)/shard_map/y_records/pallas_call | solution.py:656
  26.1 4.0 %all-to-all-start = ((f32[8,32,128]{2,1,0:T(8,128)}), f32[8,32,128]{2,1,0:T(8,128)S(1)}, u32[]{:S(2)}, u32[]{:S(2)}) async-start(f32[8,32,128]{2,1,0:T(8,128)} %y_records.1), calls=%async_computation | async-start | bytes 262144 | tf_op jit(solution)/shard_map/all_to_all | solution.py:785
  30.1 0.0 copy-start.5
  30.1 3.1 %local_updates.1 = (f32[3,16,8,128]{3,2,1,0:T(8,128)}, f32[3,16,8,128]{3,2,1,0:T(8,128)}, f32[2,128,8,128]{3,2,1,0:T(8,128)}, f32[16,2,4,8,128]{4,3,2,1,0:T(8,128)}) custom-call(f32[4]{0:T(128)S(1)} %copy-done.7, s32[16]{0:T(128)S(1)} %copy-done.8, f32[512]{0:T(512)S(1)} %copy-done.6, f32[3,16,8,128]{3,2,1,0:T(8,128)S(1)} %copy-done, ...), custom_call_target="tpu_custom_call" | custom-call | flops 10000000 | bytes 6000000 | tf_op jit(solution)/shard_map/local_updates/pallas_call | solution.py:656
  33.2 0.0 all-to-all-done.values_ref
  33.2 0.0 copy-done.5
  33.2 1.1 %x_orders.1 = f32[4,2,4,16,64]{4,3,2,1,0:T(8,128)} custom-call(f32[8,32,128]{2,1,0:T(8,128)S(1)} %all-to-all-done.values_ref, f32[128,128]{1,0:T(8,128)S(1)} %copy-done.5), custom_call_target="tpu_custom_call" | custom-call | flops 10000000 | bytes 500000 | tf_op jit(solution)/shard_map/x_orders/pallas_call | solution.py:656
Async XLA Ops:
  0.6 9.7 %copy-start.3 = (s32[16,8,128]{2,1,0:T(8,128)S(1)}, s32[16,8,128]{2,1,0:T(8,128)}, u32[]{:S(2)}) copy-start(s32[16,8,128]{2,1,0:T(8,128)} %m_ref.3) | copy-start | bytes 196612
  0.6 9.7 %copy-start.1 = (f32[3,16,8,128]{3,2,1,0:T(8,128)S(1)}, f32[3,16,8,128]{3,2,1,0:T(8,128)}, u32[]{:S(2)}) copy-start(f32[3,16,8,128]{3,2,1,0:T(8,128)} %h_ref.3) | copy-start | bytes 589828
  0.7 9.7 %copy-start = (f32[3,16,8,128]{3,2,1,0:T(8,128)S(1)}, f32[3,16,8,128]{3,2,1,0:T(8,128)}, u32[]{:S(2)}) copy-start(f32[3,16,8,128]{3,2,1,0:T(8,128)} %e_ref.3) | copy-start | bytes 589828
  2.0 8.2 %collective-permute-start = (f32[7,4,8,128]{3,2,1,0:T(8,128)S(1)}, f32[7,4,8,128]{3,2,1,0:T(8,128)S(1)}, u32[]{:S(2)}, u32[]{:S(2)}) collective-permute-start(f32[7,4,8,128]{3,2,1,0:T(8,128)S(1)} %get-tuple-element.24), channel_id=1, source_target_pairs={{0,4},{4,0},{8,12},{12,8},{16,20},{20,16},{24,28},{28,24},{1,5},{5... | collective-permute-start | bytes 344072 | tf_op jit(solution)/shard_map/ppermute | solution.py:700
  2.6 7.7 %collective-permute-start.1 = (f32[7,4,8,128]{3,2,1,0:T(8,128)S(1)}, f32[7,4,8,128]{3,2,1,0:T(8,128)S(1)}, u32[]{:S(2)}, u32[]{:S(2)}) collective-permute-start(f32[7,4,8,128]{3,2,1,0:T(8,128)S(1)} %get-tuple-element.25), channel_id=1, source_target_pairs={{0,28},{4,8},{8,4},{12,16},{16,12},{20,24},{24,20},{28,0},{1,29},{... | collective-permute-start | bytes 344072 | tf_op jit(solution)/shard_map/ppermute | solution.py:701
  6.1 12.3 %collective-permute-start.5 = (f32[4,2,4,8,128]{4,3,2,1,0:T(8,128)S(1)}, f32[4,2,4,8,128]{4,3,2,1,0:T(8,128)S(1)}, u32[]{:S(2)}, u32[]{:S(2)}) collective-permute-start(f32[4,2,4,8,128]{4,3,2,1,0:T(8,128)S(1)} %get-tuple-element.39), channel_id=1, source_target_pairs={{2,0},{3,1},{0,2},{1,3},{6,4},{7,5},{4,6},{5,7},{10,8},{11,9},{8,1... | collective-permute-start | bytes 393224 | tf_op jit(solution)/shard_map/ppermute | solution.py:42
  8.7 1.6 %copy-start.7 = (f32[4]{0:T(128)S(1)}, f32[4]{0:T(128)}, u32[]{:S(2)}) copy-start(f32[4]{0:T(128)} %perm_ref.3) | copy-start | bytes 52
  8.7 11.1 %collective-permute-start.6 = (f32[4,2,4,8,128]{4,3,2,1,0:T(8,128)S(1)}, f32[4,2,4,8,128]{4,3,2,1,0:T(8,128)S(1)}, u32[]{:S(2)}, u32[]{:S(2)}) collective-permute-start(f32[4,2,4,8,128]{4,3,2,1,0:T(8,128)S(1)} %get-tuple-element.40), channel_id=1, source_target_pairs={{3,0},{0,1},{1,2},{2,3},{7,4},{4,5},{5,6},{6,7},{11,8},{8,9},{9,10... | collective-permute-start | bytes 393224 | tf_op jit(solution)/shard_map/ppermute | solution.py:42
  11.6 9.8 %collective-permute-start.4 = (f32[4,2,4,8,128]{4,3,2,1,0:T(8,128)S(1)}, f32[4,2,4,8,128]{4,3,2,1,0:T(8,128)S(1)}, u32[]{:S(2)}, u32[]{:S(2)}) collective-permute-start(f32[4,2,4,8,128]{4,3,2,1,0:T(8,128)S(1)} %get-tuple-element.38), channel_id=1, source_target_pairs={{1,0},{2,1},{3,2},{0,3},{5,4},{6,5},{7,6},{4,7},{9,8},{10,9},{11,1... | collective-permute-start | bytes 393224 | tf_op jit(solution)/shard_map/ppermute | solution.py:42
  14.3 10.1 %collective-permute-start.2 = (f32[112,128]{1,0:T(8,128)S(1)}, f32[112,128]{1,0:T(8,128)S(1)}, u32[]{:S(2)}, u32[]{:S(2)}) collective-permute-start(f32[112,128]{1,0:T(8,128)S(1)} %get-tuple-element.28), channel_id=1, source_target_pairs={{3,0},{0,1},{1,2},{2,3},{7,4},{4,5},{5,6},{6,7},{11,8},{8,9},{9,10... | collective-permute-start | bytes 172040 | tf_op jit(solution)/shard_map/ppermute | solution.py:42
  14.3 10.1 %collective-permute-start.3 = (f32[112,128]{1,0:T(8,128)S(1)}, f32[112,128]{1,0:T(8,128)S(1)}, u32[]{:S(2)}, u32[]{:S(2)}) collective-permute-start(f32[112,128]{1,0:T(8,128)S(1)} %get-tuple-element.29), channel_id=1, source_target_pairs={{1,0},{2,1},{3,2},{0,3},{5,4},{6,5},{7,6},{4,7},{9,8},{10,9},{11,1... | collective-permute-start | bytes 172040 | tf_op jit(solution)/shard_map/ppermute | solution.py:42
  18.4 3.0 %copy-start.4 = (bf16[2,512,256]{2,1,0:T(8,128)(2,1)S(1)}, bf16[2,512,256]{2,1,0:T(8,128)(2,1)}, u32[]{:S(2)}) copy-start(bf16[2,512,256]{2,1,0:T(8,128)(2,1)} %constant.9.clone.table_ref) | copy-start | bytes 1572868
  18.4 6.0 %collective-permute-start.7 = (f32[88,128]{1,0:T(8,128)S(1)}, f32[88,128]{1,0:T(8,128)S(1)}, u32[]{:S(2)}, u32[]{:S(2)}) collective-permute-start(f32[88,128]{1,0:T(8,128)S(1)} %get-tuple-element.30.after_this.refs_0_), channel_id=1, source_target_pairs={{2,0},{3,1},{0,2},{1,3},{6,4},{7,5},{4,6},{5,7},{10,8},{11,9},{8,1... | collective-permute-start | bytes 135176 | tf_op jit(solution)/shard_map/ppermute | solution.py:42
  19.8 1.5 %copy-start.6 = (f32[512]{0:T(512)S(1)}, f32[512]{0:T(512)}, u32[]{:S(2)}) copy-start(f32[512]{0:T(512)} %constant.8.clone.coef_ref) | copy-start | bytes 6148
  21.4 0.7 %copy-start.8 = (s32[16]{0:T(128)S(1)}, s32[16]{0:T(128)}, u32[]{:S(2)}) copy-start(s32[16]{0:T(128)} %wave_ref.3) | copy-start | bytes 196
  22.0 2.4 %copy-start.2 = (bf16[2,640,256]{2,1,0:T(8,128)(2,1)S(1)}, bf16[2,640,256]{2,1,0:T(8,128)(2,1)}, u32[]{:S(2)}) copy-start(bf16[2,640,256]{2,1,0:T(8,128)(2,1)} %constant.10.clone.table_ref) | copy-start | bytes 1966084
  26.1 7.2 %all-to-all-start = ((f32[8,32,128]{2,1,0:T(8,128)}), f32[8,32,128]{2,1,0:T(8,128)S(1)}, u32[]{:S(2)}, u32[]{:S(2)}) async-start(f32[8,32,128]{2,1,0:T(8,128)} %y_records.1), calls=%async_computation | async-start | bytes 262144 | tf_op jit(solution)/shard_map/all_to_all | solution.py:785
  30.1 3.2 %copy-start.5 = (f32[128,128]{1,0:T(8,128)S(1)}, f32[128,128]{1,0:T(8,128)}, u32[]{:S(2)}) copy-start(f32[128,128]{1,0:T(8,128)} %constant.11.clone.table_ref) | copy-start | bytes 196612

commit v5 on v4

--- a/solution.py
+++ b/solution.py
@@ -318,11 +318,13 @@
     )
 
 
-def split_dot(values, tables, total):
+def split_dot(values, tables, total, contracted=((1,), (0,))):
     coarse = values.astype(jnp.bfloat16)
     fine = (values - coarse.astype(jnp.float32)).astype(jnp.bfloat16)
     for left, right in ((coarse, tables[0]), (fine, tables[0]), (coarse, tables[1])):
-        product = jnp.dot(left, right, preferred_element_type=jnp.float32)
+        product = lax.dot_general(
+            left, right, (contracted, ((), ())), preferred_element_type=jnp.float32
+        )
         total = product if total is None else total + product
     return total
 
@@ -360,11 +362,12 @@
         copy.wait()
 
 
-def y_monitor(wave_ref, coef_ref, table_ref, after_this, *refs):
+def y_monitor(wave_ref, coef_ref, table_ref, own_ref, *refs):
     *spectra, out_ref, weights_ref = refs
-    blocks = len(spectra)
+    blocks = len(spectra) + 1
     waves, _, records, rows, columns = spectra[0].shape
     me = lax.axis_index("gy")
+    spectra = [own_ref.at[pl.ds(me * waves, waves)]] + spectra
     total = None
     for block in range(blocks):
         owner = lax.rem(me + block, blocks)
@@ -403,7 +406,8 @@
 
 
 def y_records(waves, table_ref, monitor_ref, weights_ref, *refs):
-    *messages, out_ref = refs
+    *messages, out_any, out_ref, done = refs
+    messages = messages[::-1]
     blocks = len(messages)
     columns = messages[0].shape[1]
     targets, height, _ = out_ref.shape
@@ -451,7 +455,9 @@
         packed_orders(total[:, part * OY : (part + 1) * OY], STEPS * RECORDS, kept)
         for part in range(2)
     ]
+    copies = []
     for target in range(targets):
+        spot = order_of(targets).index(target)
         sides = []
         for part in range(2):
             (packed,) = packed_parts[part][target]
@@ -474,20 +480,26 @@
                         value = value + (real * sides[0][s] - imag * sides[1][s])
                     else:
                         value = value + (imag * sides[0][s] + real * sides[1][s])
-                out_ref[order_of(targets).index(target), place, :] = value
+                out_ref[spot, place, :] = value
+        copies.append(
+            pltpu.make_async_copy(out_ref.at[spot], out_any.at[spot], done.at[spot])
+        )
+        copies[-1].start()
+    for copy in copies:
+        copy.wait()
 
 
 def x_orders(kept, values_ref, table_ref, out_ref):
     sources, height, lanes = values_ref.shape
     waves, _, records, _, _ = out_ref.shape
-    depth = table_ref.shape[0]
+    depth = table_ref.shape[1]
     rows = depth // sources
     per_tile = lanes // kept
     for tile in range(height // rows):
         values = jnp.concatenate(
             [values_ref[source, pl.ds(tile * rows, rows), :] for source in range(sources)], axis=0
         )
-        result = exact_dot(values, table_ref[...], ((0,), (0,)))
+        result = split_dot(values, [table_ref[0], table_ref[1]], None, ((0,), (0,)))
         for place in range(per_tile):
             wave, record = divmod(tile * per_tile + place, records)
             if wave < waves:
@@ -506,8 +518,8 @@
     same_ref,
     cross_ref,
     edges_ref,
+    message_after_ref,
     message_before_ref,
-    message_after_ref,
     slab_ref,
     monitor_ref,
     e_any,
@@ -647,7 +659,7 @@
     real = np.concatenate([np.cos(angles), -np.sin(angles)], axis=2)
     imag = np.concatenate([np.sin(angles), np.cos(angles)], axis=2)
     table = np.stack([real, imag], axis=1) * scaling
-    return table.reshape(2 * length, 2 * OX).astype(np.float32)
+    return split_table(table.reshape(2 * length, 2 * OX))
 
 
 def call(kernel, in_specs, shapes, *operands, name, flops=0, moved=0, **more):
@@ -678,11 +690,11 @@
     faces = (KINDS, groups, rows, columns)
     block = (group_waves,) + monitor_spectra.shape[1:]
     late = [1]
-    early = [distance for distance in range(y_blocks) if distance not in late]
+    early = [distance for distance in range(1, y_blocks) if distance not in late]
     same, cross, *blocks = call(
         functools.partial(pack_faces, early + late),
         [HBM] * 5,
-        [faces, faces] + [block] * y_blocks,
+        [faces, faces] + [block] * (y_blocks - 1),
         *[in_hbm(array) for array in (permittivity, *fields, monitor_spectra)],
         name="pack_faces",
         flops=10**5,
@@ -693,15 +705,14 @@
             pltpu.VMEM(magnetic.shape, jnp.float32),
             pltpu.VMEM(material.shape, jnp.int32),
             pltpu.SemaphoreType.DMA((4,)),
-            pltpu.SemaphoreType.DMA((y_blocks,)),
+            pltpu.SemaphoreType.DMA((y_blocks - 1,)),
         ],
     )
     line = range(x_blocks)
     same = lax.ppermute(same, "gx", [(i, i ^ 1) for i in line])
     cross = lax.ppermute(cross, "gx", [(i, (i + (1 if i % 2 else -1)) % x_blocks) for i in line])
     spectra = {
-        distance: passed_along(block, "gy", -distance) if distance else block
-        for distance, block in zip(early, blocks)
+        distance: passed_along(block, "gy", -distance) for distance, block in zip(early, blocks)
     }
     held_back = blocks[len(early) :]
 
@@ -728,8 +739,8 @@
         flops=10**5,
         moved=10**6,
     )
+    message_before = passed_along(forth, "gy", 1)
     message_after = passed_along(back, "gy", -1)
-    message_before = passed_along(forth, "gy", 1)
     for distance, block in zip(late, blocks):
         spectra[distance] = passed_along(block, "gy", -distance)
     messages = [far, message_after]
@@ -756,13 +767,13 @@
     )
     monitor_y, weights = call(
         y_monitor,
-        [SMEM] * 2 + [VMEM, ANY] + [VMEM] * y_blocks,
+        [SMEM] * 2 + [VMEM] * (1 + y_blocks),
         [(x_blocks, out_tiles * 2 * rows, OY), (out_tiles * STEPS * 2, rows, OY)],
         wave_index,
         coefs,
         sums_y,
-        slab_here,
-        *[spectra[distance] for distance in range(y_blocks)],
+        monitor_here,
+        *[spectra[distance] for distance in range(1, y_blocks)],
         name="y_monitor",
         flops=10**8,
         moved=2 * 10**6,
@@ -774,7 +785,12 @@
         record_table(length_y, y_blocks),
         monitor_y,
         weights,
-        *messages,
+        *messages[::-1],
+        out_specs=[HBM],
+        scratch_shapes=[
+            pltpu.VMEM(monitor_y.shape, jnp.float32),
+            pltpu.SemaphoreType.DMA((x_blocks,)),
+        ],
         name="y_records",
         flops=10**8,
         moved=2 * 10**6,
@@ -797,8 +813,8 @@
         same,
         cross,
         edges,
+        message_after,
         message_before,
-        message_after,
         slab_here,
         monitor_here,
         name="local_updates",
@@ -820,7 +836,7 @@
         [VMEM] * 2,
         [(group_waves, 2, RECORDS, kept, OX)],
         swapped,
-        jnp.asarray(x_table(length_x, x_blocks, scaling)),
+        x_table(length_x, x_blocks, scaling),
         name="x_orders",
         flops=10**7,
         moved=5 * 10**5,

time: 34.6 us -> 34.6 us (level)
  waiting for transfers between devices: 2.8 us -> 5.23 us
  starting transfers between devices: 18.8 us -> 17 us
  local copies, waits for them, and re-layouts: 0.68 us -> 0.04 us
    ppermute x6, waiting for transfers between devices: 2.79 us -> 5.22 us  [passed_along(): return lax.ppermute(block, axis, route)]
    ppermute x6, starting transfers between devices: 10.7 us -> 8.9 us  [passed_along(): return lax.ppermute(block, axis, route)]
    unnamed x18, local copies, waits for them, and re-layouts: 0.68 us -> 0.04 us
where the time goes in v5:
time: 34.6 us; the launch traced here: 34.3 us
  starting transfers between devices  17 us (49%)
  Pallas kernels  11.2 us (32%)
  waiting for transfers between devices  5.23 us (15%)
  between operations  0.78 us (2%)
    pallas_call x7, Pallas kernels, call(): pl.pallas_call(kernel, out_shape=out, in_specs=in_specs, out_specs=more.p...  11.2 us
    ppermute x6, starting transfers between devices, passed_along(): return lax.ppermute(block, axis, route)  8.9 us
    ppermute x6, waiting for transfers between devices, passed_along(): return lax.ppermute(block, axis, route)  5.22 us
    all_to_all x1, starting transfers between devices, per_device(): lax.all_to_all(spectrum_y, ('gx', 'gy'), split_axis=0, concat_axis=0, axi...  4.02 us
    ppermute x1, starting transfers between devices, per_device(): lax.ppermute(cross, 'gx', [(i, (i + (1 if i % 2 else -1)) % x_blocks) for...  3.56 us
  transfers between devices with their start and end apart: 9, of which 3 were waited for; matrix products, arithmetic and copies ran while one was open for 0% of the time, Pallas kernels for 21%

profile of v5, /device:TPU:0, one launch (start us, length us, event | category | flops | bytes accessed | tf_op | source)
XLA Modules:
  0.0 34.3 jit_solution(2377956158996118409)
XLA Ops:
  0.6 0.0 copy-start.3
  0.6 0.0 copy-start.1
  0.7 0.0 copy-start
  0.7 1.3 %pack_faces.1 = (f32[7,4,8,128]{3,2,1,0:T(8,128)S(1)}, f32[7,4,8,128]{3,2,1,0:T(8,128)S(1)}, f32[4,2,4,8,128]{4,3,2,1,0:T(8,128)S(1)}, f32[4,2,4,8,128]{4,3,2,1,0:T(8,128)S(1)}, f32[4,2,4,8,128]{4,3,2,1,0:T(8,128)S(1)}) custom-call(f32[4]{0:T(128)} %perm_ref.3, f32[3,16,8,128]{3,2,1,0:T(8,128)} %e_ref.3, f32[3,16,8,128]{3,2,1,0:T(8,128)} %h_ref.3, ...), custom_call_target="tpu_custom_call" | custom-call | flops 100000 | bytes 1000000 | tf_op jit(solution)/shard_map/pack_faces/pallas_call | solution.py:668
  2.0 0.5 %collective-permute-start = (f32[7,4,8,128]{3,2,1,0:T(8,128)S(1)}, f32[7,4,8,128]{3,2,1,0:T(8,128)S(1)}, u32[]{:S(2)}, u32[]{:S(2)}) collective-permute-start(f32[7,4,8,128]{3,2,1,0:T(8,128)S(1)} %get-tuple-element.23), channel_id=1, source_target_pairs={{0,4},{4,0},{8,12},{12,8},{16,20},{20,16},{24,28},{28,24},{1,5},{5... | collective-permute-start | bytes 344072 | tf_op jit(solution)/shard_map/ppermute | solution.py:712
  2.5 3.6 %collective-permute-start.1 = (f32[7,4,8,128]{3,2,1,0:T(8,128)S(1)}, f32[7,4,8,128]{3,2,1,0:T(8,128)S(1)}, u32[]{:S(2)}, u32[]{:S(2)}) collective-permute-start(f32[7,4,8,128]{3,2,1,0:T(8,128)S(1)} %get-tuple-element.24), channel_id=1, source_target_pairs={{0,28},{4,8},{8,4},{12,16},{16,12},{20,24},{24,20},{28,0},{1,29},{... | collective-permute-start | bytes 344072 | tf_op jit(solution)/shard_map/ppermute | solution.py:713
  6.1 2.6 %collective-permute-start.5 = (f32[4,2,4,8,128]{4,3,2,1,0:T(8,128)S(1)}, f32[4,2,4,8,128]{4,3,2,1,0:T(8,128)S(1)}, u32[]{:S(2)}, u32[]{:S(2)}) collective-permute-start(f32[4,2,4,8,128]{4,3,2,1,0:T(8,128)S(1)} %get-tuple-element.37), channel_id=1, source_target_pairs={{2,0},{3,1},{0,2},{1,3},{6,4},{7,5},{4,6},{5,7},{10,8},{11,9},{8,1... | collective-permute-start | bytes 393224 | tf_op jit(solution)/shard_map/ppermute | solution.py:42
  8.7 0.0 copy-start.7
  8.7 1.6 %collective-permute-start.6 = (f32[4,2,4,8,128]{4,3,2,1,0:T(8,128)S(1)}, f32[4,2,4,8,128]{4,3,2,1,0:T(8,128)S(1)}, u32[]{:S(2)}, u32[]{:S(2)}) collective-permute-start(f32[4,2,4,8,128]{4,3,2,1,0:T(8,128)S(1)} %get-tuple-element.38), channel_id=1, source_target_pairs={{3,0},{0,1},{1,2},{2,3},{7,4},{4,5},{5,6},{6,7},{11,8},{8,9},{9,10... | collective-permute-start | bytes 393224 | tf_op jit(solution)/shard_map/ppermute | solution.py:42
  10.3 0.0 collective-permute-done.same_ref
  10.3 0.0 collective-permute-done.1.cross_ref
  10.3 0.0 copy-done.3
  10.3 0.0 copy-done.1
  10.3 0.0 copy-done
  10.3 0.0 copy-done.7
  10.3 1.3 %monitor_message.1 = (f32[112,128]{1,0:T(8,128)S(1)}, f32[112,128]{1,0:T(8,128)S(1)}, f32[88,128]{1,0:T(8,128)S(1)}, f32[7,16,128]{2,1,0:T(8,128)S(1)}, f32[4,2,4,8,128]{4,3,2,1,0:T(8,128)S(1)}) custom-call(f32[4]{0:T(128)S(1)} %copy-done.7, f32[3,16,8,128]{3,2,1,0:T(8,128)S(1)} %copy-done, ...), custom_call_target="tpu_custom_call", output_to_operand_aliasing={{4}: (6, {})} | custom-call | flops 100000 | bytes 1000000 | tf_op jit(solution)/shard_map/monitor_message/pallas_call | solution.py:668
  11.6 2.7 %collective-permute-start.4 = (f32[4,2,4,8,128]{4,3,2,1,0:T(8,128)S(1)}, f32[4,2,4,8,128]{4,3,2,1,0:T(8,128)S(1)}, u32[]{:S(2)}, u32[]{:S(2)}) collective-permute-start(f32[4,2,4,8,128]{4,3,2,1,0:T(8,128)S(1)} %get-tuple-element.36), channel_id=1, source_target_pairs={{1,0},{2,1},{3,2},{0,3},{5,4},{6,5},{7,6},{4,7},{9,8},{10,9},{11,1... | collective-permute-start | bytes 393224 | tf_op jit(solution)/shard_map/ppermute | solution.py:42
  14.3 0.4 %collective-permute-start.2 = (f32[112,128]{1,0:T(8,128)S(1)}, f32[112,128]{1,0:T(8,128)S(1)}, u32[]{:S(2)}, u32[]{:S(2)}) collective-permute-start(f32[112,128]{1,0:T(8,128)S(1)} %get-tuple-element.27), channel_id=1, source_target_pairs={{1,0},{2,1},{3,2},{0,3},{5,4},{6,5},{7,6},{4,7},{9,8},{10,9},{11,1... | collective-permute-start | bytes 172040 | tf_op jit(solution)/shard_map/ppermute | solution.py:42
  14.7 1.6 %collective-permute-start.3 = (f32[112,128]{1,0:T(8,128)S(1)}, f32[112,128]{1,0:T(8,128)S(1)}, u32[]{:S(2)}, u32[]{:S(2)}) collective-permute-start(f32[112,128]{1,0:T(8,128)S(1)} %get-tuple-element.28), channel_id=1, source_target_pairs={{3,0},{0,1},{1,2},{2,3},{7,4},{4,5},{5,6},{6,7},{11,8},{8,9},{9,10... | collective-permute-start | bytes 172040 | tf_op jit(solution)/shard_map/ppermute | solution.py:42
  16.3 2.1 %collective-permute-done.5.refs_1_ = f32[4,2,4,8,128]{4,3,2,1,0:T(8,128)S(1)} collective-permute-done((f32[4,2,4,8,128]{4,3,2,1,0:T(8,128)S(1)}, f32[4,2,4,8,128]{4,3,2,1,0:T(8,128)S(1)}, u32[]{:S(2)}, u32[]{:S(2)}) %collective-permute-start.5) | collective-permute-done | bytes 131104 | tf_op jit(solution)/shard_map/ppermute | solution.py:42
  18.3 0.0 copy-start.4
  18.3 0.0 collective-permute-start.7
  18.4 0.0 copy-start.6
  18.4 1.4 %fetch.1 = (f32[2,128,8,128]{3,2,1,0:T(8,128)S(1)}, f32[16,2,4,8,128]{4,3,2,1,0:T(8,128)S(1)}) custom-call(f32[88,128]{1,0:T(8,128)S(1)} %get-tuple-element.29.after_this.refs_3_, f32[2,128,8,128]{3,2,1,0:T(8,128)} %slab_any.1, f32[16,2,4,8,128]{4,3,2,1,0:T(8,128)} %monitor_any.1), custom_call_target="tpu_custom_call" | custom-call | flops 1 | bytes 3000000 | tf_op jit(solution)/shard_map/fetch/pallas_call | solution.py:668
  19.8 0.0 copy-start.8
  19.8 0.0 collective-permute-done.6.refs_2_
  19.8 1.2 %collective-permute-done.4.refs_0_ = f32[4,2,4,8,128]{4,3,2,1,0:T(8,128)S(1)} collective-permute-done((f32[4,2,4,8,128]{4,3,2,1,0:T(8,128)S(1)}, f32[4,2,4,8,128]{4,3,2,1,0:T(8,128)S(1)}, u32[]{:S(2)}, u32[]{:S(2)}) %collective-permute-start.4) | collective-permute-done | bytes 131104 | tf_op jit(solution)/shard_map/ppermute | solution.py:42
  21.0 0.0 copy-done.4
  21.0 0.0 copy-done.6
  21.0 0.0 copy-done.8
  21.0 0.0 copy-start.2
  21.1 1.4 %y_monitor.1 = (f32[8,32,128]{2,1,0:T(8,128)S(1)}, f32[8,8,128]{2,1,0:T(8,128)S(1)}) custom-call(s32[16]{0:T(128)S(1)} %copy-done.8, f32[512]{0:T(512)S(1)} %copy-done.6, bf16[2,512,256]{2,1,0:T(8,128)(2,1)S(1)} %copy-done.4, f32[16,2,4,8,128]{4,3,2,1,0:T(8,128)S(1)} %get-tuple-element.31.monitor_ref.own_ref, ...), custom_call_target="tpu_custom_call" | custom-call | flops 100000000 | bytes 2000000 | tf_op jit(solution)/shard_map/y_monitor/pallas_call | solution.py:668
  22.4 1.9 %collective-permute-done.7.refs_1_ = f32[88,128]{1,0:T(8,128)S(1)} collective-permute-done((f32[88,128]{1,0:T(8,128)S(1)}, f32[88,128]{1,0:T(8,128)S(1)}, u32[]{:S(2)}, u32[]{:S(2)}) %collective-permute-start.7) | collective-permute-done | bytes 45088 | tf_op jit(solution)/shard_map/ppermute | solution.py:42
  24.4 0.0 collective-permute-done.2.message_after_ref.refs_2_
  24.4 0.0 collective-permute-done.3.message_before_ref.refs_0_
  24.4 0.0 copy-done.2
  24.4 1.7 %y_records.1 = f32[8,32,128]{2,1,0:T(8,128)} custom-call(bf16[2,640,256]{2,1,0:T(8,128)(2,1)S(1)} %copy-done.2, f32[8,32,128]{2,1,0:T(8,128)S(1)} %get-tuple-element.39.monitor_ref, f32[8,8,128]{2,1,0:T(8,128)S(1)} %get-tuple-element.40.weights_ref, f32[112,128]{1,0:T(8,128)S(1)} %collective-permute-done.3.message_before_ref.refs_0_, ...), custom_call_target="tpu_custom_call" | custom-call | flops 100000000 | bytes 2000000 | tf_op jit(solution)/shard_map/y_records/pallas_call | solution.py:668
  26.1 4.0 %all-to-all-start = ((f32[8,32,128]{2,1,0:T(8,128)}), f32[8,32,128]{2,1,0:T(8,128)S(1)}, u32[]{:S(2)}, u32[]{:S(2)}) async-start(f32[8,32,128]{2,1,0:T(8,128)} %y_records.1), calls=%async_computation | async-start | bytes 262144 | tf_op jit(solution)/shard_map/all_to_all | solution.py:801
  30.1 0.0 copy-start.5
  30.1 3.1 %local_updates.1 = (f32[3,16,8,128]{3,2,1,0:T(8,128)}, f32[3,16,8,128]{3,2,1,0:T(8,128)}, f32[2,128,8,128]{3,2,1,0:T(8,128)}, f32[16,2,4,8,128]{4,3,2,1,0:T(8,128)}) custom-call(f32[4]{0:T(128)S(1)} %copy-done.7, s32[16]{0:T(128)S(1)} %copy-done.8, f32[512]{0:T(512)S(1)} %copy-done.6, f32[3,16,8,128]{3,2,1,0:T(8,128)S(1)} %copy-done, ...), custom_call_target="tpu_custom_call" | custom-call | flops 10000000 | bytes 6000000 | tf_op jit(solution)/shard_map/local_updates/pallas_call | solution.py:668
  33.2 0.0 all-to-all-done.values_ref
  33.3 0.0 copy-done.5
  33.3 1.0 %x_orders.1 = f32[4,2,4,16,64]{4,3,2,1,0:T(8,128)} custom-call(f32[8,32,128]{2,1,0:T(8,128)S(1)} %all-to-all-done.values_ref, bf16[2,128,128]{2,1,0:T(8,128)(2,1)S(1)} %copy-done.5), custom_call_target="tpu_custom_call" | custom-call | flops 10000000 | bytes 500000 | tf_op jit(solution)/shard_map/x_orders/pallas_call | solution.py:668
Async XLA Ops:
  0.6 9.6 %copy-start.3 = (s32[16,8,128]{2,1,0:T(8,128)S(1)}, s32[16,8,128]{2,1,0:T(8,128)}, u32[]{:S(2)}) copy-start(s32[16,8,128]{2,1,0:T(8,128)} %m_ref.3) | copy-start | bytes 196612
  0.6 9.6 %copy-start.1 = (f32[3,16,8,128]{3,2,1,0:T(8,128)S(1)}, f32[3,16,8,128]{3,2,1,0:T(8,128)}, u32[]{:S(2)}) copy-start(f32[3,16,8,128]{3,2,1,0:T(8,128)} %h_ref.3) | copy-start | bytes 589828
  0.7 9.6 %copy-start = (f32[3,16,8,128]{3,2,1,0:T(8,128)S(1)}, f32[3,16,8,128]{3,2,1,0:T(8,128)}, u32[]{:S(2)}) copy-start(f32[3,16,8,128]{3,2,1,0:T(8,128)} %e_ref.3) | copy-start | bytes 589828
  2.0 8.2 %collective-permute-start = (f32[7,4,8,128]{3,2,1,0:T(8,128)S(1)}, f32[7,4,8,128]{3,2,1,0:T(8,128)S(1)}, u32[]{:S(2)}, u32[]{:S(2)}) collective-permute-start(f32[7,4,8,128]{3,2,1,0:T(8,128)S(1)} %get-tuple-element.23), channel_id=1, source_target_pairs={{0,4},{4,0},{8,12},{12,8},{16,20},{20,16},{24,28},{28,24},{1,5},{5... | collective-permute-start | bytes 344072 | tf_op jit(solution)/shard_map/ppermute | solution.py:712
  2.5 7.7 %collective-permute-start.1 = (f32[7,4,8,128]{3,2,1,0:T(8,128)S(1)}, f32[7,4,8,128]{3,2,1,0:T(8,128)S(1)}, u32[]{:S(2)}, u32[]{:S(2)}) collective-permute-start(f32[7,4,8,128]{3,2,1,0:T(8,128)S(1)} %get-tuple-element.24), channel_id=1, source_target_pairs={{0,28},{4,8},{8,4},{12,16},{16,12},{20,24},{24,20},{28,0},{1,29},{... | collective-permute-start | bytes 344072 | tf_op jit(solution)/shard_map/ppermute | solution.py:713
  6.1 12.3 %collective-permute-start.5 = (f32[4,2,4,8,128]{4,3,2,1,0:T(8,128)S(1)}, f32[4,2,4,8,128]{4,3,2,1,0:T(8,128)S(1)}, u32[]{:S(2)}, u32[]{:S(2)}) collective-permute-start(f32[4,2,4,8,128]{4,3,2,1,0:T(8,128)S(1)} %get-tuple-element.37), channel_id=1, source_target_pairs={{2,0},{3,1},{0,2},{1,3},{6,4},{7,5},{4,6},{5,7},{10,8},{11,9},{8,1... | collective-permute-start | bytes 393224 | tf_op jit(solution)/shard_map/ppermute | solution.py:42
  8.7 1.6 %copy-start.7 = (f32[4]{0:T(128)S(1)}, f32[4]{0:T(128)}, u32[]{:S(2)}) copy-start(f32[4]{0:T(128)} %perm_ref.3) | copy-start | bytes 52
  8.7 11.1 %collective-permute-start.6 = (f32[4,2,4,8,128]{4,3,2,1,0:T(8,128)S(1)}, f32[4,2,4,8,128]{4,3,2,1,0:T(8,128)S(1)}, u32[]{:S(2)}, u32[]{:S(2)}) collective-permute-start(f32[4,2,4,8,128]{4,3,2,1,0:T(8,128)S(1)} %get-tuple-element.38), channel_id=1, source_target_pairs={{3,0},{0,1},{1,2},{2,3},{7,4},{4,5},{5,6},{6,7},{11,8},{8,9},{9,10... | collective-permute-start | bytes 393224 | tf_op jit(solution)/shard_map/ppermute | solution.py:42
  11.6 9.5 %collective-permute-start.4 = (f32[4,2,4,8,128]{4,3,2,1,0:T(8,128)S(1)}, f32[4,2,4,8,128]{4,3,2,1,0:T(8,128)S(1)}, u32[]{:S(2)}, u32[]{:S(2)}) collective-permute-start(f32[4,2,4,8,128]{4,3,2,1,0:T(8,128)S(1)} %get-tuple-element.36), channel_id=1, source_target_pairs={{1,0},{2,1},{3,2},{0,3},{5,4},{6,5},{7,6},{4,7},{9,8},{10,9},{11,1... | collective-permute-start | bytes 393224 | tf_op jit(solution)/shard_map/ppermute | solution.py:42
  14.3 10.1 %collective-permute-start.2 = (f32[112,128]{1,0:T(8,128)S(1)}, f32[112,128]{1,0:T(8,128)S(1)}, u32[]{:S(2)}, u32[]{:S(2)}) collective-permute-start(f32[112,128]{1,0:T(8,128)S(1)} %get-tuple-element.27), channel_id=1, source_target_pairs={{1,0},{2,1},{3,2},{0,3},{5,4},{6,5},{7,6},{4,7},{9,8},{10,9},{11,1... | collective-permute-start | bytes 172040 | tf_op jit(solution)/shard_map/ppermute | solution.py:42
  14.7 9.7 %collective-permute-start.3 = (f32[112,128]{1,0:T(8,128)S(1)}, f32[112,128]{1,0:T(8,128)S(1)}, u32[]{:S(2)}, u32[]{:S(2)}) collective-permute-start(f32[112,128]{1,0:T(8,128)S(1)} %get-tuple-element.28), channel_id=1, source_target_pairs={{3,0},{0,1},{1,2},{2,3},{7,4},{4,5},{5,6},{6,7},{11,8},{8,9},{9,10... | collective-permute-start | bytes 172040 | tf_op jit(solution)/shard_map/ppermute | solution.py:42
  18.3 2.7 %copy-start.4 = (bf16[2,512,256]{2,1,0:T(8,128)(2,1)S(1)}, bf16[2,512,256]{2,1,0:T(8,128)(2,1)}, u32[]{:S(2)}) copy-start(bf16[2,512,256]{2,1,0:T(8,128)(2,1)} %constant.9.clone.table_ref) | copy-start | bytes 1572868
  18.3 6.0 %collective-permute-start.7 = (f32[88,128]{1,0:T(8,128)S(1)}, f32[88,128]{1,0:T(8,128)S(1)}, u32[]{:S(2)}, u32[]{:S(2)}) collective-permute-start(f32[88,128]{1,0:T(8,128)S(1)} %get-tuple-element.29.after_this.refs_3_), channel_id=1, source_target_pairs={{2,0},{3,1},{0,2},{1,3},{6,4},{7,5},{4,6},{5,7},{10,8},{11,9},{8,1... | collective-permute-start | bytes 135176 | tf_op jit(solution)/shard_map/ppermute | solution.py:42
  18.4 2.7 %copy-start.6 = (f32[512]{0:T(512)S(1)}, f32[512]{0:T(512)}, u32[]{:S(2)}) copy-start(f32[512]{0:T(512)} %constant.8.clone.coef_ref) | copy-start | bytes 6148
  19.8 1.2 %copy-start.8 = (s32[16]{0:T(128)S(1)}, s32[16]{0:T(128)}, u32[]{:S(2)}) copy-start(s32[16]{0:T(128)} %wave_ref.3) | copy-start | bytes 196
  21.0 3.3 %copy-start.2 = (bf16[2,640,256]{2,1,0:T(8,128)(2,1)S(1)}, bf16[2,640,256]{2,1,0:T(8,128)(2,1)}, u32[]{:S(2)}) copy-start(bf16[2,640,256]{2,1,0:T(8,128)(2,1)} %constant.10.clone.table_ref) | copy-start | bytes 1966084
  26.1 7.2 %all-to-all-start = ((f32[8,32,128]{2,1,0:T(8,128)}), f32[8,32,128]{2,1,0:T(8,128)S(1)}, u32[]{:S(2)}, u32[]{:S(2)}) async-start(f32[8,32,128]{2,1,0:T(8,128)} %y_records.1), calls=%async_computation | async-start | bytes 262144 | tf_op jit(solution)/shard_map/all_to_all | solution.py:801
  30.1 3.2 %copy-start.5 = (bf16[2,128,128]{2,1,0:T(8,128)(2,1)S(1)}, bf16[2,128,128]{2,1,0:T(8,128)(2,1)}, u32[]{:S(2)}) copy-start(bf16[2,128,128]{2,1,0:T(8,128)(2,1)} %constant.11.clone.table_ref) | copy-start | bytes 196612

commit v6 on v5

--- a/solution.py
+++ b/solution.py
@@ -262,12 +262,10 @@
     m_ref,
     same_ref,
     cross_ref,
-    block_any,
     forth_ref,
     back_ref,
     far_ref,
     edges_ref,
-    block_out,
 ):
     layers, rows, columns = m_ref.shape
     rates = rates_of(perm_ref, perm_ref.shape[0], (rows, columns))
@@ -364,6 +362,8 @@
 
 def y_monitor(wave_ref, coef_ref, table_ref, own_ref, *refs):
     *spectra, out_ref, weights_ref = refs
+    half = len(spectra) // 2
+    spectra = spectra[half + 1 :] + spectra[:1] + spectra[1 : half + 1]
     blocks = len(spectra) + 1
     waves, _, records, rows, columns = spectra[0].shape
     me = lax.axis_index("gy")
@@ -422,6 +422,11 @@
     edges = [pair_of_tiles(message, 0, rows) for message in messages]
 
     total = None
+    for block in range(blocks):
+        owner = lax.rem(me + block, blocks)
+        place = pl.ds(pl.multiple_of(blocks * span + owner * columns, span), columns)
+        values = messages[block][pl.ds(0, base), :]
+        total = split_dot(values, [table_ref[part, place, :] for part in range(2)], total)
     for tile in range(-(-blocks // per_tile)):
         seams = range(tile * per_tile, min(blocks, (tile + 1) * per_tile))
         kinds = []
@@ -443,11 +448,6 @@
             for part in range(2)
         ]
         total = split_dot(values, tables, total)
-    for block in range(blocks):
-        owner = lax.rem(me + block, blocks)
-        place = pl.ds(pl.multiple_of(blocks * span + owner * columns, span), columns)
-        values = messages[block][pl.ds(0, base), :]
-        total = split_dot(values, [table_ref[part, place, :] for part in range(2)], total)
     lane = iota((rows, OY), 1)
     per_wave = RECORDS * kept
     per_tile = OY // per_wave
@@ -689,7 +689,7 @@
 
     faces = (KINDS, groups, rows, columns)
     block = (group_waves,) + monitor_spectra.shape[1:]
-    late = [1]
+    late = []
     early = [distance for distance in range(1, y_blocks) if distance not in late]
     same, cross, *blocks = call(
         functools.partial(pack_faces, early + late),
@@ -720,7 +720,7 @@
     near_height = far_height + 3 * rows
     forth, back, far, edges, *blocks = call(
         monitor_message,
-        [SMEM] + [VMEM] * 5 + [ANY],
+        [SMEM] + [VMEM] * 5,
         [
             (near_height, columns),
             (near_height, columns),
@@ -733,11 +733,9 @@
         same,
         cross,
         *held_back,
-        input_output_aliases={6: 4},
-        out_specs=[VMEM] * 4 + [ANY],
         name="monitor_message",
-        flops=10**5,
-        moved=10**6,
+        flops=1,
+        moved=1,
     )
     message_before = passed_along(forth, "gy", 1)
     message_after = passed_along(back, "gy", -1)
@@ -773,7 +771,7 @@
         coefs,
         sums_y,
         monitor_here,
-        *[spectra[distance] for distance in range(1, y_blocks)],
+        *[spectra[distance] for distance in [y_blocks // 2] + list(range(y_blocks // 2 + 1, y_blocks)) + list(range(1, y_blocks // 2))],
         name="y_monitor",
         flops=10**8,
         moved=2 * 10**6,

time: 34.6 us -> 33.1 us (0.957)
  waiting for transfers between devices: 5.23 us -> 3.69 us
    ppermute x6, waiting for transfers between devices: 5.22 us -> 3.42 us  [passed_along(): return lax.ppermute(block, axis, route)]
    ppermute x6, starting transfers between devices: 8.9 us -> 10.3 us  [passed_along(): return lax.ppermute(block, axis, route)]
    ppermute x1, starting transfers between devices: 3.56 us -> 2.56 us  [per_device(): lax.ppermute(cross, 'gx', [(i, (i + (1 if i % 2 else -1)) % x_blocks) for...]
    ppermute x1, starting transfers between devices: 0.52 us -> 0.01 us  [per_device(): same = lax.ppermute(same, 'gx', [(i, i ^ 1) for i in line])]
  transfers between devices with their start and end apart: 9 -> 9, of which waited for: 3 -> 3; matrix products, arithmetic and copies ran while one was open for 0% -> 0% of each run, Pallas kernels for 21% -> 22%
where the time goes in v6:
time: 33.1 us; the launch traced here: 32.8 us
  starting transfers between devices  17.2 us (52%)
  Pallas kernels  11.1 us (34%)
  waiting for transfers between devices  3.69 us (11%)
  between operations  0.77 us (2%)
    pallas_call x7, Pallas kernels, call(): pl.pallas_call(kernel, out_shape=out, in_specs=in_specs, out_specs=more.p...  11.1 us
    ppermute x6, starting transfers between devices, passed_along(): return lax.ppermute(block, axis, route)  10.3 us
    all_to_all x1, starting transfers between devices, per_device(): lax.all_to_all(spectrum_y, ('gx', 'gy'), split_axis=0, concat_axis=0, axi...  4.36 us
    ppermute x6, waiting for transfers between devices, passed_along(): return lax.ppermute(block, axis, route)  3.42 us
    ppermute x1, starting transfers between devices, per_device(): lax.ppermute(cross, 'gx', [(i, (i + (1 if i % 2 else -1)) % x_blocks) for...  2.56 us
  transfers between devices with their start and end apart: 9, of which 3 were waited for; matrix products, arithmetic and copies ran while one was open for 0% of the time, Pallas kernels for 22%

profile of v6, /device:TPU:0, one launch (start us, length us, event | category | flops | bytes accessed | tf_op | source)
XLA Modules:
  0.0 32.8 jit_solution(13351241165094361468)
XLA Ops:
  0.6 0.0 copy-start.3
  0.6 0.0 copy-start.1
  0.7 0.0 copy-start
  0.7 1.3 %pack_faces.1 = (f32[7,4,8,128]{3,2,1,0:T(8,128)S(1)}, f32[7,4,8,128]{3,2,1,0:T(8,128)S(1)}, f32[4,2,4,8,128]{4,3,2,1,0:T(8,128)S(1)}, f32[4,2,4,8,128]{4,3,2,1,0:T(8,128)S(1)}, f32[4,2,4,8,128]{4,3,2,1,0:T(8,128)S(1)}) custom-call(f32[4]{0:T(128)} %perm_ref.3, f32[3,16,8,128]{3,2,1,0:T(8,128)} %e_ref.3, f32[3,16,8,128]{3,2,1,0:T(8,128)} %h_ref.3, ...), custom_call_target="tpu_custom_call" | custom-call | flops 100000 | bytes 1000000 | tf_op jit(solution)/shard_map/pack_faces/pallas_call | solution.py:668
  2.0 4.1 %collective-permute-start.4 = (f32[4,2,4,8,128]{4,3,2,1,0:T(8,128)S(1)}, f32[4,2,4,8,128]{4,3,2,1,0:T(8,128)S(1)}, u32[]{:S(2)}, u32[]{:S(2)}) collective-permute-start(f32[4,2,4,8,128]{4,3,2,1,0:T(8,128)S(1)} %get-tuple-element.34), channel_id=1, source_target_pairs={{2,0},{3,1},{0,2},{1,3},{6,4},{7,5},{4,6},{5,7},{10,8},{11,9},{8,1... | collective-permute-start | bytes 393224 | tf_op jit(solution)/shard_map/ppermute | solution.py:42
  6.1 0.0 collective-permute-start
  6.1 2.6 %collective-permute-start.1 = (f32[7,4,8,128]{3,2,1,0:T(8,128)S(1)}, f32[7,4,8,128]{3,2,1,0:T(8,128)S(1)}, u32[]{:S(2)}, u32[]{:S(2)}) collective-permute-start(f32[7,4,8,128]{3,2,1,0:T(8,128)S(1)} %get-tuple-element.23), channel_id=1, source_target_pairs={{0,28},{4,8},{8,4},{12,16},{16,12},{20,24},{24,20},{28,0},{1,29},{... | collective-permute-start | bytes 344072 | tf_op jit(solution)/shard_map/ppermute | solution.py:713
  8.7 0.0 copy-start.7
  8.7 1.6 %collective-permute-start.5 = (f32[4,2,4,8,128]{4,3,2,1,0:T(8,128)S(1)}, f32[4,2,4,8,128]{4,3,2,1,0:T(8,128)S(1)}, u32[]{:S(2)}, u32[]{:S(2)}) collective-permute-start(f32[4,2,4,8,128]{4,3,2,1,0:T(8,128)S(1)} %get-tuple-element.35), channel_id=1, source_target_pairs={{3,0},{0,1},{1,2},{2,3},{7,4},{4,5},{5,6},{6,7},{11,8},{8,9},{9,10... | collective-permute-start | bytes 393224 | tf_op jit(solution)/shard_map/ppermute | solution.py:42
  10.3 2.2 %collective-permute-start.6 = (f32[4,2,4,8,128]{4,3,2,1,0:T(8,128)S(1)}, f32[4,2,4,8,128]{4,3,2,1,0:T(8,128)S(1)}, u32[]{:S(2)}, u32[]{:S(2)}) collective-permute-start(f32[4,2,4,8,128]{4,3,2,1,0:T(8,128)S(1)} %get-tuple-element.36), channel_id=1, source_target_pairs={{1,0},{2,1},{3,2},{0,3},{5,4},{6,5},{7,6},{4,7},{9,8},{10,9},{11,1... | collective-permute-start | bytes 393224 | tf_op jit(solution)/shard_map/ppermute | solution.py:42
  12.5 0.0 collective-permute-done.same_ref
  12.5 0.0 collective-permute-done.1.cross_ref
  12.5 0.0 copy-done.3
  12.5 0.0 copy-done.1
  12.5 0.0 copy-done
  12.5 0.0 copy-done.7
  12.5 1.3 %monitor_message.1 = (f32[112,128]{1,0:T(8,128)S(1)}, f32[112,128]{1,0:T(8,128)S(1)}, f32[88,128]{1,0:T(8,128)S(1)}, f32[7,16,128]{2,1,0:T(8,128)S(1)}) custom-call(f32[4]{0:T(128)S(1)} %copy-done.7, f32[3,16,8,128]{3,2,1,0:T(8,128)S(1)} %copy-done, f32[3,16,8,128]{3,2,1,0:T(8,128)S(1)} %copy-done.1, s32[16,8,128]{2,1,0:T(8,128)S(1)} %copy-done.3, ...), custom_call_target="tpu_custom_call" | custom-call | flops 1 | bytes 1 | tf_op jit(solution)/shard_map/monitor_message/pallas_call | solution.py:668
  13.8 0.6 %collective-permute-start.2 = (f32[112,128]{1,0:T(8,128)S(1)}, f32[112,128]{1,0:T(8,128)S(1)}, u32[]{:S(2)}, u32[]{:S(2)}) collective-permute-start(f32[112,128]{1,0:T(8,128)S(1)} %get-tuple-element.25), channel_id=1, source_target_pairs={{1,0},{2,1},{3,2},{0,3},{5,4},{6,5},{7,6},{4,7},{9,8},{10,9},{11,1... | collective-permute-start | bytes 172040 | tf_op jit(solution)/shard_map/ppermute | solution.py:42
  14.4 1.4 %collective-permute-start.3 = (f32[112,128]{1,0:T(8,128)S(1)}, f32[112,128]{1,0:T(8,128)S(1)}, u32[]{:S(2)}, u32[]{:S(2)}) collective-permute-start(f32[112,128]{1,0:T(8,128)S(1)} %get-tuple-element.26), channel_id=1, source_target_pairs={{3,0},{0,1},{1,2},{2,3},{7,4},{4,5},{5,6},{6,7},{11,8},{8,9},{9,10... | collective-permute-start | bytes 172040 | tf_op jit(solution)/shard_map/ppermute | solution.py:42
  15.9 0.0 collective-permute-done.4.refs_0_
  15.9 0.0 copy-start.4
  15.9 0.3 collective-permute-start.7
  16.2 0.0 copy-start.6
  16.2 1.4 %fetch.1 = (f32[2,128,8,128]{3,2,1,0:T(8,128)S(1)}, f32[16,2,4,8,128]{4,3,2,1,0:T(8,128)S(1)}) custom-call(f32[88,128]{1,0:T(8,128)S(1)} %get-tuple-element.27.after_this.refs_3_, f32[2,128,8,128]{3,2,1,0:T(8,128)} %slab_any.1, f32[16,2,4,8,128]{4,3,2,1,0:T(8,128)} %monitor_any.1), custom_call_target="tpu_custom_call" | custom-call | flops 1 | bytes 3000000 | tf_op jit(solution)/shard_map/fetch/pallas_call | solution.py:668
  17.6 0.0 copy-start.8
  17.6 0.0 collective-permute-done.5.refs_1_
  17.6 1.0 %collective-permute-done.6.refs_2_ = f32[4,2,4,8,128]{4,3,2,1,0:T(8,128)S(1)} collective-permute-done((f32[4,2,4,8,128]{4,3,2,1,0:T(8,128)S(1)}, f32[4,2,4,8,128]{4,3,2,1,0:T(8,128)S(1)}, u32[]{:S(2)}, u32[]{:S(2)}) %collective-permute-start.6) | collective-permute-done | bytes 131104 | tf_op jit(solution)/shard_map/ppermute | solution.py:42
  18.6 0.0 copy-done.4
  18.6 0.0 copy-done.6
  18.6 0.0 copy-done.8
  18.6 0.0 copy-start.2
  18.6 1.4 %y_monitor.1 = (f32[8,32,128]{2,1,0:T(8,128)S(1)}, f32[8,8,128]{2,1,0:T(8,128)S(1)}) custom-call(s32[16]{0:T(128)S(1)} %copy-done.8, f32[512]{0:T(512)S(1)} %copy-done.6, bf16[2,512,256]{2,1,0:T(8,128)(2,1)S(1)} %copy-done.4, f32[16,2,4,8,128]{4,3,2,1,0:T(8,128)S(1)} %get-tuple-element.29.monitor_ref.own_ref, ...), custom_call_target="tpu_custom_call" | custom-call | flops 100000000 | bytes 2000000 | tf_op jit(solution)/shard_map/y_monitor/pallas_call | solution.py:668
  20.0 2.5 %collective-permute-done.7.refs_1_ = f32[88,128]{1,0:T(8,128)S(1)} collective-permute-done((f32[88,128]{1,0:T(8,128)S(1)}, f32[88,128]{1,0:T(8,128)S(1)}, u32[]{:S(2)}, u32[]{:S(2)}) %collective-permute-start.7) | collective-permute-done | bytes 45088 | tf_op jit(solution)/shard_map/ppermute | solution.py:42
  22.4 0.0 collective-permute-done.2.message_after_ref.refs_2_
  22.4 0.0 collective-permute-done.3.message_before_ref.refs_0_
  22.4 0.0 copy-done.2
  22.4 1.6 %y_records.1 = f32[8,32,128]{2,1,0:T(8,128)} custom-call(bf16[2,640,256]{2,1,0:T(8,128)(2,1)S(1)} %copy-done.2, f32[8,32,128]{2,1,0:T(8,128)S(1)} %get-tuple-element.37.monitor_ref, f32[8,8,128]{2,1,0:T(8,128)S(1)} %get-tuple-element.38.weights_ref, f32[112,128]{1,0:T(8,128)S(1)} %collective-permute-done.3.message_before_ref.refs_0_, ...), custom_call_target="tpu_custom_call" | custom-call | flops 100000000 | bytes 2000000 | tf_op jit(solution)/shard_map/y_records/pallas_call | solution.py:668
  24.0 4.4 %all-to-all-start = ((f32[8,32,128]{2,1,0:T(8,128)}), f32[8,32,128]{2,1,0:T(8,128)S(1)}, u32[]{:S(2)}, u32[]{:S(2)}) async-start(f32[8,32,128]{2,1,0:T(8,128)} %y_records.1), calls=%async_computation | async-start | bytes 262144 | tf_op jit(solution)/shard_map/all_to_all | solution.py:799
  28.4 0.0 copy-start.5
  28.4 3.1 %local_updates.1 = (f32[3,16,8,128]{3,2,1,0:T(8,128)}, f32[3,16,8,128]{3,2,1,0:T(8,128)}, f32[2,128,8,128]{3,2,1,0:T(8,128)}, f32[16,2,4,8,128]{4,3,2,1,0:T(8,128)}) custom-call(f32[4]{0:T(128)S(1)} %copy-done.7, s32[16]{0:T(128)S(1)} %copy-done.8, f32[512]{0:T(512)S(1)} %copy-done.6, f32[3,16,8,128]{3,2,1,0:T(8,128)S(1)} %copy-done, ...), custom_call_target="tpu_custom_call" | custom-call | flops 10000000 | bytes 6000000 | tf_op jit(solution)/shard_map/local_updates/pallas_call | solution.py:668
  31.5 0.3 all-to-all-done.values_ref
  31.8 0.0 copy-done.5
  31.8 1.0 %x_orders.1 = f32[4,2,4,16,64]{4,3,2,1,0:T(8,128)} custom-call(f32[8,32,128]{2,1,0:T(8,128)S(1)} %all-to-all-done.values_ref, bf16[2,128,128]{2,1,0:T(8,128)(2,1)S(1)} %copy-done.5), custom_call_target="tpu_custom_call" | custom-call | flops 10000000 | bytes 500000 | tf_op jit(solution)/shard_map/x_orders/pallas_call | solution.py:668
Async XLA Ops:
  0.6 11.9 %copy-start.3 = (s32[16,8,128]{2,1,0:T(8,128)S(1)}, s32[16,8,128]{2,1,0:T(8,128)}, u32[]{:S(2)}) copy-start(s32[16,8,128]{2,1,0:T(8,128)} %m_ref.3) | copy-start | bytes 196612
  0.6 11.9 %copy-start.1 = (f32[3,16,8,128]{3,2,1,0:T(8,128)S(1)}, f32[3,16,8,128]{3,2,1,0:T(8,128)}, u32[]{:S(2)}) copy-start(f32[3,16,8,128]{3,2,1,0:T(8,128)} %h_ref.3) | copy-start | bytes 589828
  0.7 11.9 %copy-start = (f32[3,16,8,128]{3,2,1,0:T(8,128)S(1)}, f32[3,16,8,128]{3,2,1,0:T(8,128)}, u32[]{:S(2)}) copy-start(f32[3,16,8,128]{3,2,1,0:T(8,128)} %e_ref.3) | copy-start | bytes 589828
  2.0 13.9 %collective-permute-start.4 = (f32[4,2,4,8,128]{4,3,2,1,0:T(8,128)S(1)}, f32[4,2,4,8,128]{4,3,2,1,0:T(8,128)S(1)}, u32[]{:S(2)}, u32[]{:S(2)}) collective-permute-start(f32[4,2,4,8,128]{4,3,2,1,0:T(8,128)S(1)} %get-tuple-element.34), channel_id=1, source_target_pairs={{2,0},{3,1},{0,2},{1,3},{6,4},{7,5},{4,6},{5,7},{10,8},{11,9},{8,1... | collective-permute-start | bytes 393224 | tf_op jit(solution)/shard_map/ppermute | solution.py:42
  6.1 6.4 %collective-permute-start = (f32[7,4,8,128]{3,2,1,0:T(8,128)S(1)}, f32[7,4,8,128]{3,2,1,0:T(8,128)S(1)}, u32[]{:S(2)}, u32[]{:S(2)}) collective-permute-start(f32[7,4,8,128]{3,2,1,0:T(8,128)S(1)} %get-tuple-element.22), channel_id=1, source_target_pairs={{0,4},{4,0},{8,12},{12,8},{16,20},{20,16},{24,28},{28,24},{1,5},{5... | collective-permute-start | bytes 344072 | tf_op jit(solution)/shard_map/ppermute | solution.py:712
  6.1 6.4 %collective-permute-start.1 = (f32[7,4,8,128]{3,2,1,0:T(8,128)S(1)}, f32[7,4,8,128]{3,2,1,0:T(8,128)S(1)}, u32[]{:S(2)}, u32[]{:S(2)}) collective-permute-start(f32[7,4,8,128]{3,2,1,0:T(8,128)S(1)} %get-tuple-element.23), channel_id=1, source_target_pairs={{0,28},{4,8},{8,4},{12,16},{16,12},{20,24},{24,20},{28,0},{1,29},{... | collective-permute-start | bytes 344072 | tf_op jit(solution)/shard_map/ppermute | solution.py:713
  8.7 3.9 %copy-start.7 = (f32[4]{0:T(128)S(1)}, f32[4]{0:T(128)}, u32[]{:S(2)}) copy-start(f32[4]{0:T(128)} %perm_ref.3) | copy-start | bytes 52
  8.7 8.9 %collective-permute-start.5 = (f32[4,2,4,8,128]{4,3,2,1,0:T(8,128)S(1)}, f32[4,2,4,8,128]{4,3,2,1,0:T(8,128)S(1)}, u32[]{:S(2)}, u32[]{:S(2)}) collective-permute-start(f32[4,2,4,8,128]{4,3,2,1,0:T(8,128)S(1)} %get-tuple-element.35), channel_id=1, source_target_pairs={{3,0},{0,1},{1,2},{2,3},{7,4},{4,5},{5,6},{6,7},{11,8},{8,9},{9,10... | collective-permute-start | bytes 393224 | tf_op jit(solution)/shard_map/ppermute | solution.py:42
  10.3 8.3 %collective-permute-start.6 = (f32[4,2,4,8,128]{4,3,2,1,0:T(8,128)S(1)}, f32[4,2,4,8,128]{4,3,2,1,0:T(8,128)S(1)}, u32[]{:S(2)}, u32[]{:S(2)}) collective-permute-start(f32[4,2,4,8,128]{4,3,2,1,0:T(8,128)S(1)} %get-tuple-element.36), channel_id=1, source_target_pairs={{1,0},{2,1},{3,2},{0,3},{5,4},{6,5},{7,6},{4,7},{9,8},{10,9},{11,1... | collective-permute-start | bytes 393224 | tf_op jit(solution)/shard_map/ppermute | solution.py:42
  13.8 8.6 %collective-permute-start.2 = (f32[112,128]{1,0:T(8,128)S(1)}, f32[112,128]{1,0:T(8,128)S(1)}, u32[]{:S(2)}, u32[]{:S(2)}) collective-permute-start(f32[112,128]{1,0:T(8,128)S(1)} %get-tuple-element.25), channel_id=1, source_target_pairs={{1,0},{2,1},{3,2},{0,3},{5,4},{6,5},{7,6},{4,7},{9,8},{10,9},{11,1... | collective-permute-start | bytes 172040 | tf_op jit(solution)/shard_map/ppermute | solution.py:42
  14.4 8.0 %collective-permute-start.3 = (f32[112,128]{1,0:T(8,128)S(1)}, f32[112,128]{1,0:T(8,128)S(1)}, u32[]{:S(2)}, u32[]{:S(2)}) collective-permute-start(f32[112,128]{1,0:T(8,128)S(1)} %get-tuple-element.26), channel_id=1, source_target_pairs={{3,0},{0,1},{1,2},{2,3},{7,4},{4,5},{5,6},{6,7},{11,8},{8,9},{9,10... | collective-permute-start | bytes 172040 | tf_op jit(solution)/shard_map/ppermute | solution.py:42
  15.9 2.7 %copy-start.4 = (bf16[2,512,256]{2,1,0:T(8,128)(2,1)S(1)}, bf16[2,512,256]{2,1,0:T(8,128)(2,1)}, u32[]{:S(2)}) copy-start(bf16[2,512,256]{2,1,0:T(8,128)(2,1)} %constant.9.clone.table_ref) | copy-start | bytes 1572868
  15.9 6.5 %collective-permute-start.7 = (f32[88,128]{1,0:T(8,128)S(1)}, f32[88,128]{1,0:T(8,128)S(1)}, u32[]{:S(2)}, u32[]{:S(2)}) collective-permute-start(f32[88,128]{1,0:T(8,128)S(1)} %get-tuple-element.27.after_this.refs_3_), channel_id=1, source_target_pairs={{2,0},{3,1},{0,2},{1,3},{6,4},{7,5},{4,6},{5,7},{10,8},{11,9},{8,1... | collective-permute-start | bytes 135176 | tf_op jit(solution)/shard_map/ppermute | solution.py:42
  16.2 2.4 %copy-start.6 = (f32[512]{0:T(512)S(1)}, f32[512]{0:T(512)}, u32[]{:S(2)}) copy-start(f32[512]{0:T(512)} %constant.8.clone.coef_ref) | copy-start | bytes 6148
  17.6 1.0 %copy-start.8 = (s32[16]{0:T(128)S(1)}, s32[16]{0:T(128)}, u32[]{:S(2)}) copy-start(s32[16]{0:T(128)} %wave_ref.3) | copy-start | bytes 196
  18.6 3.8 %copy-start.2 = (bf16[2,640,256]{2,1,0:T(8,128)(2,1)S(1)}, bf16[2,640,256]{2,1,0:T(8,128)(2,1)}, u32[]{:S(2)}) copy-start(bf16[2,640,256]{2,1,0:T(8,128)(2,1)} %constant.10.clone.table_ref) | copy-start | bytes 1966084
  24.0 7.8 %all-to-all-start = ((f32[8,32,128]{2,1,0:T(8,128)}), f32[8,32,128]{2,1,0:T(8,128)S(1)}, u32[]{:S(2)}, u32[]{:S(2)}) async-start(f32[8,32,128]{2,1,0:T(8,128)} %y_records.1), calls=%async_computation | async-start | bytes 262144 | tf_op jit(solution)/shard_map/all_to_all | solution.py:799
  28.4 3.4 %copy-start.5 = (bf16[2,128,128]{2,1,0:T(8,128)(2,1)S(1)}, bf16[2,128,128]{2,1,0:T(8,128)(2,1)}, u32[]{:S(2)}) copy-start(bf16[2,128,128]{2,1,0:T(8,128)(2,1)} %constant.11.clone.table_ref) | copy-start | bytes 196612

commit v7 on v6

--- a/solution.py
+++ b/solution.py
@@ -157,6 +157,18 @@
     owner = lax.rem(lax.axis_index("gy") + blocks - distance, blocks)
     source = spectra_any.at[pl.ds(owner * waves, waves)]
     return pltpu.make_async_copy(source, block_ref, semaphore)
+
+
+def other_blocks(distances, after_this, spectra_any, *refs):
+    *block_refs, sent = refs
+    copies = [
+        block_copy(distance, spectra_any, block_ref, sent.at[i])
+        for i, (distance, block_ref) in enumerate(zip(distances, block_refs))
+    ]
+    for copy in copies:
+        copy.start()
+    for copy in copies:
+        copy.wait()
 
 
 def pack_faces(
@@ -689,12 +701,12 @@
 
     faces = (KINDS, groups, rows, columns)
     block = (group_waves,) + monitor_spectra.shape[1:]
-    late = []
-    early = [distance for distance in range(1, y_blocks) if distance not in late]
-    same, cross, *blocks = call(
-        functools.partial(pack_faces, early + late),
+    early = [y_blocks // 2]
+    late = [distance for distance in range(1, y_blocks) if distance not in early]
+    packed, cross, *blocks = call(
+        functools.partial(pack_faces, early),
         [HBM] * 5,
-        [faces, faces] + [block] * (y_blocks - 1),
+        [faces, faces] + [block] * len(early),
         *[in_hbm(array) for array in (permittivity, *fields, monitor_spectra)],
         name="pack_faces",
         flops=10**5,
@@ -705,20 +717,32 @@
             pltpu.VMEM(magnetic.shape, jnp.float32),
             pltpu.VMEM(material.shape, jnp.int32),
             pltpu.SemaphoreType.DMA((4,)),
-            pltpu.SemaphoreType.DMA((y_blocks - 1,)),
+            pltpu.SemaphoreType.DMA((len(early),)),
         ],
     )
     line = range(x_blocks)
-    same = lax.ppermute(same, "gx", [(i, i ^ 1) for i in line])
+    same = lax.ppermute(packed, "gx", [(i, i ^ 1) for i in line])
     cross = lax.ppermute(cross, "gx", [(i, (i + (1 if i % 2 else -1)) % x_blocks) for i in line])
     spectra = {
         distance: passed_along(block, "gy", -distance) for distance, block in zip(early, blocks)
     }
-    held_back = blocks[len(early) :]
+    blocks = call(
+        functools.partial(other_blocks, late),
+        [ANY, HBM],
+        [block] * len(late),
+        packed,
+        in_hbm(monitor_spectra),
+        name="other_blocks",
+        flops=1,
+        moved=1,
+        scratch_shapes=[pltpu.SemaphoreType.DMA((len(late),))],
+    )
+    for distance, block in zip(late, blocks):
+        spectra[distance] = passed_along(block, "gy", -distance)
 
     far_height = (STEPS * RECORDS + 3) * rows
     near_height = far_height + 3 * rows
-    forth, back, far, edges, *blocks = call(
+    forth, back, far, edges = call(
         monitor_message,
         [SMEM] + [VMEM] * 5,
         [
@@ -726,21 +750,17 @@
             (near_height, columns),
             (far_height, columns),
             (KINDS, 2 * rows, layers * SEAM),
-        ]
-        + [block] * len(late),
+        ],
         permittivity,
         *fields,
         same,
         cross,
-        *held_back,
         name="monitor_message",
         flops=1,
         moved=1,
     )
     message_before = passed_along(forth, "gy", 1)
     message_after = passed_along(back, "gy", -1)
-    for distance, block in zip(late, blocks):
-        spectra[distance] = passed_along(block, "gy", -distance)
     messages = [far, message_after]
     for distance in range(2, y_blocks - 1):
         messages.append(passed_along(far, "gy", -distance))

time: 33.1 us -> 32.9 us (level)
  Pallas kernels: 11.1 us -> 12 us
  starting transfers between devices: 17.2 us -> 16.4 us
    ppermute x1, starting transfers between devices: 2.56 us -> 1.61 us  [per_device(): lax.ppermute(cross, 'gx', [(i, (i + (1 if i % 2 else -1)) % x_blocks) for...]
    pallas_call x7 -> x8, Pallas kernels: 11.1 us -> 12 us  [call(): pl.pallas_call(kernel, out_shape=out, in_specs=in_specs, out_specs=more.p...]
    ppermute x6, starting transfers between devices: 10.3 us -> 10.8 us  [passed_along(): return lax.ppermute(block, axis, route)]
    all_to_all x1, starting transfers between devices: 4.36 us -> 3.96 us  [per_device(): lax.all_to_all(spectrum_y, ('gx', 'gy'), split_axis=0, concat_axis=0, axi...]
  transfers between devices with their start and end apart: 9 -> 9, of which waited for: 3 -> 2; matrix products, arithmetic and copies ran while one was open for 0% -> 0% of each run, Pallas kernels for 22% -> 25%
where the time goes in v7:
time: 32.9 us; the launch traced here: 32.6 us
  starting transfers between devices  16.4 us (50%)
  Pallas kernels  12 us (36%)
  waiting for transfers between devices  3.42 us (10%)
  between operations  0.77 us (2%)
    pallas_call x8, Pallas kernels, call(): pl.pallas_call(kernel, out_shape=out, in_specs=in_specs, out_specs=more.p...  12 us
    ppermute x6, starting transfers between devices, passed_along(): return lax.ppermute(block, axis, route)  10.8 us
    all_to_all x1, starting transfers between devices, per_device(): lax.all_to_all(spectrum_y, ('gx', 'gy'), split_axis=0, concat_axis=0, axi...  3.96 us
    ppermute x6, waiting for transfers between devices, passed_along(): return lax.ppermute(block, axis, route)  3.38 us
    ppermute x1, starting transfers between devices, per_device(): lax.ppermute(cross, 'gx', [(i, (i + (1 if i % 2 else -1)) % x_blocks) for...  1.61 us
  transfers between devices with their start and end apart: 9, of which 2 were waited for; matrix products, arithmetic and copies ran while one was open for 0% of the time, Pallas kernels for 25%

profile of v7, /device:TPU:0, one launch (start us, length us, event | category | flops | bytes accessed | tf_op | source)
XLA Modules:
  0.0 32.6 jit_solution(16237406970030298880)
XLA Ops:
  0.6 1.2 %pack_faces.1 = (f32[7,4,8,128]{3,2,1,0:T(8,128)S(1)}, f32[7,4,8,128]{3,2,1,0:T(8,128)S(1)}, f32[4,2,4,8,128]{4,3,2,1,0:T(8,128)S(1)}) custom-call(f32[4]{0:T(128)} %perm_ref.3, f32[3,16,8,128]{3,2,1,0:T(8,128)} %e_ref.3, f32[3,16,8,128]{3,2,1,0:T(8,128)} %h_ref.3, s32[16,8,128]{2,1,0:T(8,128)} %m_ref.3, f32[16,2,4,8,128]{4,3,2,1,0:T(8,128)} %spectra_any.3), custom_call_target="tpu_custom_call" | custom-call | flops 100000 | bytes 1000000 | tf_op jit(solution)/shard_map/pack_faces/pallas_call | solution.py:680
  1.8 4.1 %collective-permute-start.4 = (f32[4,2,4,8,128]{4,3,2,1,0:T(8,128)S(1)}, f32[4,2,4,8,128]{4,3,2,1,0:T(8,128)S(1)}, u32[]{:S(2)}, u32[]{:S(2)}) collective-permute-start(f32[4,2,4,8,128]{4,3,2,1,0:T(8,128)S(1)} %get-tuple-element.34), channel_id=1, source_target_pairs={{2,0},{3,1},{0,2},{1,3},{6,4},{7,5},{4,6},{5,7},{10,8},{11,9},{8,1... | collective-permute-start | bytes 393224 | tf_op jit(solution)/shard_map/ppermute | solution.py:42
  5.9 1.6 %collective-permute-start.1 = (f32[7,4,8,128]{3,2,1,0:T(8,128)S(1)}, f32[7,4,8,128]{3,2,1,0:T(8,128)S(1)}, u32[]{:S(2)}, u32[]{:S(2)}) collective-permute-start(f32[7,4,8,128]{3,2,1,0:T(8,128)S(1)} %get-tuple-element.23), channel_id=1, source_target_pairs={{0,28},{4,8},{8,4},{12,16},{16,12},{20,24},{24,20},{28,0},{1,29},{... | collective-permute-start | bytes 344072 | tf_op jit(solution)/shard_map/ppermute | solution.py:725
  7.5 0.0 copy-start
  7.5 0.0 copy-start.1
  7.5 0.0 copy-start.3
  7.5 0.0 collective-permute-start
  7.5 1.0 %other_blocks.1 = (f32[4,2,4,8,128]{4,3,2,1,0:T(8,128)S(1)}, f32[4,2,4,8,128]{4,3,2,1,0:T(8,128)S(1)}) custom-call(f32[7,4,8,128]{3,2,1,0:T(8,128)S(1)} %get-tuple-element.22.after_this, f32[16,2,4,8,128]{4,3,2,1,0:T(8,128)} %spectra_any.3), custom_call_target="tpu_custom_call" | custom-call | flops 1 | bytes 1 | tf_op jit(solution)/shard_map/other_blocks/pallas_call | solution.py:680
  8.6 0.0 copy-start.7
  8.6 1.6 %collective-permute-start.5 = (f32[4,2,4,8,128]{4,3,2,1,0:T(8,128)S(1)}, f32[4,2,4,8,128]{4,3,2,1,0:T(8,128)S(1)}, u32[]{:S(2)}, u32[]{:S(2)}) collective-permute-start(f32[4,2,4,8,128]{4,3,2,1,0:T(8,128)S(1)} %get-tuple-element.35), channel_id=1, source_target_pairs={{3,0},{0,1},{1,2},{2,3},{7,4},{4,5},{5,6},{6,7},{11,8},{8,9},{9,10... | collective-permute-start | bytes 393224 | tf_op jit(solution)/shard_map/ppermute | solution.py:42
  10.2 2.2 %collective-permute-start.6 = (f32[4,2,4,8,128]{4,3,2,1,0:T(8,128)S(1)}, f32[4,2,4,8,128]{4,3,2,1,0:T(8,128)S(1)}, u32[]{:S(2)}, u32[]{:S(2)}) collective-permute-start(f32[4,2,4,8,128]{4,3,2,1,0:T(8,128)S(1)} %get-tuple-element.36), channel_id=1, source_target_pairs={{1,0},{2,1},{3,2},{0,3},{5,4},{6,5},{7,6},{4,7},{9,8},{10,9},{11,1... | collective-permute-start | bytes 393224 | tf_op jit(solution)/shard_map/ppermute | solution.py:42
  12.5 0.0 collective-permute-done.1.cross_ref
  12.5 0.0 collective-permute-done.same_ref
  12.5 0.0 copy-done
  12.5 0.0 copy-done.1
  12.5 0.0 copy-done.3
  12.5 0.0 copy-done.7
  12.5 1.3 %monitor_message.1 = (f32[112,128]{1,0:T(8,128)S(1)}, f32[112,128]{1,0:T(8,128)S(1)}, f32[88,128]{1,0:T(8,128)S(1)}, f32[7,16,128]{2,1,0:T(8,128)S(1)}) custom-call(f32[4]{0:T(128)S(1)} %copy-done.7, f32[3,16,8,128]{3,2,1,0:T(8,128)S(1)} %copy-done, f32[3,16,8,128]{3,2,1,0:T(8,128)S(1)} %copy-done.1, s32[16,8,128]{2,1,0:T(8,128)S(1)} %copy-done.3, ...), custom_call_target="tpu_custom_call" | custom-call | flops 1 | bytes 1 | tf_op jit(solution)/shard_map/monitor_message/pallas_call | solution.py:680
  13.8 1.1 %collective-permute-start.2 = (f32[112,128]{1,0:T(8,128)S(1)}, f32[112,128]{1,0:T(8,128)S(1)}, u32[]{:S(2)}, u32[]{:S(2)}) collective-permute-start(f32[112,128]{1,0:T(8,128)S(1)} %get-tuple-element.25), channel_id=1, source_target_pairs={{1,0},{2,1},{3,2},{0,3},{5,4},{6,5},{7,6},{4,7},{9,8},{10,9},{11,1... | collective-permute-start | bytes 172040 | tf_op jit(solution)/shard_map/ppermute | solution.py:42
  14.9 1.0 %collective-permute-start.3 = (f32[112,128]{1,0:T(8,128)S(1)}, f32[112,128]{1,0:T(8,128)S(1)}, u32[]{:S(2)}, u32[]{:S(2)}) collective-permute-start(f32[112,128]{1,0:T(8,128)S(1)} %get-tuple-element.26), channel_id=1, source_target_pairs={{3,0},{0,1},{1,2},{2,3},{7,4},{4,5},{5,6},{6,7},{11,8},{8,9},{9,10... | collective-permute-start | bytes 172040 | tf_op jit(solution)/shard_map/ppermute | solution.py:42
  15.9 0.0 collective-permute-done.4.refs_0_
  15.9 0.0 copy-start.4
  15.9 0.7 %collective-permute-start.7 = (f32[88,128]{1,0:T(8,128)S(1)}, f32[88,128]{1,0:T(8,128)S(1)}, u32[]{:S(2)}, u32[]{:S(2)}) collective-permute-start(f32[88,128]{1,0:T(8,128)S(1)} %get-tuple-element.27.after_this.refs_3_), channel_id=1, source_target_pairs={{2,0},{3,1},{0,2},{1,3},{6,4},{7,5},{4,6},{5,7},{10,8},{11,9},{8,1... | collective-permute-start | bytes 135176 | tf_op jit(solution)/shard_map/ppermute | solution.py:42
  16.6 0.0 copy-start.6
  16.6 1.4 %fetch.1 = (f32[2,128,8,128]{3,2,1,0:T(8,128)S(1)}, f32[16,2,4,8,128]{4,3,2,1,0:T(8,128)S(1)}) custom-call(f32[88,128]{1,0:T(8,128)S(1)} %get-tuple-element.27.after_this.refs_3_, f32[2,128,8,128]{3,2,1,0:T(8,128)} %slab_any.1, f32[16,2,4,8,128]{4,3,2,1,0:T(8,128)} %spectra_any.3), custom_call_target="tpu_custom_call" | custom-call | flops 1 | bytes 3000000 | tf_op jit(solution)/shard_map/fetch/pallas_call | solution.py:680
  18.0 0.0 copy-start.8
  18.0 0.0 collective-permute-done.5.refs_1_
  18.0 1.2 %collective-permute-done.6.refs_2_ = f32[4,2,4,8,128]{4,3,2,1,0:T(8,128)S(1)} collective-permute-done((f32[4,2,4,8,128]{4,3,2,1,0:T(8,128)S(1)}, f32[4,2,4,8,128]{4,3,2,1,0:T(8,128)S(1)}, u32[]{:S(2)}, u32[]{:S(2)}) %collective-permute-start.6) | collective-permute-done | bytes 131104 | tf_op jit(solution)/shard_map/ppermute | solution.py:42
  19.2 0.0 copy-done.4
  19.2 0.0 copy-done.6
  19.2 0.0 copy-done.8
  19.2 0.0 copy-start.2
  19.3 1.4 %y_monitor.1 = (f32[8,32,128]{2,1,0:T(8,128)S(1)}, f32[8,8,128]{2,1,0:T(8,128)S(1)}) custom-call(s32[16]{0:T(128)S(1)} %copy-done.8, f32[512]{0:T(512)S(1)} %copy-done.6, bf16[2,512,256]{2,1,0:T(8,128)(2,1)S(1)} %copy-done.4, f32[16,2,4,8,128]{4,3,2,1,0:T(8,128)S(1)} %get-tuple-element.29.monitor_ref.own_ref, ...), custom_call_target="tpu_custom_call" | custom-call | flops 100000000 | bytes 2000000 | tf_op jit(solution)/shard_map/y_monitor/pallas_call | solution.py:680
  20.6 2.2 %collective-permute-done.7.refs_1_ = f32[88,128]{1,0:T(8,128)S(1)} collective-permute-done((f32[88,128]{1,0:T(8,128)S(1)}, f32[88,128]{1,0:T(8,128)S(1)}, u32[]{:S(2)}, u32[]{:S(2)}) %collective-permute-start.7) | collective-permute-done | bytes 45088 | tf_op jit(solution)/shard_map/ppermute | solution.py:42
  22.8 0.0 collective-permute-done.2.message_after_ref.refs_2_
  22.8 0.0 collective-permute-done.3.message_before_ref.refs_0_
  22.8 0.0 copy-done.2
  22.8 1.6 %y_records.1 = f32[8,32,128]{2,1,0:T(8,128)} custom-call(bf16[2,640,256]{2,1,0:T(8,128)(2,1)S(1)} %copy-done.2, f32[8,32,128]{2,1,0:T(8,128)S(1)} %get-tuple-element.37.monitor_ref, f32[8,8,128]{2,1,0:T(8,128)S(1)} %get-tuple-element.38.weights_ref, f32[112,128]{1,0:T(8,128)S(1)} %collective-permute-done.3.message_before_ref.refs_0_, ...), custom_call_target="tpu_custom_call" | custom-call | flops 100000000 | bytes 2000000 | tf_op jit(solution)/shard_map/y_records/pallas_call | solution.py:680
  24.4 4.0 %all-to-all-start = ((f32[8,32,128]{2,1,0:T(8,128)}), f32[8,32,128]{2,1,0:T(8,128)S(1)}, u32[]{:S(2)}, u32[]{:S(2)}) async-start(f32[8,32,128]{2,1,0:T(8,128)} %y_records.1), calls=%async_computation | async-start | bytes 262144 | tf_op jit(solution)/shard_map/all_to_all | solution.py:819
  28.4 0.0 copy-start.5
  28.4 3.1 %local_updates.1 = (f32[3,16,8,128]{3,2,1,0:T(8,128)}, f32[3,16,8,128]{3,2,1,0:T(8,128)}, f32[2,128,8,128]{3,2,1,0:T(8,128)}, f32[16,2,4,8,128]{4,3,2,1,0:T(8,128)}) custom-call(f32[4]{0:T(128)S(1)} %copy-done.7, s32[16]{0:T(128)S(1)} %copy-done.8, f32[512]{0:T(512)S(1)} %copy-done.6, f32[3,16,8,128]{3,2,1,0:T(8,128)S(1)} %copy-done, ...), custom_call_target="tpu_custom_call" | custom-call | flops 10000000 | bytes 6000000 | tf_op jit(solution)/shard_map/local_updates/pallas_call | solution.py:680
  31.5 0.0 all-to-all-done.values_ref
  31.6 0.0 copy-done.5
  31.6 1.0 %x_orders.1 = f32[4,2,4,16,64]{4,3,2,1,0:T(8,128)} custom-call(f32[8,32,128]{2,1,0:T(8,128)S(1)} %all-to-all-done.values_ref, bf16[2,128,128]{2,1,0:T(8,128)(2,1)S(1)} %copy-done.5), custom_call_target="tpu_custom_call" | custom-call | flops 10000000 | bytes 500000 | tf_op jit(solution)/shard_map/x_orders/pallas_call | solution.py:680
Async XLA Ops:
  1.8 14.1 %collective-permute-start.4 = (f32[4,2,4,8,128]{4,3,2,1,0:T(8,128)S(1)}, f32[4,2,4,8,128]{4,3,2,1,0:T(8,128)S(1)}, u32[]{:S(2)}, u32[]{:S(2)}) collective-permute-start(f32[4,2,4,8,128]{4,3,2,1,0:T(8,128)S(1)} %get-tuple-element.34), channel_id=1, source_target_pairs={{2,0},{3,1},{0,2},{1,3},{6,4},{7,5},{4,6},{5,7},{10,8},{11,9},{8,1... | collective-permute-start | bytes 393224 | tf_op jit(solution)/shard_map/ppermute | solution.py:42
  5.9 6.6 %collective-permute-start.1 = (f32[7,4,8,128]{3,2,1,0:T(8,128)S(1)}, f32[7,4,8,128]{3,2,1,0:T(8,128)S(1)}, u32[]{:S(2)}, u32[]{:S(2)}) collective-permute-start(f32[7,4,8,128]{3,2,1,0:T(8,128)S(1)} %get-tuple-element.23), channel_id=1, source_target_pairs={{0,28},{4,8},{8,4},{12,16},{16,12},{20,24},{24,20},{28,0},{1,29},{... | collective-permute-start | bytes 344072 | tf_op jit(solution)/shard_map/ppermute | solution.py:725
  7.5 5.0 %copy-start = (f32[3,16,8,128]{3,2,1,0:T(8,128)S(1)}, f32[3,16,8,128]{3,2,1,0:T(8,128)}, u32[]{:S(2)}) copy-start(f32[3,16,8,128]{3,2,1,0:T(8,128)} %e_ref.3) | copy-start | bytes 589828
  7.5 5.0 %copy-start.1 = (f32[3,16,8,128]{3,2,1,0:T(8,128)S(1)}, f32[3,16,8,128]{3,2,1,0:T(8,128)}, u32[]{:S(2)}) copy-start(f32[3,16,8,128]{3,2,1,0:T(8,128)} %h_ref.3) | copy-start | bytes 589828
  7.5 5.0 %copy-start.3 = (s32[16,8,128]{2,1,0:T(8,128)S(1)}, s32[16,8,128]{2,1,0:T(8,128)}, u32[]{:S(2)}) copy-start(s32[16,8,128]{2,1,0:T(8,128)} %m_ref.3) | copy-start | bytes 196612
  7.5 5.0 %collective-permute-start = (f32[7,4,8,128]{3,2,1,0:T(8,128)S(1)}, f32[7,4,8,128]{3,2,1,0:T(8,128)S(1)}, u32[]{:S(2)}, u32[]{:S(2)}) collective-permute-start(f32[7,4,8,128]{3,2,1,0:T(8,128)S(1)} %get-tuple-element.22.after_this), channel_id=1, source_target_pairs={{0,4},{4,0},{8,12},{12,8},{16,20},{20,16},{24,28},{28,24},{1,5},{5... | collective-permute-start | bytes 344072 | tf_op jit(solution)/shard_map/ppermute | solution.py:724
  8.6 3.9 %copy-start.7 = (f32[4]{0:T(128)S(1)}, f32[4]{0:T(128)}, u32[]{:S(2)}) copy-start(f32[4]{0:T(128)} %perm_ref.3) | copy-start | bytes 52
  8.6 9.4 %collective-permute-start.5 = (f32[4,2,4,8,128]{4,3,2,1,0:T(8,128)S(1)}, f32[4,2,4,8,128]{4,3,2,1,0:T(8,128)S(1)}, u32[]{:S(2)}, u32[]{:S(2)}) collective-permute-start(f32[4,2,4,8,128]{4,3,2,1,0:T(8,128)S(1)} %get-tuple-element.35), channel_id=1, source_target_pairs={{3,0},{0,1},{1,2},{2,3},{7,4},{4,5},{5,6},{6,7},{11,8},{8,9},{9,10... | collective-permute-start | bytes 393224 | tf_op jit(solution)/shard_map/ppermute | solution.py:42
  10.2 9.0 %collective-permute-start.6 = (f32[4,2,4,8,128]{4,3,2,1,0:T(8,128)S(1)}, f32[4,2,4,8,128]{4,3,2,1,0:T(8,128)S(1)}, u32[]{:S(2)}, u32[]{:S(2)}) collective-permute-start(f32[4,2,4,8,128]{4,3,2,1,0:T(8,128)S(1)} %get-tuple-element.36), channel_id=1, source_target_pairs={{1,0},{2,1},{3,2},{0,3},{5,4},{6,5},{7,6},{4,7},{9,8},{10,9},{11,1... | collective-permute-start | bytes 393224 | tf_op jit(solution)/shard_map/ppermute | solution.py:42
  13.8 9.0 %collective-permute-start.2 = (f32[112,128]{1,0:T(8,128)S(1)}, f32[112,128]{1,0:T(8,128)S(1)}, u32[]{:S(2)}, u32[]{:S(2)}) collective-permute-start(f32[112,128]{1,0:T(8,128)S(1)} %get-tuple-element.25), channel_id=1, source_target_pairs={{1,0},{2,1},{3,2},{0,3},{5,4},{6,5},{7,6},{4,7},{9,8},{10,9},{11,1... | collective-permute-start | bytes 172040 | tf_op jit(solution)/shard_map/ppermute | solution.py:42
  14.9 8.0 %collective-permute-start.3 = (f32[112,128]{1,0:T(8,128)S(1)}, f32[112,128]{1,0:T(8,128)S(1)}, u32[]{:S(2)}, u32[]{:S(2)}) collective-permute-start(f32[112,128]{1,0:T(8,128)S(1)} %get-tuple-element.26), channel_id=1, source_target_pairs={{3,0},{0,1},{1,2},{2,3},{7,4},{4,5},{5,6},{6,7},{11,8},{8,9},{9,10... | collective-permute-start | bytes 172040 | tf_op jit(solution)/shard_map/ppermute | solution.py:42
  15.9 3.4 %copy-start.4 = (bf16[2,512,256]{2,1,0:T(8,128)(2,1)S(1)}, bf16[2,512,256]{2,1,0:T(8,128)(2,1)}, u32[]{:S(2)}) copy-start(bf16[2,512,256]{2,1,0:T(8,128)(2,1)} %constant.9.clone.table_ref) | copy-start | bytes 1572868
  15.9 6.9 %collective-permute-start.7 = (f32[88,128]{1,0:T(8,128)S(1)}, f32[88,128]{1,0:T(8,128)S(1)}, u32[]{:S(2)}, u32[]{:S(2)}) collective-permute-start(f32[88,128]{1,0:T(8,128)S(1)} %get-tuple-element.27.after_this.refs_3_), channel_id=1, source_target_pairs={{2,0},{3,1},{0,2},{1,3},{6,4},{7,5},{4,6},{5,7},{10,8},{11,9},{8,1... | collective-permute-start | bytes 135176 | tf_op jit(solution)/shard_map/ppermute | solution.py:42
  16.6 2.6 %copy-start.6 = (f32[512]{0:T(512)S(1)}, f32[512]{0:T(512)}, u32[]{:S(2)}) copy-start(f32[512]{0:T(512)} %constant.8.clone.coef_ref) | copy-start | bytes 6148
  18.0 1.2 %copy-start.8 = (s32[16]{0:T(128)S(1)}, s32[16]{0:T(128)}, u32[]{:S(2)}) copy-start(s32[16]{0:T(128)} %wave_ref.3) | copy-start | bytes 196
  19.2 3.6 %copy-start.2 = (bf16[2,640,256]{2,1,0:T(8,128)(2,1)S(1)}, bf16[2,640,256]{2,1,0:T(8,128)(2,1)}, u32[]{:S(2)}) copy-start(bf16[2,640,256]{2,1,0:T(8,128)(2,1)} %constant.10.clone.table_ref) | copy-start | bytes 1966084
  24.4 7.1 %all-to-all-start = ((f32[8,32,128]{2,1,0:T(8,128)}), f32[8,32,128]{2,1,0:T(8,128)S(1)}, u32[]{:S(2)}, u32[]{:S(2)}) async-start(f32[8,32,128]{2,1,0:T(8,128)} %y_records.1), calls=%async_computation | async-start | bytes 262144 | tf_op jit(solution)/shard_map/all_to_all | solution.py:819
  28.4 3.2 %copy-start.5 = (bf16[2,128,128]{2,1,0:T(8,128)(2,1)S(1)}, bf16[2,128,128]{2,1,0:T(8,128)(2,1)}, u32[]{:S(2)}) copy-start(bf16[2,128,128]{2,1,0:T(8,128)(2,1)} %constant.11.clone.table_ref) | copy-start | bytes 196612

commit v8 on v7

--- a/solution.py
+++ b/solution.py
@@ -501,12 +501,13 @@
         copy.wait()
 
 
-def x_orders(kept, values_ref, table_ref, out_ref):
+def x_orders(kept, values_ref, table_ref, out_any, out_ref, done):
     sources, height, lanes = values_ref.shape
     waves, _, records, _, _ = out_ref.shape
     depth = table_ref.shape[1]
     rows = depth // sources
     per_tile = lanes // kept
+    copies = []
     for tile in range(height // rows):
         values = jnp.concatenate(
             [values_ref[source, pl.ds(tile * rows, rows), :] for source in range(sources)], axis=0
@@ -518,6 +519,13 @@
                 here = result[place * kept : (place + 1) * kept]
                 out_ref[wave, 0, record] = here[:, :OX]
                 out_ref[wave, 1, record] = here[:, OX:]
+                if record == records - 1:
+                    copies.append(
+                        pltpu.make_async_copy(out_ref.at[wave], out_any.at[wave], done.at[wave])
+                    )
+                    copies[-1].start()
+    for copy in copies:
+        copy.wait()
 
 
 def local_updates(
@@ -855,6 +863,11 @@
         [(group_waves, 2, RECORDS, kept, OX)],
         swapped,
         x_table(length_x, x_blocks, scaling),
+        out_specs=[HBM],
+        scratch_shapes=[
+            pltpu.VMEM((group_waves, 2, RECORDS, kept, OX), jnp.float32),
+            pltpu.SemaphoreType.DMA((group_waves,)),
+        ],
         name="x_orders",
         flops=10**7,
         moved=5 * 10**5,

time: 32.9 us -> 32.9 us (level)
  no operation moved by 1% of the time
where the time goes in v8:
time: 32.9 us; the launch traced here: 32.6 us
  starting transfers between devices  16.4 us (50%)
  Pallas kernels  12 us (36%)
  waiting for transfers between devices  3.42 us (10%)
  between operations  0.77 us (2%)
    pallas_call x8, Pallas kernels, call(): pl.pallas_call(kernel, out_shape=out, in_specs=in_specs, out_specs=more.p...  12 us
    ppermute x6, starting transfers between devices, passed_along(): return lax.ppermute(block, axis, route)  10.8 us
    all_to_all x1, starting transfers between devices, per_device(): lax.all_to_all(spectrum_y, ('gx', 'gy'), split_axis=0, concat_axis=0, axi...  3.96 us
    ppermute x6, waiting for transfers between devices, passed_along(): return lax.ppermute(block, axis, route)  3.38 us
    ppermute x1, starting transfers between devices, per_device(): lax.ppermute(cross, 'gx', [(i, (i + (1 if i % 2 else -1)) % x_blocks) for...  1.61 us
  transfers between devices with their start and end apart: 9, of which 2 were waited for; matrix products, arithmetic and copies ran while one was open for 0% of the time, Pallas kernels for 25%

profile of v8, /device:TPU:0, one launch (start us, length us, event | category | flops | bytes accessed | tf_op | source)
XLA Modules:
  0.0 32.6 jit_solution(7934153999777707546)
XLA Ops:
  0.6 1.2 %pack_faces.1 = (f32[7,4,8,128]{3,2,1,0:T(8,128)S(1)}, f32[7,4,8,128]{3,2,1,0:T(8,128)S(1)}, f32[4,2,4,8,128]{4,3,2,1,0:T(8,128)S(1)}) custom-call(f32[4]{0:T(128)} %perm_ref.3, f32[3,16,8,128]{3,2,1,0:T(8,128)} %e_ref.3, f32[3,16,8,128]{3,2,1,0:T(8,128)} %h_ref.3, s32[16,8,128]{2,1,0:T(8,128)} %m_ref.3, f32[16,2,4,8,128]{4,3,2,1,0:T(8,128)} %spectra_any.3), custom_call_target="tpu_custom_call" | custom-call | flops 100000 | bytes 1000000 | tf_op jit(solution)/shard_map/pack_faces/pallas_call | solution.py:688
  1.8 4.1 %collective-permute-start.4 = (f32[4,2,4,8,128]{4,3,2,1,0:T(8,128)S(1)}, f32[4,2,4,8,128]{4,3,2,1,0:T(8,128)S(1)}, u32[]{:S(2)}, u32[]{:S(2)}) collective-permute-start(f32[4,2,4,8,128]{4,3,2,1,0:T(8,128)S(1)} %get-tuple-element.34), channel_id=1, source_target_pairs={{2,0},{3,1},{0,2},{1,3},{6,4},{7,5},{4,6},{5,7},{10,8},{11,9},{8,1... | collective-permute-start | bytes 393224 | tf_op jit(solution)/shard_map/ppermute | solution.py:42
  5.9 1.6 %collective-permute-start.1 = (f32[7,4,8,128]{3,2,1,0:T(8,128)S(1)}, f32[7,4,8,128]{3,2,1,0:T(8,128)S(1)}, u32[]{:S(2)}, u32[]{:S(2)}) collective-permute-start(f32[7,4,8,128]{3,2,1,0:T(8,128)S(1)} %get-tuple-element.23), channel_id=1, source_target_pairs={{0,28},{4,8},{8,4},{12,16},{16,12},{20,24},{24,20},{28,0},{1,29},{... | collective-permute-start | bytes 344072 | tf_op jit(solution)/shard_map/ppermute | solution.py:733
  7.5 0.0 copy-start
  7.5 0.0 copy-start.1
  7.5 0.0 copy-start.3
  7.5 0.0 collective-permute-start
  7.5 1.0 %other_blocks.1 = (f32[4,2,4,8,128]{4,3,2,1,0:T(8,128)S(1)}, f32[4,2,4,8,128]{4,3,2,1,0:T(8,128)S(1)}) custom-call(f32[7,4,8,128]{3,2,1,0:T(8,128)S(1)} %get-tuple-element.22.after_this, f32[16,2,4,8,128]{4,3,2,1,0:T(8,128)} %spectra_any.3), custom_call_target="tpu_custom_call" | custom-call | flops 1 | bytes 1 | tf_op jit(solution)/shard_map/other_blocks/pallas_call | solution.py:688
  8.6 0.0 copy-start.7
  8.6 1.6 %collective-permute-start.5 = (f32[4,2,4,8,128]{4,3,2,1,0:T(8,128)S(1)}, f32[4,2,4,8,128]{4,3,2,1,0:T(8,128)S(1)}, u32[]{:S(2)}, u32[]{:S(2)}) collective-permute-start(f32[4,2,4,8,128]{4,3,2,1,0:T(8,128)S(1)} %get-tuple-element.35), channel_id=1, source_target_pairs={{3,0},{0,1},{1,2},{2,3},{7,4},{4,5},{5,6},{6,7},{11,8},{8,9},{9,10... | collective-permute-start | bytes 393224 | tf_op jit(solution)/shard_map/ppermute | solution.py:42
  10.2 2.2 %collective-permute-start.6 = (f32[4,2,4,8,128]{4,3,2,1,0:T(8,128)S(1)}, f32[4,2,4,8,128]{4,3,2,1,0:T(8,128)S(1)}, u32[]{:S(2)}, u32[]{:S(2)}) collective-permute-start(f32[4,2,4,8,128]{4,3,2,1,0:T(8,128)S(1)} %get-tuple-element.36), channel_id=1, source_target_pairs={{1,0},{2,1},{3,2},{0,3},{5,4},{6,5},{7,6},{4,7},{9,8},{10,9},{11,1... | collective-permute-start | bytes 393224 | tf_op jit(solution)/shard_map/ppermute | solution.py:42
  12.5 0.0 collective-permute-done.1.cross_ref
  12.5 0.0 collective-permute-done.same_ref
  12.5 0.0 copy-done
  12.5 0.0 copy-done.1
  12.5 0.0 copy-done.3
  12.5 0.0 copy-done.7
  12.5 1.3 %monitor_message.1 = (f32[112,128]{1,0:T(8,128)S(1)}, f32[112,128]{1,0:T(8,128)S(1)}, f32[88,128]{1,0:T(8,128)S(1)}, f32[7,16,128]{2,1,0:T(8,128)S(1)}) custom-call(f32[4]{0:T(128)S(1)} %copy-done.7, f32[3,16,8,128]{3,2,1,0:T(8,128)S(1)} %copy-done, f32[3,16,8,128]{3,2,1,0:T(8,128)S(1)} %copy-done.1, s32[16,8,128]{2,1,0:T(8,128)S(1)} %copy-done.3, ...), custom_call_target="tpu_custom_call" | custom-call | flops 1 | bytes 1 | tf_op jit(solution)/shard_map/monitor_message/pallas_call | solution.py:688
  13.8 1.1 %collective-permute-start.2 = (f32[112,128]{1,0:T(8,128)S(1)}, f32[112,128]{1,0:T(8,128)S(1)}, u32[]{:S(2)}, u32[]{:S(2)}) collective-permute-start(f32[112,128]{1,0:T(8,128)S(1)} %get-tuple-element.25), channel_id=1, source_target_pairs={{1,0},{2,1},{3,2},{0,3},{5,4},{6,5},{7,6},{4,7},{9,8},{10,9},{11,1... | collective-permute-start | bytes 172040 | tf_op jit(solution)/shard_map/ppermute | solution.py:42
  14.9 1.0 %collective-permute-start.3 = (f32[112,128]{1,0:T(8,128)S(1)}, f32[112,128]{1,0:T(8,128)S(1)}, u32[]{:S(2)}, u32[]{:S(2)}) collective-permute-start(f32[112,128]{1,0:T(8,128)S(1)} %get-tuple-element.26), channel_id=1, source_target_pairs={{3,0},{0,1},{1,2},{2,3},{7,4},{4,5},{5,6},{6,7},{11,8},{8,9},{9,10... | collective-permute-start | bytes 172040 | tf_op jit(solution)/shard_map/ppermute | solution.py:42
  15.9 0.0 collective-permute-done.4.refs_0_
  15.9 0.0 copy-start.4
  15.9 0.7 %collective-permute-start.7 = (f32[88,128]{1,0:T(8,128)S(1)}, f32[88,128]{1,0:T(8,128)S(1)}, u32[]{:S(2)}, u32[]{:S(2)}) collective-permute-start(f32[88,128]{1,0:T(8,128)S(1)} %get-tuple-element.27.after_this.refs_3_), channel_id=1, source_target_pairs={{2,0},{3,1},{0,2},{1,3},{6,4},{7,5},{4,6},{5,7},{10,8},{11,9},{8,1... | collective-permute-start | bytes 135176 | tf_op jit(solution)/shard_map/ppermute | solution.py:42
  16.6 0.0 copy-start.6
  16.6 1.4 %fetch.1 = (f32[2,128,8,128]{3,2,1,0:T(8,128)S(1)}, f32[16,2,4,8,128]{4,3,2,1,0:T(8,128)S(1)}) custom-call(f32[88,128]{1,0:T(8,128)S(1)} %get-tuple-element.27.after_this.refs_3_, f32[2,128,8,128]{3,2,1,0:T(8,128)} %slab_any.1, f32[16,2,4,8,128]{4,3,2,1,0:T(8,128)} %spectra_any.3), custom_call_target="tpu_custom_call" | custom-call | flops 1 | bytes 3000000 | tf_op jit(solution)/shard_map/fetch/pallas_call | solution.py:688
  18.0 0.0 copy-start.8
  18.0 0.0 collective-permute-done.5.refs_1_
  18.0 1.2 %collective-permute-done.6.refs_2_ = f32[4,2,4,8,128]{4,3,2,1,0:T(8,128)S(1)} collective-permute-done((f32[4,2,4,8,128]{4,3,2,1,0:T(8,128)S(1)}, f32[4,2,4,8,128]{4,3,2,1,0:T(8,128)S(1)}, u32[]{:S(2)}, u32[]{:S(2)}) %collective-permute-start.6) | collective-permute-done | bytes 131104 | tf_op jit(solution)/shard_map/ppermute | solution.py:42
  19.2 0.0 copy-done.4
  19.2 0.0 copy-done.6
  19.2 0.0 copy-done.8
  19.2 0.0 copy-start.2
  19.3 1.4 %y_monitor.1 = (f32[8,32,128]{2,1,0:T(8,128)S(1)}, f32[8,8,128]{2,1,0:T(8,128)S(1)}) custom-call(s32[16]{0:T(128)S(1)} %copy-done.8, f32[512]{0:T(512)S(1)} %copy-done.6, bf16[2,512,256]{2,1,0:T(8,128)(2,1)S(1)} %copy-done.4, f32[16,2,4,8,128]{4,3,2,1,0:T(8,128)S(1)} %get-tuple-element.29.monitor_ref.own_ref, ...), custom_call_target="tpu_custom_call" | custom-call | flops 100000000 | bytes 2000000 | tf_op jit(solution)/shard_map/y_monitor/pallas_call | solution.py:688
  20.6 2.2 %collective-permute-done.7.refs_1_ = f32[88,128]{1,0:T(8,128)S(1)} collective-permute-done((f32[88,128]{1,0:T(8,128)S(1)}, f32[88,128]{1,0:T(8,128)S(1)}, u32[]{:S(2)}, u32[]{:S(2)}) %collective-permute-start.7) | collective-permute-done | bytes 45088 | tf_op jit(solution)/shard_map/ppermute | solution.py:42
  22.8 0.0 collective-permute-done.2.message_after_ref.refs_2_
  22.8 0.0 collective-permute-done.3.message_before_ref.refs_0_
  22.8 0.0 copy-done.2
  22.8 1.6 %y_records.1 = f32[8,32,128]{2,1,0:T(8,128)} custom-call(bf16[2,640,256]{2,1,0:T(8,128)(2,1)S(1)} %copy-done.2, f32[8,32,128]{2,1,0:T(8,128)S(1)} %get-tuple-element.37.monitor_ref, f32[8,8,128]{2,1,0:T(8,128)S(1)} %get-tuple-element.38.weights_ref, f32[112,128]{1,0:T(8,128)S(1)} %collective-permute-done.3.message_before_ref.refs_0_, ...), custom_call_target="tpu_custom_call" | custom-call | flops 100000000 | bytes 2000000 | tf_op jit(solution)/shard_map/y_records/pallas_call | solution.py:688
  24.4 4.0 %all-to-all-start = ((f32[8,32,128]{2,1,0:T(8,128)}), f32[8,32,128]{2,1,0:T(8,128)S(1)}, u32[]{:S(2)}, u32[]{:S(2)}) async-start(f32[8,32,128]{2,1,0:T(8,128)} %y_records.1), calls=%async_computation | async-start | bytes 262144 | tf_op jit(solution)/shard_map/all_to_all | solution.py:827
  28.4 0.0 copy-start.5
  28.4 3.1 %local_updates.1 = (f32[3,16,8,128]{3,2,1,0:T(8,128)}, f32[3,16,8,128]{3,2,1,0:T(8,128)}, f32[2,128,8,128]{3,2,1,0:T(8,128)}, f32[16,2,4,8,128]{4,3,2,1,0:T(8,128)}) custom-call(f32[4]{0:T(128)S(1)} %copy-done.7, s32[16]{0:T(128)S(1)} %copy-done.8, f32[512]{0:T(512)S(1)} %copy-done.6, f32[3,16,8,128]{3,2,1,0:T(8,128)S(1)} %copy-done, ...), custom_call_target="tpu_custom_call" | custom-call | flops 10000000 | bytes 6000000 | tf_op jit(solution)/shard_map/local_updates/pallas_call | solution.py:688
  31.5 0.0 all-to-all-done.values_ref
  31.6 0.0 copy-done.5
  31.6 1.0 %x_orders.1 = f32[4,2,4,16,64]{4,3,2,1,0:T(8,128)} custom-call(f32[8,32,128]{2,1,0:T(8,128)S(1)} %all-to-all-done.values_ref, bf16[2,128,128]{2,1,0:T(8,128)(2,1)S(1)} %copy-done.5), custom_call_target="tpu_custom_call" | custom-call | flops 10000000 | bytes 500000 | tf_op jit(solution)/shard_map/x_orders/pallas_call | solution.py:688
Async XLA Ops:
  1.8 14.1 %collective-permute-start.4 = (f32[4,2,4,8,128]{4,3,2,1,0:T(8,128)S(1)}, f32[4,2,4,8,128]{4,3,2,1,0:T(8,128)S(1)}, u32[]{:S(2)}, u32[]{:S(2)}) collective-permute-start(f32[4,2,4,8,128]{4,3,2,1,0:T(8,128)S(1)} %get-tuple-element.34), channel_id=1, source_target_pairs={{2,0},{3,1},{0,2},{1,3},{6,4},{7,5},{4,6},{5,7},{10,8},{11,9},{8,1... | collective-permute-start | bytes 393224 | tf_op jit(solution)/shard_map/ppermute | solution.py:42
  5.9 6.6 %collective-permute-start.1 = (f32[7,4,8,128]{3,2,1,0:T(8,128)S(1)}, f32[7,4,8,128]{3,2,1,0:T(8,128)S(1)}, u32[]{:S(2)}, u32[]{:S(2)}) collective-permute-start(f32[7,4,8,128]{3,2,1,0:T(8,128)S(1)} %get-tuple-element.23), channel_id=1, source_target_pairs={{0,28},{4,8},{8,4},{12,16},{16,12},{20,24},{24,20},{28,0},{1,29},{... | collective-permute-start | bytes 344072 | tf_op jit(solution)/shard_map/ppermute | solution.py:733
  7.5 5.0 %copy-start = (f32[3,16,8,128]{3,2,1,0:T(8,128)S(1)}, f32[3,16,8,128]{3,2,1,0:T(8,128)}, u32[]{:S(2)}) copy-start(f32[3,16,8,128]{3,2,1,0:T(8,128)} %e_ref.3) | copy-start | bytes 589828
  7.5 5.0 %copy-start.1 = (f32[3,16,8,128]{3,2,1,0:T(8,128)S(1)}, f32[3,16,8,128]{3,2,1,0:T(8,128)}, u32[]{:S(2)}) copy-start(f32[3,16,8,128]{3,2,1,0:T(8,128)} %h_ref.3) | copy-start | bytes 589828
  7.5 5.0 %copy-start.3 = (s32[16,8,128]{2,1,0:T(8,128)S(1)}, s32[16,8,128]{2,1,0:T(8,128)}, u32[]{:S(2)}) copy-start(s32[16,8,128]{2,1,0:T(8,128)} %m_ref.3) | copy-start | bytes 196612
  7.5 5.0 %collective-permute-start = (f32[7,4,8,128]{3,2,1,0:T(8,128)S(1)}, f32[7,4,8,128]{3,2,1,0:T(8,128)S(1)}, u32[]{:S(2)}, u32[]{:S(2)}) collective-permute-start(f32[7,4,8,128]{3,2,1,0:T(8,128)S(1)} %get-tuple-element.22.after_this), channel_id=1, source_target_pairs={{0,4},{4,0},{8,12},{12,8},{16,20},{20,16},{24,28},{28,24},{1,5},{5... | collective-permute-start | bytes 344072 | tf_op jit(solution)/shard_map/ppermute | solution.py:732
  8.6 3.9 %copy-start.7 = (f32[4]{0:T(128)S(1)}, f32[4]{0:T(128)}, u32[]{:S(2)}) copy-start(f32[4]{0:T(128)} %perm_ref.3) | copy-start | bytes 52
  8.6 9.4 %collective-permute-start.5 = (f32[4,2,4,8,128]{4,3,2,1,0:T(8,128)S(1)}, f32[4,2,4,8,128]{4,3,2,1,0:T(8,128)S(1)}, u32[]{:S(2)}, u32[]{:S(2)}) collective-permute-start(f32[4,2,4,8,128]{4,3,2,1,0:T(8,128)S(1)} %get-tuple-element.35), channel_id=1, source_target_pairs={{3,0},{0,1},{1,2},{2,3},{7,4},{4,5},{5,6},{6,7},{11,8},{8,9},{9,10... | collective-permute-start | bytes 393224 | tf_op jit(solution)/shard_map/ppermute | solution.py:42
  10.2 9.0 %collective-permute-start.6 = (f32[4,2,4,8,128]{4,3,2,1,0:T(8,128)S(1)}, f32[4,2,4,8,128]{4,3,2,1,0:T(8,128)S(1)}, u32[]{:S(2)}, u32[]{:S(2)}) collective-permute-start(f32[4,2,4,8,128]{4,3,2,1,0:T(8,128)S(1)} %get-tuple-element.36), channel_id=1, source_target_pairs={{1,0},{2,1},{3,2},{0,3},{5,4},{6,5},{7,6},{4,7},{9,8},{10,9},{11,1... | collective-permute-start | bytes 393224 | tf_op jit(solution)/shard_map/ppermute | solution.py:42
  13.8 9.0 %collective-permute-start.2 = (f32[112,128]{1,0:T(8,128)S(1)}, f32[112,128]{1,0:T(8,128)S(1)}, u32[]{:S(2)}, u32[]{:S(2)}) collective-permute-start(f32[112,128]{1,0:T(8,128)S(1)} %get-tuple-element.25), channel_id=1, source_target_pairs={{1,0},{2,1},{3,2},{0,3},{5,4},{6,5},{7,6},{4,7},{9,8},{10,9},{11,1... | collective-permute-start | bytes 172040 | tf_op jit(solution)/shard_map/ppermute | solution.py:42
  14.9 8.0 %collective-permute-start.3 = (f32[112,128]{1,0:T(8,128)S(1)}, f32[112,128]{1,0:T(8,128)S(1)}, u32[]{:S(2)}, u32[]{:S(2)}) collective-permute-start(f32[112,128]{1,0:T(8,128)S(1)} %get-tuple-element.26), channel_id=1, source_target_pairs={{3,0},{0,1},{1,2},{2,3},{7,4},{4,5},{5,6},{6,7},{11,8},{8,9},{9,10... | collective-permute-start | bytes 172040 | tf_op jit(solution)/shard_map/ppermute | solution.py:42
  15.9 3.4 %copy-start.4 = (bf16[2,512,256]{2,1,0:T(8,128)(2,1)S(1)}, bf16[2,512,256]{2,1,0:T(8,128)(2,1)}, u32[]{:S(2)}) copy-start(bf16[2,512,256]{2,1,0:T(8,128)(2,1)} %constant.9.clone.table_ref) | copy-start | bytes 1572868
  15.9 6.9 %collective-permute-start.7 = (f32[88,128]{1,0:T(8,128)S(1)}, f32[88,128]{1,0:T(8,128)S(1)}, u32[]{:S(2)}, u32[]{:S(2)}) collective-permute-start(f32[88,128]{1,0:T(8,128)S(1)} %get-tuple-element.27.after_this.refs_3_), channel_id=1, source_target_pairs={{2,0},{3,1},{0,2},{1,3},{6,4},{7,5},{4,6},{5,7},{10,8},{11,9},{8,1... | collective-permute-start | bytes 135176 | tf_op jit(solution)/shard_map/ppermute | solution.py:42
  16.6 2.6 %copy-start.6 = (f32[512]{0:T(512)S(1)}, f32[512]{0:T(512)}, u32[]{:S(2)}) copy-start(f32[512]{0:T(512)} %constant.8.clone.coef_ref) | copy-start | bytes 6148
  18.0 1.2 %copy-start.8 = (s32[16]{0:T(128)S(1)}, s32[16]{0:T(128)}, u32[]{:S(2)}) copy-start(s32[16]{0:T(128)} %wave_ref.3) | copy-start | bytes 196
  19.2 3.6 %copy-start.2 = (bf16[2,640,256]{2,1,0:T(8,128)(2,1)S(1)}, bf16[2,640,256]{2,1,0:T(8,128)(2,1)}, u32[]{:S(2)}) copy-start(bf16[2,640,256]{2,1,0:T(8,128)(2,1)} %constant.10.clone.table_ref) | copy-start | bytes 1966084
  24.4 7.1 %all-to-all-start = ((f32[8,32,128]{2,1,0:T(8,128)}), f32[8,32,128]{2,1,0:T(8,128)S(1)}, u32[]{:S(2)}, u32[]{:S(2)}) async-start(f32[8,32,128]{2,1,0:T(8,128)} %y_records.1), calls=%async_computation | async-start | bytes 262144 | tf_op jit(solution)/shard_map/all_to_all | solution.py:827
  28.4 3.2 %copy-start.5 = (bf16[2,128,128]{2,1,0:T(8,128)(2,1)S(1)}, bf16[2,128,128]{2,1,0:T(8,128)(2,1)}, u32[]{:S(2)}) copy-start(bf16[2,128,128]{2,1,0:T(8,128)(2,1)} %constant.11.clone.table_ref) | copy-start | bytes 196612

commit v9 on v8

--- a/solution.py
+++ b/solution.py
@@ -375,7 +375,7 @@
 def y_monitor(wave_ref, coef_ref, table_ref, own_ref, *refs):
     *spectra, out_ref, weights_ref = refs
     half = len(spectra) // 2
-    spectra = spectra[half + 1 :] + spectra[:1] + spectra[1 : half + 1]
+    spectra = spectra[1 : half + 1] + spectra[:1] + spectra[half + 1 :]
     blocks = len(spectra) + 1
     waves, _, records, rows, columns = spectra[0].shape
     me = lax.axis_index("gy")
@@ -799,7 +799,7 @@
         coefs,
         sums_y,
         monitor_here,
-        *[spectra[distance] for distance in [y_blocks // 2] + list(range(y_blocks // 2 + 1, y_blocks)) + list(range(1, y_blocks // 2))],
+        *[spectra[distance] for distance in [y_blocks // 2] + list(range(1, y_blocks // 2)) + list(range(y_blocks // 2 + 1, y_blocks))],
         name="y_monitor",
         flops=10**8,
         moved=2 * 10**6,

time: 32.9 us -> 32.9 us (level)
  starting transfers between devices: 16.4 us -> 14.9 us
  waiting for transfers between devices: 3.42 us -> 4.31 us
  local copies, waits for them, and re-layouts: 0.04 us -> 0.64 us
    ppermute x1, waiting for transfers between devices: 0.01 us -> 1.47 us  [per_device(): lax.ppermute(cross, 'gx', [(i, (i + (1 if i % 2 else -1)) % x_blocks) for...]
    ppermute x6, starting transfers between devices: 10.8 us -> 9.34 us  [passed_along(): return lax.ppermute(block, axis, route)]
    ppermute x6, waiting for transfers between devices: 3.38 us -> 2.7 us  [passed_along(): return lax.ppermute(block, axis, route)]
    unnamed x18, local copies, waits for them, and re-layouts: 0.04 us -> 0.64 us
  transfers between devices with their start and end apart: 9 -> 9, of which waited for: 2 -> 3; matrix products, arithmetic and copies ran while one was open for 0% -> 0% of each run, Pallas kernels for 25% -> 25%
where the time goes in v9:
time: 32.9 us; the launch traced here: 32.6 us
  starting transfers between devices  14.9 us (45%)
  Pallas kernels  12 us (36%)
  waiting for transfers between devices  4.31 us (13%)
  between operations  0.75 us (2%)
  local copies, waits for them, and re-layouts  0.64 us (2%)
    pallas_call x8, Pallas kernels, call(): pl.pallas_call(kernel, out_shape=out, in_specs=in_specs, out_specs=more.p...  12 us
    ppermute x6, starting transfers between devices, passed_along(): return lax.ppermute(block, axis, route)  9.34 us
    all_to_all x1, starting transfers between devices, per_device(): lax.all_to_all(spectrum_y, ('gx', 'gy'), split_axis=0, concat_axis=0, axi...  3.96 us
    ppermute x6, waiting for transfers between devices, passed_along(): return lax.ppermute(block, axis, route)  2.7 us
    ppermute x1, starting transfers between devices, per_device(): lax.ppermute(cross, 'gx', [(i, (i + (1 if i % 2 else -1)) % x_blocks) for...  1.61 us
    ppermute x1, waiting for transfers between devices, per_device(): lax.ppermute(cross, 'gx', [(i, (i + (1 if i % 2 else -1)) % x_blocks) for...  1.47 us
  transfers between devices with their start and end apart: 9, of which 3 were waited for; matrix products, arithmetic and copies ran while one was open for 0% of the time, Pallas kernels for 25%

profile of v9, /device:TPU:0, one launch (start us, length us, event | category | flops | bytes accessed | tf_op | source)
XLA Modules:
  0.0 32.6 jit_solution(6574247399913915448)
XLA Ops:
  0.6 1.2 %pack_faces.1 = (f32[7,4,8,128]{3,2,1,0:T(8,128)S(1)}, f32[7,4,8,128]{3,2,1,0:T(8,128)S(1)}, f32[4,2,4,8,128]{4,3,2,1,0:T(8,128)S(1)}) custom-call(f32[4]{0:T(128)} %perm_ref.3, f32[3,16,8,128]{3,2,1,0:T(8,128)} %e_ref.3, f32[3,16,8,128]{3,2,1,0:T(8,128)} %h_ref.3, s32[16,8,128]{2,1,0:T(8,128)} %m_ref.3, f32[16,2,4,8,128]{4,3,2,1,0:T(8,128)} %spectra_any.3), custom_call_target="tpu_custom_call" | custom-call | flops 100000 | bytes 1000000 | tf_op jit(solution)/shard_map/pack_faces/pallas_call | solution.py:688
  1.8 4.1 %collective-permute-start.4 = (f32[4,2,4,8,128]{4,3,2,1,0:T(8,128)S(1)}, f32[4,2,4,8,128]{4,3,2,1,0:T(8,128)S(1)}, u32[]{:S(2)}, u32[]{:S(2)}) collective-permute-start(f32[4,2,4,8,128]{4,3,2,1,0:T(8,128)S(1)} %get-tuple-element.34), channel_id=1, source_target_pairs={{2,0},{3,1},{0,2},{1,3},{6,4},{7,5},{4,6},{5,7},{10,8},{11,9},{8,1... | collective-permute-start | bytes 393224 | tf_op jit(solution)/shard_map/ppermute | solution.py:42
  5.9 1.6 %collective-permute-start.1 = (f32[7,4,8,128]{3,2,1,0:T(8,128)S(1)}, f32[7,4,8,128]{3,2,1,0:T(8,128)S(1)}, u32[]{:S(2)}, u32[]{:S(2)}) collective-permute-start(f32[7,4,8,128]{3,2,1,0:T(8,128)S(1)} %get-tuple-element.23), channel_id=1, source_target_pairs={{0,28},{4,8},{8,4},{12,16},{16,12},{20,24},{24,20},{28,0},{1,29},{... | collective-permute-start | bytes 344072 | tf_op jit(solution)/shard_map/ppermute | solution.py:733
  7.5 0.0 copy-start
  7.5 0.0 copy-start.1
  7.5 0.0 copy-start.3
  7.5 0.0 collective-permute-start
  7.5 1.0 %other_blocks.1 = (f32[4,2,4,8,128]{4,3,2,1,0:T(8,128)S(1)}, f32[4,2,4,8,128]{4,3,2,1,0:T(8,128)S(1)}) custom-call(f32[7,4,8,128]{3,2,1,0:T(8,128)S(1)} %get-tuple-element.22.after_this, f32[16,2,4,8,128]{4,3,2,1,0:T(8,128)} %spectra_any.3), custom_call_target="tpu_custom_call" | custom-call | flops 1 | bytes 1 | tf_op jit(solution)/shard_map/other_blocks/pallas_call | solution.py:688
  8.6 0.0 copy-start.7
  8.6 1.4 %collective-permute-start.5 = (f32[4,2,4,8,128]{4,3,2,1,0:T(8,128)S(1)}, f32[4,2,4,8,128]{4,3,2,1,0:T(8,128)S(1)}, u32[]{:S(2)}, u32[]{:S(2)}) collective-permute-start(f32[4,2,4,8,128]{4,3,2,1,0:T(8,128)S(1)} %get-tuple-element.35), channel_id=1, source_target_pairs={{1,0},{2,1},{3,2},{0,3},{5,4},{6,5},{7,6},{4,7},{9,8},{10,9},{11,1... | collective-permute-start | bytes 393224 | tf_op jit(solution)/shard_map/ppermute | solution.py:42
  10.0 0.7 %collective-permute-start.6 = (f32[4,2,4,8,128]{4,3,2,1,0:T(8,128)S(1)}, f32[4,2,4,8,128]{4,3,2,1,0:T(8,128)S(1)}, u32[]{:S(2)}, u32[]{:S(2)}) collective-permute-start(f32[4,2,4,8,128]{4,3,2,1,0:T(8,128)S(1)} %get-tuple-element.36), channel_id=1, source_target_pairs={{3,0},{0,1},{1,2},{2,3},{7,4},{4,5},{5,6},{6,7},{11,8},{8,9},{9,10... | collective-permute-start | bytes 393224 | tf_op jit(solution)/shard_map/ppermute | solution.py:42
  10.7 1.5 %collective-permute-done.1.cross_ref = f32[7,4,8,128]{3,2,1,0:T(8,128)S(1)} collective-permute-done((f32[7,4,8,128]{3,2,1,0:T(8,128)S(1)}, f32[7,4,8,128]{3,2,1,0:T(8,128)S(1)}, u32[]{:S(2)}, u32[]{:S(2)}) %collective-permute-start.1) | collective-permute-done | bytes 114720 | tf_op jit(solution)/shard_map/ppermute | solution.py:733
  12.2 0.0 collective-permute-done.same_ref
  12.2 0.0 copy-done
  12.2 0.0 copy-done.1
  12.2 0.0 copy-done.3
  12.2 0.0 copy-done.7
  12.2 1.3 %monitor_message.1 = (f32[112,128]{1,0:T(8,128)S(1)}, f32[112,128]{1,0:T(8,128)S(1)}, f32[88,128]{1,0:T(8,128)S(1)}, f32[7,16,128]{2,1,0:T(8,128)S(1)}) custom-call(f32[4]{0:T(128)S(1)} %copy-done.7, f32[3,16,8,128]{3,2,1,0:T(8,128)S(1)} %copy-done, f32[3,16,8,128]{3,2,1,0:T(8,128)S(1)} %copy-done.1, s32[16,8,128]{2,1,0:T(8,128)S(1)} %copy-done.3, ...), custom_call_target="tpu_custom_call" | custom-call | flops 1 | bytes 1 | tf_op jit(solution)/shard_map/monitor_message/pallas_call | solution.py:688
  13.5 1.8 %collective-permute-start.2 = (f32[112,128]{1,0:T(8,128)S(1)}, f32[112,128]{1,0:T(8,128)S(1)}, u32[]{:S(2)}, u32[]{:S(2)}) collective-permute-start(f32[112,128]{1,0:T(8,128)S(1)} %get-tuple-element.25), channel_id=1, source_target_pairs={{1,0},{2,1},{3,2},{0,3},{5,4},{6,5},{7,6},{4,7},{9,8},{10,9},{11,1... | collective-permute-start | bytes 172040 | tf_op jit(solution)/shard_map/ppermute | solution.py:42
  15.2 0.3 collective-permute-start.3
  15.5 0.0 collective-permute-done.4.refs_0_
  15.5 0.0 copy-start.4
  15.5 1.1 %collective-permute-start.7 = (f32[88,128]{1,0:T(8,128)S(1)}, f32[88,128]{1,0:T(8,128)S(1)}, u32[]{:S(2)}, u32[]{:S(2)}) collective-permute-start(f32[88,128]{1,0:T(8,128)S(1)} %get-tuple-element.27.after_this.refs_3_), channel_id=1, source_target_pairs={{2,0},{3,1},{0,2},{1,3},{6,4},{7,5},{4,6},{5,7},{10,8},{11,9},{8,1... | collective-permute-start | bytes 135176 | tf_op jit(solution)/shard_map/ppermute | solution.py:42
  16.6 0.0 copy-start.6
  16.6 1.4 %fetch.1 = (f32[2,128,8,128]{3,2,1,0:T(8,128)S(1)}, f32[16,2,4,8,128]{4,3,2,1,0:T(8,128)S(1)}) custom-call(f32[88,128]{1,0:T(8,128)S(1)} %get-tuple-element.27.after_this.refs_3_, f32[2,128,8,128]{3,2,1,0:T(8,128)} %slab_any.1, f32[16,2,4,8,128]{4,3,2,1,0:T(8,128)} %spectra_any.3), custom_call_target="tpu_custom_call" | custom-call | flops 1 | bytes 3000000 | tf_op jit(solution)/shard_map/fetch/pallas_call | solution.py:688
  18.0 0.0 copy-start.8
  18.0 0.0 collective-permute-done.5.refs_1_
  18.0 0.0 collective-permute-done.6.refs_2_
  18.1 0.0 copy-done.4
  18.1 0.0 copy-done.6
  18.1 0.6 %copy-done.8 = s32[16]{0:T(128)S(1)} copy-done((s32[16]{0:T(128)S(1)}, s32[16]{0:T(128)}, u32[]{:S(2)}) %copy-start.8) | copy-done | bytes 88
  18.7 0.0 copy-start.2
  18.7 1.4 %y_monitor.1 = (f32[8,32,128]{2,1,0:T(8,128)S(1)}, f32[8,8,128]{2,1,0:T(8,128)S(1)}) custom-call(s32[16]{0:T(128)S(1)} %copy-done.8, f32[512]{0:T(512)S(1)} %copy-done.6, bf16[2,512,256]{2,1,0:T(8,128)(2,1)S(1)} %copy-done.4, f32[16,2,4,8,128]{4,3,2,1,0:T(8,128)S(1)} %get-tuple-element.29.monitor_ref.own_ref, ...), custom_call_target="tpu_custom_call" | custom-call | flops 100000000 | bytes 2000000 | tf_op jit(solution)/shard_map/y_monitor/pallas_call | solution.py:688
  20.1 2.7 %collective-permute-done.7.refs_1_ = f32[88,128]{1,0:T(8,128)S(1)} collective-permute-done((f32[88,128]{1,0:T(8,128)S(1)}, f32[88,128]{1,0:T(8,128)S(1)}, u32[]{:S(2)}, u32[]{:S(2)}) %collective-permute-start.7) | collective-permute-done | bytes 45088 | tf_op jit(solution)/shard_map/ppermute | solution.py:42
  22.7 0.0 collective-permute-done.2.message_after_ref.refs_2_
  22.7 0.0 collective-permute-done.3.message_before_ref.refs_0_
  22.7 0.0 copy-done.2
  22.7 1.6 %y_records.1 = f32[8,32,128]{2,1,0:T(8,128)} custom-call(bf16[2,640,256]{2,1,0:T(8,128)(2,1)S(1)} %copy-done.2, f32[8,32,128]{2,1,0:T(8,128)S(1)} %get-tuple-element.37.monitor_ref, f32[8,8,128]{2,1,0:T(8,128)S(1)} %get-tuple-element.38.weights_ref, f32[112,128]{1,0:T(8,128)S(1)} %collective-permute-done.3.message_before_ref.refs_0_, ...), custom_call_target="tpu_custom_call" | custom-call | flops 100000000 | bytes 2000000 | tf_op jit(solution)/shard_map/y_records/pallas_call | solution.py:688
  24.3 4.0 %all-to-all-start = ((f32[8,32,128]{2,1,0:T(8,128)}), f32[8,32,128]{2,1,0:T(8,128)S(1)}, u32[]{:S(2)}, u32[]{:S(2)}) async-start(f32[8,32,128]{2,1,0:T(8,128)} %y_records.1), calls=%async_computation | async-start | bytes 262144 | tf_op jit(solution)/shard_map/all_to_all | solution.py:827
  28.3 0.0 copy-start.5
  28.3 3.1 %local_updates.1 = (f32[3,16,8,128]{3,2,1,0:T(8,128)}, f32[3,16,8,128]{3,2,1,0:T(8,128)}, f32[2,128,8,128]{3,2,1,0:T(8,128)}, f32[16,2,4,8,128]{4,3,2,1,0:T(8,128)}) custom-call(f32[4]{0:T(128)S(1)} %copy-done.7, s32[16]{0:T(128)S(1)} %copy-done.8, f32[512]{0:T(512)S(1)} %copy-done.6, f32[3,16,8,128]{3,2,1,0:T(8,128)S(1)} %copy-done, ...), custom_call_target="tpu_custom_call" | custom-call | flops 10000000 | bytes 6000000 | tf_op jit(solution)/shard_map/local_updates/pallas_call | solution.py:688
  31.4 0.1 all-to-all-done.values_ref
  31.6 0.0 copy-done.5
  31.6 1.0 %x_orders.1 = f32[4,2,4,16,64]{4,3,2,1,0:T(8,128)} custom-call(f32[8,32,128]{2,1,0:T(8,128)S(1)} %all-to-all-done.values_ref, bf16[2,128,128]{2,1,0:T(8,128)(2,1)S(1)} %copy-done.5), custom_call_target="tpu_custom_call" | custom-call | flops 10000000 | bytes 500000 | tf_op jit(solution)/shard_map/x_orders/pallas_call | solution.py:688
Async XLA Ops:
  1.8 13.7 %collective-permute-start.4 = (f32[4,2,4,8,128]{4,3,2,1,0:T(8,128)S(1)}, f32[4,2,4,8,128]{4,3,2,1,0:T(8,128)S(1)}, u32[]{:S(2)}, u32[]{:S(2)}) collective-permute-start(f32[4,2,4,8,128]{4,3,2,1,0:T(8,128)S(1)} %get-tuple-element.34), channel_id=1, source_target_pairs={{2,0},{3,1},{0,2},{1,3},{6,4},{7,5},{4,6},{5,7},{10,8},{11,9},{8,1... | collective-permute-start | bytes 393224 | tf_op jit(solution)/shard_map/ppermute | solution.py:42
  5.9 6.2 %collective-permute-start.1 = (f32[7,4,8,128]{3,2,1,0:T(8,128)S(1)}, f32[7,4,8,128]{3,2,1,0:T(8,128)S(1)}, u32[]{:S(2)}, u32[]{:S(2)}) collective-permute-start(f32[7,4,8,128]{3,2,1,0:T(8,128)S(1)} %get-tuple-element.23), channel_id=1, source_target_pairs={{0,28},{4,8},{8,4},{12,16},{16,12},{20,24},{24,20},{28,0},{1,29},{... | collective-permute-start | bytes 344072 | tf_op jit(solution)/shard_map/ppermute | solution.py:733
  7.5 4.6 %copy-start = (f32[3,16,8,128]{3,2,1,0:T(8,128)S(1)}, f32[3,16,8,128]{3,2,1,0:T(8,128)}, u32[]{:S(2)}) copy-start(f32[3,16,8,128]{3,2,1,0:T(8,128)} %e_ref.3) | copy-start | bytes 589828
  7.5 4.6 %copy-start.1 = (f32[3,16,8,128]{3,2,1,0:T(8,128)S(1)}, f32[3,16,8,128]{3,2,1,0:T(8,128)}, u32[]{:S(2)}) copy-start(f32[3,16,8,128]{3,2,1,0:T(8,128)} %h_ref.3) | copy-start | bytes 589828
  7.5 4.6 %copy-start.3 = (s32[16,8,128]{2,1,0:T(8,128)S(1)}, s32[16,8,128]{2,1,0:T(8,128)}, u32[]{:S(2)}) copy-start(s32[16,8,128]{2,1,0:T(8,128)} %m_ref.3) | copy-start | bytes 196612
  7.5 4.6 %collective-permute-start = (f32[7,4,8,128]{3,2,1,0:T(8,128)S(1)}, f32[7,4,8,128]{3,2,1,0:T(8,128)S(1)}, u32[]{:S(2)}, u32[]{:S(2)}) collective-permute-start(f32[7,4,8,128]{3,2,1,0:T(8,128)S(1)} %get-tuple-element.22.after_this), channel_id=1, source_target_pairs={{0,4},{4,0},{8,12},{12,8},{16,20},{20,16},{24,28},{28,24},{1,5},{5... | collective-permute-start | bytes 344072 | tf_op jit(solution)/shard_map/ppermute | solution.py:732
  8.6 3.6 %copy-start.7 = (f32[4]{0:T(128)S(1)}, f32[4]{0:T(128)}, u32[]{:S(2)}) copy-start(f32[4]{0:T(128)} %perm_ref.3) | copy-start | bytes 52
  8.6 9.4 %collective-permute-start.5 = (f32[4,2,4,8,128]{4,3,2,1,0:T(8,128)S(1)}, f32[4,2,4,8,128]{4,3,2,1,0:T(8,128)S(1)}, u32[]{:S(2)}, u32[]{:S(2)}) collective-permute-start(f32[4,2,4,8,128]{4,3,2,1,0:T(8,128)S(1)} %get-tuple-element.35), channel_id=1, source_target_pairs={{1,0},{2,1},{3,2},{0,3},{5,4},{6,5},{7,6},{4,7},{9,8},{10,9},{11,1... | collective-permute-start | bytes 393224 | tf_op jit(solution)/shard_map/ppermute | solution.py:42
  10.0 8.0 %collective-permute-start.6 = (f32[4,2,4,8,128]{4,3,2,1,0:T(8,128)S(1)}, f32[4,2,4,8,128]{4,3,2,1,0:T(8,128)S(1)}, u32[]{:S(2)}, u32[]{:S(2)}) collective-permute-start(f32[4,2,4,8,128]{4,3,2,1,0:T(8,128)S(1)} %get-tuple-element.36), channel_id=1, source_target_pairs={{3,0},{0,1},{1,2},{2,3},{7,4},{4,5},{5,6},{6,7},{11,8},{8,9},{9,10... | collective-permute-start | bytes 393224 | tf_op jit(solution)/shard_map/ppermute | solution.py:42
  13.5 9.3 %collective-permute-start.2 = (f32[112,128]{1,0:T(8,128)S(1)}, f32[112,128]{1,0:T(8,128)S(1)}, u32[]{:S(2)}, u32[]{:S(2)}) collective-permute-start(f32[112,128]{1,0:T(8,128)S(1)} %get-tuple-element.25), channel_id=1, source_target_pairs={{1,0},{2,1},{3,2},{0,3},{5,4},{6,5},{7,6},{4,7},{9,8},{10,9},{11,1... | collective-permute-start | bytes 172040 | tf_op jit(solution)/shard_map/ppermute | solution.py:42
  15.2 7.5 %collective-permute-start.3 = (f32[112,128]{1,0:T(8,128)S(1)}, f32[112,128]{1,0:T(8,128)S(1)}, u32[]{:S(2)}, u32[]{:S(2)}) collective-permute-start(f32[112,128]{1,0:T(8,128)S(1)} %get-tuple-element.26), channel_id=1, source_target_pairs={{3,0},{0,1},{1,2},{2,3},{7,4},{4,5},{5,6},{6,7},{11,8},{8,9},{9,10... | collective-permute-start | bytes 172040 | tf_op jit(solution)/shard_map/ppermute | solution.py:42
  15.5 2.5 %copy-start.4 = (bf16[2,512,256]{2,1,0:T(8,128)(2,1)S(1)}, bf16[2,512,256]{2,1,0:T(8,128)(2,1)}, u32[]{:S(2)}) copy-start(bf16[2,512,256]{2,1,0:T(8,128)(2,1)} %constant.9.clone.table_ref) | copy-start | bytes 1572868
  15.5 7.2 %collective-permute-start.7 = (f32[88,128]{1,0:T(8,128)S(1)}, f32[88,128]{1,0:T(8,128)S(1)}, u32[]{:S(2)}, u32[]{:S(2)}) collective-permute-start(f32[88,128]{1,0:T(8,128)S(1)} %get-tuple-element.27.after_this.refs_3_), channel_id=1, source_target_pairs={{2,0},{3,1},{0,2},{1,3},{6,4},{7,5},{4,6},{5,7},{10,8},{11,9},{8,1... | collective-permute-start | bytes 135176 | tf_op jit(solution)/shard_map/ppermute | solution.py:42
  16.6 1.5 %copy-start.6 = (f32[512]{0:T(512)S(1)}, f32[512]{0:T(512)}, u32[]{:S(2)}) copy-start(f32[512]{0:T(512)} %constant.8.clone.coef_ref) | copy-start | bytes 6148
  18.0 0.7 %copy-start.8 = (s32[16]{0:T(128)S(1)}, s32[16]{0:T(128)}, u32[]{:S(2)}) copy-start(s32[16]{0:T(128)} %wave_ref.3) | copy-start | bytes 196
  18.7 4.0 %copy-start.2 = (bf16[2,640,256]{2,1,0:T(8,128)(2,1)S(1)}, bf16[2,640,256]{2,1,0:T(8,128)(2,1)}, u32[]{:S(2)}) copy-start(bf16[2,640,256]{2,1,0:T(8,128)(2,1)} %constant.10.clone.table_ref) | copy-start | bytes 1966084
  24.3 7.2 %all-to-all-start = ((f32[8,32,128]{2,1,0:T(8,128)}), f32[8,32,128]{2,1,0:T(8,128)S(1)}, u32[]{:S(2)}, u32[]{:S(2)}) async-start(f32[8,32,128]{2,1,0:T(8,128)} %y_records.1), calls=%async_computation | async-start | bytes 262144 | tf_op jit(solution)/shard_map/all_to_all | solution.py:827
  28.3 3.3 %copy-start.5 = (bf16[2,128,128]{2,1,0:T(8,128)(2,1)S(1)}, bf16[2,128,128]{2,1,0:T(8,128)(2,1)}, u32[]{:S(2)}) copy-start(bf16[2,128,128]{2,1,0:T(8,128)(2,1)} %constant.11.clone.table_ref) | copy-start | bytes 196612
